TPU v7x, 32 devices: a whole 2x2x4 slice. The times are simulated.
32 devices in a mesh: dp: 4 (over z), fsdp: 8 (over y, x, core).
Axes of the slice: x: 2, y: 2, z: 4, core: 2. Of those that a mesh axis runs over, the one named last changes fastest.
Arguments:
- tokens: bfloat16 [32, 512, 768], P(('dp', 'fsdp')), may hold values from -6 to 6
- cotangent: bfloat16 [32, 512, 768], P(('dp', 'fsdp')), may hold values from -6 to 6
- lengths: int32 [32], P(('dp', 'fsdp')), may hold values from 128 to 512, as said below
- weights: float32 [440, 128, 128], P('dp', 'fsdp')
- vectors: float32 [13, 768], replicated
- moments: float32 [13, 768], replicated
- left_stats: float32 [440, 128, 128], P('dp', 'fsdp')
- right_stats: float32 [440, 128, 128], P('dp', 'fsdp')
- left_root: float32 [440, 128, 128], P('dp', 'fsdp')
- right_root: float32 [440, 128, 128], P('dp', 'fsdp'), as said below
- decays: float32 [440, 2], P('dp'), may hold values from 0.9 to 0.99
Outputs:
- outputs: bfloat16 [32, 512, 768], P(('dp', 'fsdp'))
- input_grads: bfloat16 [32, 512, 768], P(('dp', 'fsdp'))
- new_weights: float32 [440, 128, 128], P('dp', 'fsdp')
- weight_grads: float32 [440, 128, 128], P('dp', 'fsdp')
- new_left: float32 [440, 128, 128], P('dp', 'fsdp')
- new_right: float32 [440, 128, 128], P('dp', 'fsdp')
- new_vectors: float32 [13, 768], replicated
- new_moments: float32 [13, 768], replicated
- summary_norms: float32 [2], replicated
Inputs may be any that keep to these rules, and one draw needn't show every extreme that they name: `lengths`: some slot has length exactly 512. `right_root`: every block is symmetric.
All inputs are finite; a program needn't handle non-finite values.
Results may differ from a plain program's by a relative error of at most 0.02.
The roundings to bfloat16 on the way count: a program that leaves them out, or rounds other values in their place, can miss the bound.
Values may be sent and summed in bfloat16 or wider, within the bound.
No kernel may reach another device: no remote copies, remote signals or barrier semaphores. Data moves between devices by JAX's collectives and lax.ppermute only.
A program may use at most 192 MiB of HBM per device.

v0:
```python
import jax
import jax.numpy as jnp
from jax import lax
from jax.sharding import PartitionSpec as P

D = 768
H = 12
HD = 64
FF = 3072
K = 256
NMAX = 512
TB = 128


HIGHEST_PRECISION = lax.Precision.HIGHEST
EPS_NORM = 1e-05
EPS_STEP = 1e-06
STEP_RATE = 0.25
MOMENT_DECAY = 0.9
SQRT_HALF = 0.7071067811865476
INV_SQRT_TWO_PI = 0.3989422804014327


def forward_tiles(rows_in, tiles, out_width):
    tile_size = tiles.shape[1]
    leading = rows_in.shape[:-1]
    tile_grid = tiles.reshape(
        rows_in.shape[-1] // tile_size, out_width // tile_size, tile_size, tile_size
    )
    shaped = rows_in.reshape(leading + (rows_in.shape[-1] // tile_size, tile_size))
    product = jnp.einsum("snic,ijcd->snjd", shaped, tile_grid, preferred_element_type=jnp.float32)
    return product.reshape(leading + (out_width,))


def backward_tiles(grads_out, tiles, in_width):
    tile_size = tiles.shape[1]
    leading = grads_out.shape[:-1]
    tile_grid = tiles.reshape(
        in_width // tile_size, grads_out.shape[-1] // tile_size, tile_size, tile_size
    )
    shaped = grads_out.reshape(leading + (grads_out.shape[-1] // tile_size, tile_size))
    product = jnp.einsum("snjd,ijcd->snic", shaped, tile_grid, preferred_element_type=jnp.float32)
    return product.reshape(leading + (in_width,))


def gradient_tiles(rows_in, grads_out, tile_size):
    leading = rows_in.shape[:-1]
    left_shaped = rows_in.reshape(leading + (rows_in.shape[-1] // tile_size, tile_size))
    right_shaped = grads_out.reshape(leading + (grads_out.shape[-1] // tile_size, tile_size))
    product = jnp.einsum(
        "snic,snjd->ijcd", left_shaped, right_shaped, preferred_element_type=jnp.float32
    )
    return product.reshape(-1, tile_size, tile_size)


def untile(tiles, height, width):
    tile_size = tiles.shape[1]
    return (
        tiles.reshape(height // tile_size, width // tile_size, tile_size, tile_size)
        .transpose(0, 2, 1, 3)
        .reshape(height, width)
    )


def retile(matrix, tile_size):
    height, width = matrix.shape
    return (
        matrix.reshape(height // tile_size, tile_size, width // tile_size, tile_size)
        .transpose(0, 2, 1, 3)
        .reshape(-1, tile_size, tile_size)
    )


def layer_norm(value):
    centre = jnp.mean(value, axis=-1, keepdims=True)
    shifted = value - centre
    spread = jnp.mean(shifted * shifted, axis=-1, keepdims=True)
    inverse = lax.rsqrt(spread + EPS_NORM)
    return (shifted * inverse, inverse)


def norm_backward(grad_out, normed, inverse, gain):
    scaled = grad_out * gain
    centred = scaled - jnp.mean(scaled, axis=-1, keepdims=True)
    return inverse * (centred - normed * jnp.mean(scaled * normed, axis=-1, keepdims=True))


def token_sum(value):
    return jnp.sum(value, axis=(0, 1), dtype=jnp.float32)


def gelu_value(value):
    return value * 0.5 * (1.0 + lax.erf(value * SQRT_HALF))


def gelu_slope(value):
    return 0.5 * (1.0 + lax.erf(value * SQRT_HALF)) + value * INV_SQRT_TWO_PI * jnp.exp(
        -0.5 * value * value
    )


def widen(tile_part):
    return lax.all_gather(tile_part, "fsdp", axis=1, tiled=True)


def gather_tiles(weights, att_count):
    narrow = lax.all_gather(weights.astype(jnp.bfloat16), "dp", axis=0, tiled=True)
    return (widen(narrow[:att_count]), widen(narrow[att_count:]))


def local(
    tokens,
    cotangent,
    lengths,
    weights,
    vectors,
    moments,
    left_stats,
    right_stats,
    left_root,
    right_root,
    decays,
):
    quarter = (D // TB) ** 2
    att_count = 4 * quarter + NMAX // TB * (K // TB)
    hidden_count = D // TB * (FF // TB)
    spread_rows = FF // D
    seq_count = tokens.shape[0]
    seq_total = seq_count * lax.axis_size("dp") * lax.axis_size("fsdp")
    score_scale = HD ** (-0.5)
    bias_query = vectors[0]
    bias_key = vectors[1]
    bias_value = vectors[2]
    bias_output = vectors[3]
    gain_first = vectors[4]
    shift_first = vectors[5]
    bias_hidden = vectors[6 : 6 + spread_rows].reshape(FF)
    bias_return = vectors[6 + spread_rows]
    gain_second = vectors[7 + spread_rows]
    shift_second = vectors[8 + spread_rows]
    att_tiles, ffn_tiles = gather_tiles(weights, att_count)
    compress = untile(att_tiles[4 * quarter :], NMAX, K)
    positions = lax.broadcasted_iota(jnp.int32, (seq_count, NMAX), 1)
    validity = (positions < lengths[:, None]).astype(jnp.float32)
    masked = compress[None, :, :] * validity[:, :, None].astype(jnp.bfloat16)
    queries = (forward_tiles(tokens, att_tiles[:quarter], D) + bias_query).astype(jnp.bfloat16)
    key_rows = (forward_tiles(tokens, att_tiles[quarter : 2 * quarter], D) + bias_key).astype(
        jnp.bfloat16
    )
    value_rows = (
        forward_tiles(tokens, att_tiles[2 * quarter : 3 * quarter], D) + bias_value
    ).astype(jnp.bfloat16)
    key_summary = jnp.einsum(
        "snk,snd->skd", masked, key_rows, preferred_element_type=jnp.float32
    ).astype(jnp.bfloat16)
    value_summary = jnp.einsum(
        "snk,snd->skd", masked, value_rows, preferred_element_type=jnp.float32
    ).astype(jnp.bfloat16)
    key_norms = jnp.sqrt(jnp.sum(jnp.square(key_summary.astype(jnp.float32)), axis=(1, 2)))
    value_norms = jnp.sqrt(jnp.sum(jnp.square(value_summary.astype(jnp.float32)), axis=(1, 2)))
    head_queries = queries.reshape(seq_count, NMAX, H, HD)
    head_keys = key_summary.reshape(seq_count, K, H, HD)
    head_values = value_summary.reshape(seq_count, K, H, HD)
    scores = (
        jnp.einsum("snhd,skhd->shnk", head_queries, head_keys, preferred_element_type=jnp.float32)
        * score_scale
    )
    row_peak = jnp.max(scores, axis=-1, keepdims=True)
    raised = jnp.exp(scores - row_peak)
    totals = jnp.sum(raised, axis=-1, keepdims=True)
    attend_low = (raised / totals).astype(jnp.bfloat16)
    log_totals = row_peak + jnp.log(totals)
    mixed_low = jnp.einsum(
        "shnk,skhd->snhd", attend_low, head_values, preferred_element_type=jnp.float32
    )
    mixed_low = mixed_low.reshape(seq_count, NMAX, D).astype(jnp.bfloat16)
    branch = forward_tiles(mixed_low, att_tiles[3 * quarter : 4 * quarter], D) + bias_output
    normed_first, inverse_first = layer_norm(tokens.astype(jnp.float32) + branch)
    first = normed_first * gain_first + shift_first
    first_low = first.astype(jnp.bfloat16)
    hidden = forward_tiles(first_low, ffn_tiles[:hidden_count], FF) + bias_hidden
    active_low = gelu_value(hidden).astype(jnp.bfloat16)
    second = forward_tiles(active_low, ffn_tiles[hidden_count:], D) + bias_return
    normed_second, inverse_second = layer_norm(first + second)
    result = normed_second * gain_second + shift_second
    outputs = (result * validity[:, :, None]).astype(jnp.bfloat16)
    att_tiles, ffn_tiles = gather_tiles(weights, att_count)
    grad_result = cotangent.astype(jnp.float32) * validity[:, :, None]
    grad_gain_second = token_sum(grad_result * normed_second)
    grad_shift_second = token_sum(grad_result)
    grad_second = norm_backward(grad_result, normed_second, inverse_second, gain_second)
    grad_second_low = grad_second.astype(jnp.bfloat16)
    grad_bias_return = token_sum(grad_second_low)
    return_terms = gradient_tiles(active_low, grad_second_low, TB)
    grad_active = backward_tiles(grad_second_low, ffn_tiles[hidden_count:], FF)
    grad_hidden_low = (grad_active * gelu_slope(hidden)).astype(jnp.bfloat16)
    grad_bias_hidden = token_sum(grad_hidden_low)
    hidden_terms = gradient_tiles(first_low, grad_hidden_low, TB)
    grad_first = grad_second + backward_tiles(grad_hidden_low, ffn_tiles[:hidden_count], D)
    grad_gain_first = token_sum(grad_first * normed_first)
    grad_shift_first = token_sum(grad_first)
    grad_resid = norm_backward(grad_first, normed_first, inverse_first, gain_first)
    grad_branch_low = grad_resid.astype(jnp.bfloat16)
    grad_bias_output = token_sum(grad_branch_low)
    grad_mixed_low = backward_tiles(
        grad_branch_low, att_tiles[3 * quarter : 4 * quarter], D
    ).astype(jnp.bfloat16)
    scores = (
        jnp.einsum("snhd,skhd->shnk", head_queries, head_keys, preferred_element_type=jnp.float32)
        * score_scale
    )
    attend = jnp.exp(scores - log_totals)
    attend_low = attend.astype(jnp.bfloat16)
    grad_heads = grad_mixed_low.reshape(seq_count, NMAX, H, HD)
    grad_attend = jnp.einsum(
        "snhd,skhd->shnk", grad_heads, head_values, preferred_element_type=jnp.float32
    )
    grad_scores_low = (
        attend * (grad_attend - jnp.sum(grad_attend * attend, axis=-1, keepdims=True))
    ).astype(jnp.bfloat16)
    grad_value_summary = jnp.einsum(
        "shnk,snhd->skhd", attend_low, grad_heads, preferred_element_type=jnp.float32
    )
    grad_value_summary = grad_value_summary.reshape(seq_count, K, D).astype(jnp.bfloat16)
    grad_key_summary = (
        jnp.einsum(
            "shnk,snhd->skhd", grad_scores_low, head_queries, preferred_element_type=jnp.float32
        )
        * score_scale
    )
    grad_key_summary = grad_key_summary.reshape(seq_count, K, D).astype(jnp.bfloat16)
    grad_queries_low = (
        jnp.einsum(
            "shnk,skhd->snhd", grad_scores_low, head_keys, preferred_element_type=jnp.float32
        )
        * score_scale
    )
    grad_queries_low = grad_queries_low.reshape(seq_count, NMAX, D).astype(jnp.bfloat16)
    grad_key_rows = jnp.einsum(
        "snk,skd->snd", masked, grad_key_summary, preferred_element_type=jnp.float32
    ).astype(jnp.bfloat16)
    grad_value_rows = jnp.einsum(
        "snk,skd->snd", masked, grad_value_summary, preferred_element_type=jnp.float32
    ).astype(jnp.bfloat16)
    grad_masked = jnp.einsum(
        "snd,skd->snk", key_rows, grad_key_summary, preferred_element_type=jnp.float32
    )
    grad_masked = grad_masked + jnp.einsum(
        "snd,skd->snk", value_rows, grad_value_summary, preferred_element_type=jnp.float32
    )
    grad_compress = jnp.sum(grad_masked * validity[:, :, None], axis=0)
    input_grads = grad_resid + backward_tiles(grad_queries_low, att_tiles[:quarter], D)
    input_grads = input_grads + backward_tiles(grad_key_rows, att_tiles[quarter : 2 * quarter], D)
    input_grads = input_grads + backward_tiles(
        grad_value_rows, att_tiles[2 * quarter : 3 * quarter], D
    )
    input_grads = input_grads.astype(jnp.bfloat16)
    all_terms = jnp.concatenate(
        [
            gradient_tiles(tokens, grad_queries_low, TB),
            gradient_tiles(tokens, grad_key_rows, TB),
            gradient_tiles(tokens, grad_value_rows, TB),
            gradient_tiles(mixed_low, grad_branch_low, TB),
            retile(grad_compress, TB),
            hidden_terms,
            return_terms,
        ],
        axis=0,
    )
    inner_part = lax.psum_scatter(
        all_terms.astype(jnp.bfloat16), "fsdp", scatter_dimension=1, tiled=True
    )
    reduced = lax.psum_scatter(inner_part, "dp", scatter_dimension=0, tiled=True).astype(
        jnp.float32
    )
    local_vectors = jnp.concatenate(
        [
            jnp.stack(
                [
                    token_sum(grad_queries_low),
                    token_sum(grad_key_rows),
                    token_sum(grad_value_rows),
                    grad_bias_output,
                    grad_gain_first,
                    grad_shift_first,
                ]
            ),
            grad_bias_hidden.reshape(spread_rows, D),
            jnp.stack([grad_bias_return, grad_gain_second, grad_shift_second]),
        ],
        axis=0,
    )
    local_norms = jnp.stack([jnp.sum(key_norms), jnp.sum(value_norms)])
    vector_total, norm_totals = lax.psum((local_vectors, local_norms), ("dp", "fsdp"))
    vector_grad = vector_total / seq_total
    summary_norms = norm_totals / seq_total
    grad_rows = reduced / seq_total
    whole_tiles = lax.all_gather(grad_rows.astype(jnp.bfloat16), "fsdp", axis=1, tiled=True).astype(
        grad_rows.dtype
    )
    row_count = grad_rows.shape[1]
    row_start = lax.axis_index("fsdp") * row_count
    column_slab = lax.dynamic_slice_in_dim(whole_tiles, row_start, row_count, 2)
    gram_left = jnp.einsum("brc,bsc->brs", grad_rows, whole_tiles, precision=HIGHEST_PRECISION)
    gram_right = jnp.einsum("bic,bis->bcs", column_slab, whole_tiles, precision=HIGHEST_PRECISION)
    decay_left = decays[:, 0][:, None, None]
    decay_right = decays[:, 1][:, None, None]
    new_left = decay_left * left_stats + (1.0 - decay_left) * gram_left
    new_right = decay_right * right_stats + (1.0 - decay_right) * gram_right
    right_columns = jnp.einsum("bis,bcs->bic", whole_tiles, right_root, precision=HIGHEST_PRECISION)
    right_whole = lax.all_gather(
        right_columns.astype(jnp.bfloat16), "fsdp", axis=2, tiled=True
    ).astype(right_columns.dtype)
    precond = jnp.einsum("brs,bsc->brc", left_root, right_whole, precision=HIGHEST_PRECISION)
    precond_squares, weight_squares = lax.psum(
        (jnp.sum(precond * precond, axis=(1, 2)), jnp.sum(weights * weights, axis=(1, 2))), "fsdp"
    )
    tile_area = TB * TB
    weight_scale = jnp.sqrt(weight_squares / tile_area)
    precond_scale = lax.rsqrt(precond_squares / tile_area + EPS_STEP)
    new_weights = weights - STEP_RATE * (weight_scale * precond_scale)[:, None, None] * precond
    new_moments = MOMENT_DECAY * moments + (1.0 - MOMENT_DECAY) * vector_grad
    row_scale = jnp.sqrt(jnp.mean(jnp.square(vectors), axis=1, keepdims=True))
    moment_scale = lax.rsqrt(jnp.mean(jnp.square(new_moments), axis=1, keepdims=True) + EPS_STEP)
    new_vectors = vectors - STEP_RATE * row_scale * new_moments * moment_scale
    return (
        outputs,
        input_grads,
        new_weights,
        grad_rows,
        new_left,
        new_right,
        new_vectors,
        new_moments,
        summary_norms,
    )


def solution(mesh):
    in_specs = (
        P(("dp", "fsdp"), None, None),
        P(("dp", "fsdp"), None, None),
        P(("dp", "fsdp")),
        P("dp", "fsdp", None),
        P(),
        P(),
        P("dp", "fsdp", None),
        P("dp", "fsdp", None),
        P("dp", "fsdp", None),
        P("dp", "fsdp", None),
        P("dp", None),
    )
    out_specs = (
        P(("dp", "fsdp"), None, None),
        P(("dp", "fsdp"), None, None),
        P("dp", "fsdp", None),
        P("dp", "fsdp", None),
        P("dp", "fsdp", None),
        P("dp", "fsdp", None),
        P(),
        P(),
        P(),
    )
    return jax.shard_map(local, mesh=mesh, in_specs=in_specs, out_specs=out_specs, check_vma=False)
```

profile of v0, /device:TPU:0, one launch (start us, length us, event | category | flops | bytes accessed | tf_op | source)
XLA Modules:
  0.0 603.9 jit_solution(13056704971901933575)
XLA Ops:
  7.2 3.7 multiply_reduce_fusion.10
  11.0 43.7 %all-gather.6.cloned.1.call-done = bf16[440,16,128]{2,1,0:T(8,128)(2,1)} async-done(((bf16[110,16,128]{2,1,0:T(8,128)(2,1)}), bf16[440,16,128]{2,1,0:T(8,128)(2,1)}) %all-gather.6.cloned.1.call-update) | async-done | bytes 1802256 | tf_op jit(solution)/shard_map/all_gather | solution.py:107
  62.5 34.5 %all-gather.8.cloned.1.call-done = bf16[152,128,128]{2,1,0:T(8,128)(2,1)} async-done(((bf16[152,16,128]{2,1,0:T(8,128)(2,1)}), bf16[152,128,128]{2,1,0:T(8,128)(2,1)}) %all-gather.8.cloned.1.call-update) | async-done | bytes 4980752 | tf_op jit(solution)/shard_map/all_gather | solution.py:103
  96.9 4.5 fusion.70
  117.8 3.2 fusion.28
  138.9 20.5 %all-gather.10.cloned.1.call-done = bf16[288,128,128]{2,1,0:T(8,128)(2,1)} async-done(((bf16[288,16,128]{2,1,0:T(8,128)(2,1)}), bf16[288,128,128]{2,1,0:T(8,128)(2,1)}) %all-gather.10.cloned.1.call-update) | async-done | bytes 9437200 | tf_op jit(solution)/shard_map/all_gather | solution.py:103
  159.5 9.1 %fusion.69 = (bf16[144,128,128]{2,1,0:T(8,128)(2,1)}, bf16[144,128,128]{2,1,0:T(8,128)(2,1)S(1)}) fusion(bf16[288,128,128]{2,1,0:T(8,128)(2,1)} %all-gather.10.cloned.1.call-done), kind=kLoop, calls=%fused_computation.164 | loop fusion | bytes 18874368 | tf_op jit(solution)/shard_map/slice | solution.py:181
  173.8 6.7 %copy.140 = bf16[24,6,128,128]{2,3,1,0:T(8,128)(2,1)} copy(bf16[24,6,128,128]{3,2,1,0:T(8,128)(2,1)} %bitcast.333) | data formatting | bytes 9437184 | tf_op jit(solution)/shard_map/reshape | solution.py:27
  180.5 6.4 %copy.146 = bf16[6,24,128,128]{3,2,0,1:T(8,128)(2,1)} copy(bf16[6,24,128,128]{3,2,1,0:T(8,128)(2,1)} %bitcast.330) | data formatting | bytes 9437184 | tf_op jit(solution)/shard_map/reshape | solution.py:27
  186.8 6.7 %copy.138 = bf16[6,24,128,128]{2,3,1,0:T(8,128)(2,1)} copy(bf16[6,24,128,128]{3,2,1,0:T(8,128)(2,1)} %bitcast.331) | data formatting | bytes 9437184 | tf_op jit(solution)/shard_map/reshape | solution.py:27
  193.5 4.9 fusion.73
  198.6 7.9 %fusion.72 = (f32[512]{0:T(512)S(1)}, f32[1,512,768]{2,1,0:T(8,128)S(1)}) fusion(f32[768]{0:T(1024)S(1)} %copy-done.84, bf16[768,128,24]{1,0,2:T(8,128)(2,1)} %bitcast.356, f32[768]{0:T(1024)S(1)} %copy-done.71, f32[768]{0:T(1024)S(1)} %copy-done.53, f32[512]{0:T(512)S(1)} %copy-done.66, f32[1,512,768]{2,1,0:T(8,128)S(1)} %get-tuple-element.55, ...), kind=kOutput, calls=%fused_computation.167 | convolution fusion | flops 2428108288 | bytes 14183424 | tf_op jit(solution)/shard_map/snic,ijcd->snjd/dot_general | solution.py:31
  213.3 8.3 %convert_reduce_fusion = (f32[3072]{0:T(1024)}, bf16[512,3072]{1,0:T(8,128)(2,1)S(1)}) fusion(f32[3072]{0:T(1024)} %add.202, f32[512,3072,1]{1,0,2:T(8,128)} %copy-done.95, bf16[512,6,128]{0,2,1:T(8,128)(2,1)} %bitcast.397, bf16[3072,128,6]{1,0,2:T(8,128)(2,1)} %bitcast.355), kind=kOutput, calls=%fused_computation.7 | convolution fusion | flops 2436363264 | bytes 14966784 | tf_op jit(solution)/shard_map/snjd,ijcd->snic/dot_general | solution.py:42
  221.6 7.4 %multiply_reduce_fusion.3 = (f32[768]{0:T(1024)}, f32[512]{0:T(512)S(1)}, f32[512]{0:T(512)S(1)}, f32[768]{0:T(1024)}, f32[1,512,768]{2,1,0:T(8,128)S(1)}) fusion(f32[1,512,768]{2,1,0:T(8,128)S(1)} %get-tuple-element.55, f32[512]{0:T(512)S(1)} %copy-done.67, f32[512]{0:T(512)S(1)} %copy-done.59, f32[768]{0:T(1024)S(1)} %copy-done.54, ...), kind=kOutput, calls=%fused_computation.56 | convolution fusion | flops 2423387648 | bytes 13400064 | tf_op jit(solution)/shard_map/snjd,ijcd->snic/dot_general | solution.py:42
  236.2 4.9 fusion.49
  241.1 4.7 multiply_reduce_fusion
  253.0 7.0 %convert_bitcast_fusion = bf16[24,6,128,128]{2,3,0,1:T(8,128)(2,1)} fusion(bf16[512,6,128,1]{0,2,3,1:T(8,128)(2,1)S(1)} %bitcast.398, f32[512,3072,1]{1,0,2:T(8,128)} %copy-done.95, f32[3072]{0:T(1024)S(1)} %copy-done.79), kind=kOutput, calls=%fused_computation.17 | convolution fusion | flops 2427715584 | bytes 11808768 | tf_op jit(solution)/shard_map/snic,snjd->ijcd/dot_general | solution.py:50
  262.5 6.8 %copy.175 = bf16[24,6,128,128]{3,2,1,0:T(8,128)(2,1)} copy(bf16[24,6,128,128]{2,3,0,1:T(8,128)(2,1)} %convert_bitcast_fusion) | data formatting | bytes 9437184 | tf_op jit(solution)/shard_map/snic,snjd->ijcd/transpose | solution.py:50
  272.9 7.2 %convert_bitcast_fusion.1 = bf16[6,24,128,128]{2,3,0,1:T(8,128)(2,1)} fusion(bf16[512,6,128,1]{0,2,1,3:T(8,128)(2,1)} %bitcast.396, bf16[512,24,128,1]{2,1,0,3:T(8,128)(2,1)} %bitcast.371), kind=kOutput, calls=%fused_computation.18 | convolution fusion | flops 2418278400 | bytes 8650752 | tf_op jit(solution)/shard_map/snic,snjd->ijcd/dot_general | solution.py:50
  280.0 6.8 %copy.173 = bf16[6,24,128,128]{3,2,1,0:T(8,128)(2,1)} copy(bf16[6,24,128,128]{2,3,0,1:T(8,128)(2,1)} %convert_bitcast_fusion.1) | data formatting | bytes 9437184 | tf_op jit(solution)/shard_map/snic,snjd->ijcd/transpose | solution.py:50
  289.5 3.3 fusion.37
  300.9 3.3 fusion.36
  317.7 3.2 constant_dynamic-update-slice_fusion.1
  324.1 102.2 %reduce-scatter.3.cloned.1.call-done = bf16[440,16,128]{2,1,0:T(8,128)(2,1)} async-done(((bf16[440,128,128]{2,1,0:T(8,128)(2,1)}), bf16[440,16,128]{2,1,0:T(8,128)(2,1)}) %reduce-scatter.3.cloned.1.call-update) | async-done | bytes 1802256 | tf_op jit(solution)/shard_map/reduce_scatter | solution.py:270
  426.4 41.1 %reduce-scatter.5.cloned.1.call-done = bf16[110,16,128]{2,1,0:T(8,128)(2,1)} async-done(((bf16[440,16,128]{2,1,0:T(8,128)(2,1)}), bf16[110,16,128]{2,1,0:T(8,128)(2,1)}) %reduce-scatter.5.cloned.1.call-update) | async-done | bytes 450576 | tf_op jit(solution)/shard_map/reduce_scatter | solution.py:273
  469.8 34.0 %all-gather.12.cloned.1.call-done = bf16[110,128,128]{2,1,0:T(8,128)(2,1)} async-done(((bf16[110,16,128]{2,1,0:T(8,128)(2,1)}), bf16[110,128,128]{2,1,0:T(8,128)(2,1)}) %all-gather.12.cloned.1.call-update) | async-done | bytes 3604496 | tf_op jit(solution)/shard_map/all_gather | solution.py:298
  503.9 8.0 %convolution_convert_fusion.6 = bf16[110,128,16]{1,2,0:T(8,128)(2,1)} fusion(bf16[110,128,128]{2,1,0:T(8,128)(2,1)} %all-gather.12.cloned.1.call-done, f32[110,16,128]{2,1,0:T(8,128)S(1)} %copy-done.33), kind=kOutput, calls=%fused_computation.94 | convolution fusion | flops 346255360 | bytes 4956160 | tf_op jit(solution)/shard_map/bis,bcs->bic/dot_general | solution.py:310
  516.3 40.1 %all-reduce = (f32[13,768]{1,0:T(8,128)S(1)}, f32[2]{0:T(128)S(1)}) all-reduce(f32[13,768]{1,0:T(8,128)S(1)} %concatenate.8, f32[2]{0:T(128)S(1)} %pad_maximum_fusion), channel_id=1, replica_groups=mesh['dp'=4,'fsdp'=8] {'dp','fsdp'}, use_global_device_ids=true, to_apply=%region_28.0 | all-reduce | flops 9986 | bytes 79888 | tf_op jit(solution)/shard_map/psum | solution.py:294
  564.3 4.1 fusion.44
  568.5 6.6 %fusion.47 = f32[110,16,128]{2,1,0:T(8,128)} fusion(f32[110,16,128]{2,1,0:T(8,128)S(1)} %copy-done.16, bf16[110,128,128]{2,1,0:T(8,128)(2,1)S(1)} %copy-done.3, f32[110,16,128]{2,1,0:T(8,128)S(1)} %copy-done.34, f32[110]{0:T(128)S(1)} %get-tuple-element.51, f32[110]{0:T(128)S(1)} %get-tuple-element.49), kind=kOutput, calls=%fused_computation.92 | convolution fusion | flops 346705920 | bytes 6308720 | tf_op jit(solution)/shard_map/brc,bsc->brs/dot_general | solution.py:304
  575.1 8.0 %multiply_reduce_fusion.9 = (f32[110]{0:T(128)S(1)}, f32[110,128,16]{1,2,0:T(8,128)S(1)}) fusion(bf16[110,128,128]{1,2,0:T(8,128)(2,1)} %all-gather.14.cloned.1.call-done, f32[110,16,128]{2,1,0:T(8,128)S(1)} %copy-done), kind=kOutput, calls=%fused_computation.103 | convolution fusion | flops 346480512 | bytes 5407160 | tf_op jit(solution)/shard_map/brs,bsc->brc/dot_general | solution.py:314
  583.1 12.7 %all-reduce.1 = (f32[110]{0:T(128)S(1)}, f32[110]{0:T(128)S(1)}) all-reduce(f32[110]{0:T(128)S(1)} %get-tuple-element.61, f32[110]{0:T(128)S(1)} %copy-done.91), channel_id=1, replica_groups=mesh['dp'=4,'fsdp'=8] {'fsdp'}, use_global_device_ids=true, to_apply=%region_16.0 | all-reduce | flops 220 | bytes 1760 | tf_op jit(solution)/shard_map/psum | solution.py:315
  (322 shorter events, 115.1 us)
Async XLA Ops:
  7.2 567.9 %copy-start = (f32[110,16,128]{2,1,0:T(8,128)S(1)}, f32[110,16,128]{2,1,0:T(8,128)}, u32[]{:S(2)}) copy-start(f32[110,16,128]{2,1,0:T(8,128)} %param.19) | copy-start | bytes 2703364
  7.2 47.5 %all-gather.6.cloned.1.call-start = ((), (), s32[]{:S(2)}) async-start(), calls=%async_computation.2 | async-start | bytes 2252800 | tf_op jit(solution)/shard_map/all_gather | solution.py:107
  11.0 86.0 %all-gather.8.cloned.1.call-start = ((), (), s32[]{:S(2)}) async-start(), calls=%async_computation.3 | async-start | bytes 5603328 | tf_op jit(solution)/shard_map/all_gather | solution.py:103
  56.9 102.6 %all-gather.10.cloned.1.call-start = ((), (), s32[]{:S(2)}) async-start(), calls=%async_computation.4 | async-start | bytes 10616832 | tf_op jit(solution)/shard_map/all_gather | solution.py:103
  58.1 368.2 %reduce-scatter.3.cloned.1.call-start = ((), (), s32[]{:S(2)}) async-start(), calls=%async_computation.5 | async-start | bytes 16220160 | tf_op jit(solution)/shard_map/reduce_scatter | solution.py:270
  62.4 72.2 %copy-start.52 = (f32[768]{0:T(1024)}, f32[768]{0:T(1024)S(1)}, u32[]{:S(2)}) copy-start(f32[768]{0:T(1024)S(1)} %get-tuple-element.21) | copy-start | bytes 9220
  62.4 72.2 %copy-start.70 = (f32[768]{0:T(1024)}, f32[768]{0:T(1024)S(1)}, u32[]{:S(2)}) copy-start(f32[768]{0:T(1024)S(1)} %get-tuple-element.20) | copy-start | bytes 9220
  101.5 15.0 %copy-start.8 = (bf16[36,128,128]{2,1,0:T(8,128)(2,1)}, bf16[36,128,128]{2,1,0:T(8,128)(2,1)S(1)}, u32[]{:S(2)}) copy-start(bf16[36,128,128]{2,1,0:T(8,128)(2,1)S(1)} %get-tuple-element.43) | copy-start | bytes 3538948
  101.5 21.0 %copy-start.6 = (bf16[36,128,128]{2,1,0:T(8,128)(2,1)}, bf16[36,128,128]{2,1,0:T(8,128)(2,1)S(1)}, u32[]{:S(2)}) copy-start(bf16[36,128,128]{2,1,0:T(8,128)(2,1)S(1)} %get-tuple-element.44) | copy-start | bytes 3538948
  213.2 8.3 %copy-start.5 = (f32[1,512,768]{2,1,0:T(8,128)S(1)}, f32[1,512,768]{2,1,0:T(8,128)}, u32[]{:S(2)}) copy-start(f32[1,512,768]{2,1,0:T(8,128)} %copy-done.4) | copy-start | bytes 4718596
  213.2 8.3 %copy-start.25 = (bf16[1,512,768]{2,1,0:T(8,128)(2,1)S(1)}, bf16[1,512,768]{2,1,0:T(8,128)(2,1)}, u32[]{:S(2)}) copy-start(bf16[1,512,768]{2,1,0:T(8,128)(2,1)} %param.12) | copy-start | bytes 2359300
  213.2 8.3 %copy-start.54 = (f32[768]{0:T(1024)S(1)}, f32[768]{0:T(1024)}, u32[]{:S(2)}) copy-start(f32[768]{0:T(1024)} %copy-done.52) | copy-start | bytes 9220
  213.2 8.3 %copy-start.56 = (f32[768]{0:T(1024)S(1)}, f32[768]{0:T(1024)}, u32[]{:S(2)}) copy-start(f32[768]{0:T(1024)} %get-tuple-element.17) | copy-start | bytes 9220
  213.2 8.3 %copy-start.59 = (f32[512]{0:T(512)S(1)}, f32[512]{0:T(512)}, u32[]{:S(2)}) copy-start(f32[512]{0:T(512)} %copy-done.57) | copy-start | bytes 6148
  213.2 8.3 %copy-start.61 = (f32[512]{0:T(512)S(1)}, f32[512]{0:T(512)}, u32[]{:S(2)}) copy-start(f32[512]{0:T(512)} %fusion.62) | copy-start | bytes 6148
  213.2 8.3 %copy-start.64 = (f32[512]{0:T(512)S(1)}, f32[512]{0:T(512)}, u32[]{:S(2)}) copy-start(f32[512]{0:T(512)} %copy-done.63) | copy-start | bytes 6148
  213.3 8.3 %copy-start.67 = (f32[512]{0:T(512)S(1)}, f32[512]{0:T(512)}, u32[]{:S(2)}) copy-start(f32[512]{0:T(512)} %copy-done.65) | copy-start | bytes 6148
  213.3 8.3 %copy-start.69 = (f32[512]{0:T(512)S(1)}, f32[512]{0:T(512)}, u32[]{:S(2)}) copy-start(f32[512]{0:T(512)} %copy-done.68) | copy-start | bytes 6148
  213.3 8.3 %copy-start.81 = (f32[512]{0:T(512)S(1)}, f32[512]{0:T(512)}, u32[]{:S(2)}) copy-start(f32[512]{0:T(512)} %copy-done.80) | copy-start | bytes 6148
  213.3 8.3 %copy-start.83 = (f32[512]{0:T(512)S(1)}, f32[512]{0:T(512)}, u32[]{:S(2)}) copy-start(f32[512]{0:T(512)} %copy-done.82) | copy-start | bytes 6148
  236.2 9.6 %slice-start = ((s8[6291456]{0:T(1024)(128)(4,1)}), s8[4194304]{0:T(1024)(128)(4,1)S(1)}, s32[]{:S(2)}) async-start(s8[6291456]{0:T(1024)(128)(4,1)} %bitcast.328), calls=%async_computation.9 | async-start | bytes 8388608
  308.5 9.2 %slice-start.4 = ((s8[4718592]{0:T(1024)(128)(4,1)}), s8[524288]{0:T(1024)(128)(4,1)S(1)}, s32[]{:S(2)}) async-start(s8[4718592]{0:T(1024)(128)(4,1)} %bitcast.337), calls=%async_computation.13 | async-start | bytes 1048576
  324.0 179.8 %copy-start.33 = (f32[110,16,128]{2,1,0:T(8,128)S(1)}, f32[110,16,128]{2,1,0:T(8,128)}, u32[]{:S(2)}) copy-start(f32[110,16,128]{2,1,0:T(8,128)} %param.20) | copy-start | bytes 2703364
  324.0 143.5 %reduce-scatter.5.cloned.1.call-start = ((), (), s32[]{:S(2)}) async-start(), calls=%async_computation.6 | async-start | bytes 2252800 | tf_op jit(solution)/shard_map/reduce_scatter | solution.py:273
  426.3 77.5 %all-gather.12.cloned.1.call-start = ((), (), s32[]{:S(2)}) async-start(), calls=%async_computation.7 | async-start | bytes 4055040 | tf_op jit(solution)/shard_map/all_gather | solution.py:298
  469.7 42.2 %copy-start.47 = (f32[13,768]{1,0:T(8,128)S(1)}, f32[13,768]{1,0:T(8,128)}, u32[]{:S(2)}) copy-start(f32[13,768]{1,0:T(8,128)} %param.15) | copy-start | bytes 119812
  469.7 42.3 %copy-start.89 = (f32[110,2]{0,1:T(2,128)S(1)}, f32[110,2]{0,1:T(2,128)}, u32[]{:S(2)}) copy-start(f32[110,2]{0,1:T(2,128)} %param.21) | copy-start | bytes 2644
  469.8 42.3 %copy-start.10 = (bf16[36,128,128]{2,1,0:T(8,128)(2,1)S(1)}, bf16[36,128,128]{2,1,0:T(8,128)(2,1)}, u32[]{:S(2)}) copy-start(bf16[36,128,128]{2,1,0:T(8,128)(2,1)} %get-tuple-element.42) | copy-start | bytes 3538948
  469.8 105.3 %all-gather.14.cloned.1.call-start = ((), (), s32[]{:S(2)}) async-start(), calls=%async_computation.8 | async-start | bytes 4055040 | tf_op jit(solution)/shard_map/all_gather | solution.py:311
  513.3 43.7 %copy-start.51 = (f32[13,768]{1,0:T(8,128)S(1)}, f32[13,768]{1,0:T(8,128)}, u32[]{:S(2)}) copy-start(f32[13,768]{1,0:T(8,128)} %param.16) | copy-start | bytes 119812
  514.5 45.8 %copy-start.31 = (bf16[6,6,128,128]{3,2,0,1:T(8,128)(2,1)S(1)}, bf16[6,6,128,128]{3,2,0,1:T(8,128)(2,1)}, u32[]{:S(2)}) copy-start(bf16[6,6,128,128]{3,2,0,1:T(8,128)(2,1)} %copy.156) | copy-start | bytes 3538948
  575.1 20.7 %copy-start.15 = (f32[110,16,128]{2,1,0:T(8,128)S(1)}, f32[110,16,128]{2,1,0:T(8,128)}, u32[]{:S(2)}) copy-start(f32[110,16,128]{2,1,0:T(8,128)} %param.14) | copy-start | bytes 2703364
  (78 other events, 286.0 us)
Sparse Core Ops, SparseCore 0:
  11.1 43.5 all-gather.5
  57.1 39.7 all-gather.7
  98.8 60.5 all-gather.9
  324.1 102.1 reduce-scatter.2
  428.6 38.8 reduce-scatter.4
  469.9 33.9 all-gather.11
  512.0 35.2 all-gather.13
where the time goes:
time: 611 us; the launch traced here: 604 us
  waiting for transfers between devices  276 us (45%)
  matrix products  119 us (19%)
  local copies, waits for them, and re-layouts  115 us (19%)
  blocking collectives  52.8 us (9%)
  other arithmetic  22.5 us (4%)
  between operations  17.5 us (3%)
    reduce_scatter x1, waiting for transfers between devices, local(): lax.psum_scatter(all_terms.astype(jnp.bfloat16), 'fsdp', scatter_dimensio...  102 us
    all_gather x2, waiting for transfers between devices, widen(): return lax.all_gather(tile_part, 'fsdp', axis=1, tiled=True)  55 us
    all_gather x1, waiting for transfers between devices, gather_tiles(): lax.all_gather(weights.astype(jnp.bfloat16), 'dp', axis=0, tiled=True)  43.7 us
    reduce_scatter x1, waiting for transfers between devices, local(): lax.psum_scatter(inner_part, 'dp', scatter_dimension=0, tiled=True)  41.1 us
    psum x1, blocking collectives, local(): lax.psum((local_vectors, local_norms), ('dp', 'fsdp'))  40.1 us
    reshape x12, local copies, waits for them, and re-layouts, forward_tiles(): tiles.reshape(rows_in.shape[-1] // tile_size, out_width // tile_size, til...  34.5 us
    all_gather x1, waiting for transfers between devices, local(): lax.all_gather(grad_rows.astype(jnp.bfloat16), 'fsdp', axis=1, tiled=True)  34 us
    dot_general x6, matrix products, gradient_tiles(): jnp.einsum('snic,snjd->ijcd', left_shaped, right_shaped, preferred_elemen...  24.5 us
  transfers between devices with their start and end apart: 7, of which 6 were waited for; matrix products, arithmetic and copies ran while one was open for 10% of the time, Pallas kernels for 0%

commit v1 on v0

v1 whole, which is shorter than its diff:
```python
import functools

import jax
import jax.numpy as jnp
from jax import lax
from jax.experimental import pallas as pl
from jax.experimental.pallas import tpu as pltpu
from jax.sharding import PartitionSpec as P

D = 768
H = 12
HD = 64
FF = 3072
K = 256
NMAX = 512
TB = 128
LANES = 128
PART = 110
GROUPS = 8

EPS_NORM = 1e-05
EPS_STEP = 1e-06
STEP_RATE = 0.25
MOMENT_DECAY = 0.9
SQRT_HALF = 0.7071067811865476
INV_SQRT_TWO_PI = 0.3989422804014327
SCALE = HD ** (-0.5)

QUARTER = (D // TB) ** 2
ATT = 4 * QUARTER + NMAX // TB * (K // TB)
HID = D // TB * (FF // TB)
NBLK = ATT + 2 * HID
BF = jnp.bfloat16
F32 = jnp.float32

ANY = pl.BlockSpec(memory_space=pl.ANY)
VM = pl.BlockSpec(memory_space=pltpu.VMEM)
SM = pl.BlockSpec(memory_space=pltpu.SMEM)


def sds(shape, dtype):
    return jax.ShapeDtypeStruct(shape, dtype)


def nn(a, b):
    return lax.dot_general(a, b, (((1,), (0,)), ((), ())), preferred_element_type=F32)


def nt(a, b):
    return lax.dot_general(a, b, (((1,), (1,)), ((), ())), preferred_element_type=F32)


def tn(a, b):
    return lax.dot_general(a, b, (((0,), (0,)), ((), ())), preferred_element_type=F32)


def layer_norm(value):
    centre = jnp.mean(value, axis=-1, keepdims=True)
    shifted = value - centre
    spread = jnp.mean(shifted * shifted, axis=-1, keepdims=True)
    inverse = lax.rsqrt(spread + EPS_NORM)
    return shifted * inverse, inverse


def norm_backward(grad_out, normed, inverse, gain):
    scaled = grad_out * gain
    centred = scaled - jnp.mean(scaled, axis=-1, keepdims=True)
    return inverse * (centred - normed * jnp.mean(scaled * normed, axis=-1, keepdims=True))


def column_sum(value):
    return jnp.sum(value.astype(F32), axis=0, keepdims=True)


def valid_rows(length, width):
    return lax.broadcasted_iota(jnp.int32, (NMAX, width), 0) < length


def fetch(sc, pieces, steps, parts, raw, sem):
    for step in range(steps):
        for at, part in enumerate(parts):

            @pl.when(sc[8 + part] == step)
            def _():
                for s in range(GROUPS):
                    pltpu.make_async_copy(pieces[step * GROUPS + s], raw.at[at, s], sem.at[at, s]).start()


def fetched(pieces, raw, sem, at):
    for s in range(GROUPS):
        pltpu.make_async_copy(pieces[s], raw.at[at, s], sem.at[at, s]).wait()


def lay_out(slots, raw, at, first, count, dst, dst_first, per_row):
    def body(n, carry):
        b = n + dst_first
        i, j = b // per_row, b % per_row
        for r in range(GROUPS):
            dst[pl.ds(pl.multiple_of(i * TB + 16 * r, 16), 16), pl.ds(pl.multiple_of(j * TB, TB), TB)] = raw[
                at, slots[r], first + n
            ]
        return carry

    lax.fori_loop(0, count, body, 0)


def splitter(sc):
    even = sc[13] == 0
    mine = [jnp.where(even, sc[2 * m], sc[2 * m + 1]) for m in range(4)]
    other = [jnp.where(even, sc[2 * m + 1], sc[2 * m]) - 4 for m in range(4)]

    def put(keep, send, b, value):
        low = value.astype(BF)
        for m in range(4):
            first = low[32 * m : 32 * m + 16]
            second = low[32 * m + 16 : 32 * m + 32]
            keep[mine[m], b] = jnp.where(even, first, second)
            send[other[m], b] = jnp.where(even, second, first)

    return put


def attention_forward(sc, tok, vec, *rest):
    pieces = rest[:24]
    (q_o, k_o, v_o, ks_o, vs_o, lse_o, mix_o, mixt_o, nf_o, inv_o, norm_o, wq_o, wk_o, wv_o, wo_o, cm_o) = rest[24:40]
    raw, sem = rest[40:]
    fetch(sc, pieces, 3, (0, 1), raw, sem)
    slots = [sc[r] for r in range(GROUPS)]
    nb = D // TB
    for at in (0, 1):
        fetched(pieces, raw, sem, at)
    for m, dst in enumerate((wq_o, wk_o, wv_o)):
        lay_out(slots, raw, 0, m * QUARTER, QUARTER, dst, 0, nb)
    head = PART - 3 * QUARTER
    lay_out(slots, raw, 0, 3 * QUARTER, head, wo_o, 0, nb)
    lay_out(slots, raw, 1, 0, QUARTER - head, wo_o, head, nb)
    lay_out(slots, raw, 1, QUARTER - head, ATT - 4 * QUARTER, cm_o, 0, K // TB)
    x = tok[...]
    q_o[...] = (nn(x, wq_o[...]) + vec[0:1]).astype(BF)
    k_o[...] = (nn(x, wk_o[...]) + vec[1:2]).astype(BF)
    v_o[...] = (nn(x, wv_o[...]) + vec[2:3]).astype(BF)
    masked = jnp.where(valid_rows(sc[12], K), cm_o[...], jnp.zeros((), BF))
    ks_o[...] = tn(masked, k_o[...]).astype(BF)
    vs_o[...] = tn(masked, v_o[...]).astype(BF)
    for n, ref in enumerate((ks_o, vs_o)):
        square = jnp.square(ref[...].astype(F32))
        total = jnp.sum(jnp.sum(square, axis=0, keepdims=True), axis=1, keepdims=True)
        norm_o[n : n + 1, :] = jnp.broadcast_to(jnp.sqrt(total), (1, LANES))
    lane = lax.broadcasted_iota(jnp.int32, (K, LANES), 1) < HD
    for p in range(H // 2):
        cols = slice(p * LANES, (p + 1) * LANES)
        q_p, ks_p, vs_p = q_o[:, cols], ks_o[:, cols], vs_o[:, cols]
        zero = jnp.zeros((), BF)
        parts, values = [], []
        for half in range(2):
            sel = lane if half == 0 else jnp.logical_not(lane)
            scores = nt(jnp.where(sel, ks_p, zero), q_p) * SCALE
            peak = jnp.max(scores, axis=0, keepdims=True)
            raised = jnp.exp(scores - peak)
            total = jnp.sum(raised, axis=0, keepdims=True)
            lse_o[2 * p + half : 2 * p + half + 1, :] = peak + jnp.log(total)
            parts.append((raised * (1.0 / total)).astype(BF))
            values.append(jnp.where(sel, vs_p, zero))
        mixt = tn(jnp.concatenate(values, axis=0), jnp.concatenate(parts, axis=0)).astype(BF)
        mixt_o[cols, :] = mixt
        mix_o[:, cols] = mixt.T
    branch = nn(mix_o[...], wo_o[...]) + vec[3:4]
    normed, inverse = layer_norm(x.astype(F32) + branch)
    nf_o[...] = normed
    inv_o[...] = jnp.broadcast_to(inverse, (NMAX, LANES))


STEP = 256


def ffn_forward(sc, nf, cot, vec, *rest):
    pieces = rest[:32]
    (out_o, gs_o, gsl_o, slope_o, fl_o, keep_o, send_o, sums_o, wh_o, wr_o) = rest[32:42]
    raw, sem, wh, wr, act, acc, osem = rest[42:]
    fetch(sc, pieces, 4, (1, 2, 3), raw, sem)
    slots = [sc[r] for r in range(GROUPS)]
    put = splitter(sc)
    nh, nd = FF // TB, D // TB
    for at in range(3):
        fetched(pieces, raw, sem, at)
    head = ATT - PART
    lay_out(slots, raw, 0, head, PART - head, wh, 0, nh)
    rest_h = HID - (PART - head)
    lay_out(slots, raw, 1, 0, rest_h, wh, PART - head, nh)
    lay_out(slots, raw, 1, rest_h, PART - rest_h, wr, 0, nd)
    lay_out(slots, raw, 2, 0, PART, wr, PART - rest_h, nd)
    copies = [pltpu.make_async_copy(wh, wh_o, osem.at[0]), pltpu.make_async_copy(wr, wr_o, osem.at[1])]
    for copy in copies:
        copy.start()
    normed = nf[...]
    first = normed * vec[4:5] + vec[5:6]
    fl_o[...] = first.astype(BF)
    acc[...] = jnp.zeros((NMAX, D), F32)
    for g in range(FF // STEP):
        cols = slice(g * STEP, (g + 1) * STEP)
        row, off = 6 + (g * STEP) // D, (g * STEP) % D
        hidden = nn(fl_o[...], wh[:, cols]) + vec[row : row + 1, off : off + STEP]
        phi = 0.5 * (1.0 + lax.erf(hidden * SQRT_HALF))
        low = (hidden * phi).astype(BF)
        act[:, cols] = low
        slope_o[:, cols] = phi + hidden * INV_SQRT_TWO_PI * jnp.exp(-0.5 * hidden * hidden)
        acc[...] += nn(low, wr[cols, :])
    second = acc[...] + vec[10:11]
    valid = valid_rows(sc[12], D)
    normed2, inverse2 = layer_norm(first + second)
    result = normed2 * vec[11:12] + vec[12:13]
    out_o[...] = jnp.where(valid, result, 0.0).astype(BF)
    grad_result = jnp.where(valid, cot[...].astype(F32), 0.0)
    sums_o[1:2, :] = column_sum(grad_result * normed2)
    sums_o[2:3, :] = column_sum(grad_result)
    grad_second = norm_backward(grad_result, normed2, inverse2, vec[11:12])
    gs_o[...] = grad_second
    low = grad_second.astype(BF)
    gsl_o[...] = low
    sums_o[0:1, :] = column_sum(low)
    for g in range(FF // STEP):
        terms = tn(act[:, g * STEP : (g + 1) * STEP], gsl_o[...])
        for i in range(STEP // TB):
            for j in range(nd):
                put(keep_o, send_o, (g * (STEP // TB) + i) * nd + j, terms[i * TB : (i + 1) * TB, j * TB : (j + 1) * TB])
    for copy in copies:
        copy.wait()


def ffn_backward(gs, gsl, slope, nf, inv, vec, wh, wr, wo, gh_o, gr_o, gb_o, gm_o, sums_o, acc):
    low = gsl[...]
    acc[...] = jnp.zeros((NMAX, D), F32)
    for g in range(FF // STEP):
        cols = slice(g * STEP, (g + 1) * STEP)
        grad_active = nt(low, wr[cols, :])
        gh = (grad_active * slope[:, cols]).astype(BF)
        gh_o[:, cols] = gh
        row, off = (g * STEP) // D, (g * STEP) % D
        sums_o[3 + row : 4 + row, off : off + STEP] = column_sum(gh)
        acc[...] += nt(gh, wh[:, cols])
    grad_first = gs[...] + acc[...]
    normed = nf[...]
    sums_o[1:2, :] = column_sum(grad_first * normed)
    sums_o[2:3, :] = column_sum(grad_first)
    grad_resid = norm_backward(grad_first, normed, inv[:, 0:1], vec[4:5])
    gr_o[...] = grad_resid
    branch = grad_resid.astype(BF)
    gb_o[...] = branch
    sums_o[0:1, :] = column_sum(branch)
    gm_o[...] = nt(branch, wo[...]).astype(BF)


def attention_backward(q, ks, vs, lse, gm, gq_o, gks_o, gvs_o):
    lane = lax.broadcasted_iota(jnp.int32, (K, LANES), 1) < HD
    zero = jnp.zeros((), BF)
    for p in range(H // 2):
        cols = slice(p * LANES, (p + 1) * LANES)
        q_p, ks_p, vs_p, gm_p = q[:, cols], ks[:, cols], vs[:, cols], gm[:, cols]
        keys, grads, gvs, gks = [], [], [], []
        for half in range(2):
            sel = lane if half == 0 else jnp.logical_not(lane)
            key = jnp.where(sel, ks_p, zero)
            attend = jnp.exp(nt(key, q_p) * SCALE - lse[2 * p + half : 2 * p + half + 1, :])
            grad_attend = nt(jnp.where(sel, vs_p, zero), gm_p)
            mean = jnp.sum(grad_attend * attend, axis=0, keepdims=True)
            grad_scores = (attend * (grad_attend - mean)).astype(BF)
            gvs.append(nn(attend.astype(BF), gm_p))
            gks.append(nn(grad_scores, q_p))
            keys.append(key)
            grads.append(grad_scores)
        gvs_o[:, cols] = jnp.where(lane, gvs[0], gvs[1]).astype(BF)
        gks_o[:, cols] = (jnp.where(lane, gks[0], gks[1]) * SCALE).astype(BF)
        gqt = tn(jnp.concatenate(keys, axis=0), jnp.concatenate(grads, axis=0)) * SCALE
        gq_o[:, cols] = gqt.astype(BF).T


def projection_backward(sc, tok, k, v, gq, gks, gvs, gb, gr, mixt, cm, wq, wk, wv, in_o, keep_o, send_o, sums_o):
    put = splitter(sc)
    nd, nk = D // TB, K // TB
    masked = jnp.where(valid_rows(sc[12], K), cm[...], jnp.zeros((), BF))
    gk = nn(masked, gks[...]).astype(BF)
    gv = nn(masked, gvs[...]).astype(BF)
    tokt = tok[...].T
    lhs = (tokt, tokt, tokt, mixt[...])
    for m, grad in enumerate((gq[...], gk, gv, gb[...])):
        if m < 3:
            sums_o[m : m + 1, :] = column_sum(grad)
        terms = nn(lhs[m], grad)
        for i in range(nd):
            for j in range(nd):
                put(keep_o, send_o, m * QUARTER + i * nd + j, terms[i * TB : (i + 1) * TB, j * TB : (j + 1) * TB])
    comp = nt(k[...], gks[...]) + nt(v[...], gvs[...])
    comp = jnp.where(valid_rows(sc[12], K), comp, 0.0)
    for i in range(NMAX // TB):
        for j in range(nk):
            put(keep_o, send_o, 4 * QUARTER + i * nk + j, comp[i * TB : (i + 1) * TB, j * TB : (j + 1) * TB])
    total = gr[...] + nt(gq[...], wq[...])
    total = total + nt(gk, wk[...])
    total = total + nt(gv, wv[...])
    in_o[...] = total.astype(BF)


def hidden_terms(sc, fl, gh, keep_o, send_o):
    put = splitter(sc)
    nh, nd = FF // TB, D // TB
    flt = fl[...].T
    for g in range(FF // STEP):
        terms = nn(flt, gh[:, g * STEP : (g + 1) * STEP])
        for i in range(nd):
            for j in range(STEP // TB):
                put(keep_o, send_o, i * nh + g * (STEP // TB) + j, terms[i * TB : (i + 1) * TB, j * TB : (j + 1) * TB])


def step_kernel(sc, dec, own, lroot, lstat, rstat, *rest):
    gp, rp = rest[:GROUPS], rest[GROUPS : 2 * GROUPS]
    nl_o, nr_o, pre_o, sq_o = rest[2 * GROUPS : 2 * GROUPS + 4]
    graw, rraw, sem = rest[2 * GROUPS + 4 :]
    for s in range(GROUPS):
        pltpu.make_async_copy(rp[s], rraw.at[s], sem.at[1, s]).start()
        pltpu.make_async_copy(gp[s], graw.at[s], sem.at[0, s]).start()
    slots = [sc[r] for r in range(GROUPS)]
    me = sc[14]
    pick_row = lax.broadcasted_iota(jnp.int32, (16, TB), 0) + me * 16
    select = (lax.broadcasted_iota(jnp.int32, (16, TB), 1) == pick_row).astype(BF)
    for s in range(GROUPS):
        pltpu.make_async_copy(rp[s], rraw.at[s], sem.at[1, s]).wait()
        pltpu.make_async_copy(gp[s], graw.at[s], sem.at[0, s]).wait()

    def body(b, carry):
        grad = jnp.concatenate([graw[slots[r], b] for r in range(GROUPS)], axis=0)
        right = jnp.concatenate([rraw[slots[r], b] for r in range(GROUPS)], axis=0)
        rows = own[b].astype(BF)
        across = nt(jnp.concatenate([rows, select], axis=0), grad)
        decay = dec[2 * b]
        nl_o[b] = decay * lstat[b] + (1.0 - decay) * across[:16]
        root = lroot[b]
        high = root.astype(BF)
        rest_root = (root - high.astype(F32)).astype(BF)
        down = nn(jnp.concatenate([high, rest_root, across[16:].astype(BF)], axis=0), grad)
        decay = dec[2 * b + 1]
        nr_o[b] = decay * rstat[b] + (1.0 - decay) * down[32:]
        mid = down[:16] + down[16:32]
        high = mid.astype(BF)
        rest_mid = (mid - high.astype(F32)).astype(BF)
        last = nn(jnp.concatenate([high, rest_mid], axis=0), right)
        pre = last[:16] + last[16:]
        pre_o[b] = pre
        sq_o[pl.ds(b, 1), :] = jnp.sum(pre * pre, axis=0, keepdims=True)
        return carry

    lax.fori_loop(0, PART, body, 0, unroll=2)


def call(kernel, ins, outs, in_specs, out_specs=None, scratch=(), limit=60, flops=0, nbytes=0):
    return pl.pallas_call(
        kernel,
        out_shape=outs,
        in_specs=in_specs,
        out_specs=out_specs if out_specs is not None else [VM] * len(outs),
        scratch_shapes=list(scratch),
        compiler_params=pltpu.CompilerParams(vmem_limit_bytes=limit * 1024 * 1024),
        cost_estimate=pl.CostEstimate(flops=flops, bytes_accessed=nbytes, transcendentals=0),
    )(*ins)


SLOT_TABLE = (0, 4, 1, 6, 2, 5, 3, 7)


def slot_of(code, core):
    other, x, y = code & 1, (code >> 1) & 1, code >> 2
    return 4 * other + jnp.where((other ^ core) == 0, x + 2 * y, y + 2 * x)


def toward(x, move):
    return lax.ppermute(x, "fsdp", [(i, move(i)) for i in range(GROUPS)])


def near(x):
    return toward(x, lambda i: i ^ 2 if i % 2 == 0 else i ^ 4)


def far(x):
    return toward(x, lambda i: i ^ 4 if i % 2 == 0 else i ^ 2)


def sibling(x):
    return toward(x, lambda i: i ^ 1)


def along(x, pairs):
    return lax.ppermute(x, "dp", pairs)


def plane_gather(own):
    a = near(own)
    b = far(own)
    c = far(a)
    d = sibling(jnp.stack([own, a, b, c]))
    return [own, a, b, c] + [d[i] for i in range(4)]


def chosen(index, options):
    value = options[0]
    for i in range(1, len(options)):
        value = jnp.where(index == i, options[i], value)
    return value


def gather_weights(narrow):
    me = lax.axis_index("dp")
    up, down = [(0, 1), (1, 2), (2, 3)], [(3, 2), (2, 1), (1, 0)]
    u1, d1 = along(narrow, up), along(narrow, down)
    u2, d2 = along(u1, up), along(d1, down)
    u3, d3 = along(u2, up), along(d2, down)
    shards = [
        narrow,
        chosen(me, [d1, u1, u1, u2]),
        chosen(me, [d2, d1, u2, u3]),
        chosen(me, [d3, d2, d1, u1]),
    ]
    steps = chosen(me, [jnp.array(row, jnp.int32) for row in ((0, 1, 2, 3), (1, 0, 2, 3), (2, 1, 0, 3), (2, 1, 3, 0))])
    return [piece for shard in shards for piece in plane_gather(shard)], steps


def added(a, b):
    return (a.astype(F32) + b.astype(F32)).astype(BF)


def plane_scatter(keep, send):
    got = sibling(send)
    own = added(keep[0], got[0])
    first = added(keep[1], got[1])
    pair = added(keep[2:4], got[2:4])
    back = far(pair)
    first = added(first, back[1])
    last = near(first)
    return own.astype(F32) + back[0].astype(F32) + last.astype(F32)


def line_scatter(part, even_at, odd_at):
    for_even, for_odd = part
    down = along(for_even, [(1, 0), (3, 2)])
    up = along(for_odd, [(0, 1), (2, 3)])
    for_even, for_odd = added(for_even, down), added(for_odd, up)
    far_even = along(for_even, [(even_at ^ 2, even_at)])
    far_odd = along(for_odd, [(odd_at ^ 2, odd_at)])
    return for_even.astype(F32) + far_even.astype(F32), for_odd.astype(F32) + far_odd.astype(F32)


def plane_sum(x):
    for bit in (1, 2, 4):
        x = x + toward(x, lambda i, bit=bit: i ^ bit)
    return x


def whole_sum(x):
    x = plane_sum(x)
    for bit in (1, 2):
        x = x + along(x, [(i, i ^ bit) for i in range(4)])
    return x


def local(
    tokens,
    cotangent,
    lengths,
    weights,
    vectors,
    moments,
    left_stats,
    right_stats,
    left_root,
    right_root,
    decays,
):
    dp, fsdp = lax.axis_size("dp"), lax.axis_size("fsdp")
    assert tokens.shape[0] == 1
    staged = (dp, fsdp) == (4, GROUPS)
    seq_total = tokens.shape[0] * dp * fsdp
    tok, cot = tokens[0], cotangent[0]
    narrow = weights.astype(BF)
    if staged:
        me = lax.axis_index("fsdp")
        core = lax.rem(me, 2)
        slots = slot_of(jnp.arange(GROUPS, dtype=jnp.int32) ^ me, core)
        pieces, steps = gather_weights(narrow)
        roots = plane_gather(right_root.astype(BF))
    else:
        me = jnp.int32(0)
        core = jnp.int32(0)
        slots = slot_of(jnp.arange(GROUPS, dtype=jnp.int32), core)
        full = lax.all_gather(lax.all_gather(narrow, "dp", axis=0, tiled=True), "fsdp", axis=1, tiled=True)
        full = full.reshape(NBLK // PART, PART, GROUPS, TB // GROUPS, TB)
        place = [SLOT_TABLE.index(s) for s in range(GROUPS)]
        pieces = [full[t, :, place[s]] for t in range(NBLK // PART) for s in range(GROUPS)]
        steps = jnp.arange(4, dtype=jnp.int32)
    scalars = jnp.concatenate([slots, steps, lengths, core[None], me[None]]).astype(jnp.int32)

    act = sds((NMAX, D), BF)
    wide = sds((NMAX, D), F32)
    summary = sds((K, D), BF)
    square = sds((D, D), BF)
    row16 = TB // GROUPS
    piece = pltpu.VMEM((2, GROUPS, PART, row16, TB), BF)
    (q, k, v, ks, vs, lse, mix, mixt, nf, inv, norms, wq, wk, wv, wo, cm) = call(
        attention_forward,
        [scalars, tok, vectors] + pieces[:24],
        [act, act, act, summary, summary, sds((H, NMAX), F32), act, sds((D, NMAX), BF), wide,
         sds((NMAX, LANES), F32), sds((2, LANES), F32), square, square, square, square, sds((NMAX, K), BF)],
        [SM, VM, VM] + [ANY] * 24,
        scratch=[piece, pltpu.SemaphoreType.DMA((2, GROUPS))],
        limit=40, flops=5 * 10**9, nbytes=10**7,
    )
    del mix
    terms = sds((4, HID, row16, TB), BF)
    (out, gs, gsl, slope, fl, r_keep, r_send, sums_c, wh, wr) = call(
        ffn_forward,
        [scalars, nf, cot, vectors] + pieces,
        [act, wide, act, sds((NMAX, FF), F32), act, terms, terms, sds((3, D), F32), sds((D, FF), BF), sds((FF, D), BF)],
        [SM, VM, VM, VM] + [ANY] * 32,
        [VM] * 8 + [ANY] * 2,
        scratch=[
            pltpu.VMEM((3, GROUPS, PART, row16, TB), BF),
            pltpu.SemaphoreType.DMA((3, GROUPS)),
            pltpu.VMEM((D, FF), BF),
            pltpu.VMEM((FF, D), BF),
            pltpu.VMEM((NMAX, FF), BF),
            pltpu.VMEM((NMAX, D), F32),
            pltpu.SemaphoreType.DMA((2,)),
        ],
        limit=58, flops=8 * 10**9, nbytes=3 * 10**7,
    )
    gh, gr, gb, gm, sums_b = call(
        ffn_backward,
        [gs, gsl, slope, nf, inv, vectors, wh, wr, wo],
        [sds((NMAX, FF), BF), wide, act, act, sds((3 + FF // D, D), F32)],
        [VM] * 9,
        scratch=[pltpu.VMEM((NMAX, D), F32)],
        limit=44, flops=6 * 10**9, nbytes=2 * 10**7,
    )
    gq, gks, gvs = call(
        attention_backward, [q, ks, vs, lse, gm], [act, summary, summary], [VM] * 5,
        limit=32, flops=4 * 10**9, nbytes=4 * 10**6,
    )
    a_terms = sds((4, ATT, row16, TB), BF)
    in_grads, a_keep, a_send, sums_a = call(
        projection_backward,
        [scalars, tok, k, v, gq, gks, gvs, gb, gr, mixt, cm, wq, wk, wv],
        [act, a_terms, a_terms, sds((3, D), F32)],
        [SM] + [VM] * 13,
        limit=40, flops=5 * 10**9, nbytes=2 * 10**7,
    )
    h_keep, h_send = call(
        hidden_terms, [scalars, fl, gh], [terms, terms], [SM, VM, VM],
        limit=40, flops=3 * 10**9, nbytes=10**7,
    )

    local_vectors = jnp.concatenate([sums_a, sums_b, sums_c], axis=0)
    local_norms = norms[:, 0]
    if staged:
        z = lax.axis_index("dp")
        r_rows = plane_scatter(r_keep, r_send).astype(BF)
        a_rows = plane_scatter(a_keep, a_send).astype(BF)
        h_rows = plane_scatter(h_keep, h_send).astype(BF)
        cut_r = 3 * PART - (ATT + HID)
        cut_h = 2 * PART - ATT
        r_two, r_three = line_scatter((r_rows[:cut_r], r_rows[cut_r:]), 2, 3)
        a_zero, a_one = line_scatter((a_rows[:PART], a_rows[PART:]), 0, 1)
        h_two, h_one = line_scatter((h_rows[cut_h:], h_rows[:cut_h]), 2, 1)
        total = chosen(
            z, [a_zero, jnp.concatenate([a_one, h_one]), jnp.concatenate([h_two, r_two]), r_three]
        )
        grad_rows = total / seq_total
        packed = jnp.concatenate([local_vectors, jnp.pad(local_norms[None], ((0, 0), (0, D - 2)))], axis=0)
        packed = whole_sum(packed)
        vector_total, norm_totals = packed[:-1], packed[-1, :2]
        blocks = plane_gather(grad_rows.astype(BF))
        rows = sds(weights.shape, F32)
        new_left, new_right, precond, squares = call(
            step_kernel,
            [scalars, decays.reshape(-1), grad_rows, left_root, left_stats, right_stats] + blocks + roots,
            [rows, rows, rows, sds((PART, LANES), F32)],
            [SM, SM] + [VM] * 4 + [ANY] * 16,
            scratch=[
                pltpu.VMEM((GROUPS, PART, row16, TB), BF),
                pltpu.VMEM((GROUPS, PART, row16, TB), BF),
                pltpu.SemaphoreType.DMA((2, GROUPS)),
            ],
            limit=32, flops=10**9, nbytes=10**7,
        )
        both = jnp.stack([jnp.sum(squares, axis=1), jnp.sum(weights * weights, axis=(1, 2))])
        precond_squares, weight_squares = plane_sum(both)
    else:
        def join(keep, send):
            both = jnp.concatenate([keep, send], axis=0)
            return jnp.stack([both[s] for s in SLOT_TABLE], axis=1).reshape(-1, TB, TB)

        every = jnp.concatenate([join(a_keep, a_send), join(h_keep, h_send), join(r_keep, r_send)], axis=0)
        inner = lax.psum_scatter(every, "fsdp", scatter_dimension=1, tiled=True)
        total = lax.psum_scatter(inner, "dp", scatter_dimension=0, tiled=True).astype(F32)
        grad_rows = total / seq_total
        vector_total, norm_totals = lax.psum((local_vectors, local_norms), ("dp", "fsdp"))
        high = lax.Precision.HIGHEST
        whole = lax.all_gather(grad_rows.astype(BF), "fsdp", axis=1, tiled=True).astype(F32)
        count = grad_rows.shape[1]
        slab = lax.dynamic_slice_in_dim(whole, lax.axis_index("fsdp") * count, count, 2)
        gram_left = jnp.einsum("brc,bsc->brs", grad_rows, whole, precision=high)
        gram_right = jnp.einsum("bic,bis->bcs", slab, whole, precision=high)
        decay_left = decays[:, 0][:, None, None]
        decay_right = decays[:, 1][:, None, None]
        new_left = decay_left * left_stats + (1.0 - decay_left) * gram_left
        new_right = decay_right * right_stats + (1.0 - decay_right) * gram_right
        columns = jnp.einsum("bis,bcs->bic", whole, right_root, precision=high)
        applied = lax.all_gather(columns.astype(BF), "fsdp", axis=2, tiled=True).astype(F32)
        precond = jnp.einsum("brs,bsc->brc", left_root, applied, precision=high)
        precond_squares, weight_squares = lax.psum(
            (jnp.sum(precond * precond, axis=(1, 2)), jnp.sum(weights * weights, axis=(1, 2))), "fsdp"
        )
    vector_grad = vector_total / seq_total
    summary_norms = norm_totals / seq_total
    tile_area = TB * TB
    weight_scale = jnp.sqrt(weight_squares / tile_area)
    precond_scale = lax.rsqrt(precond_squares / tile_area + EPS_STEP)
    new_weights = weights - STEP_RATE * (weight_scale * precond_scale)[:, None, None] * precond
    new_moments = MOMENT_DECAY * moments + (1.0 - MOMENT_DECAY) * vector_grad
    row_scale = jnp.sqrt(jnp.mean(jnp.square(vectors), axis=1, keepdims=True))
    moment_scale = lax.rsqrt(jnp.mean(jnp.square(new_moments), axis=1, keepdims=True) + EPS_STEP)
    new_vectors = vectors - STEP_RATE * row_scale * new_moments * moment_scale
    return (
        out[None],
        in_grads[None],
        new_weights,
        grad_rows,
        new_left,
        new_right,
        new_vectors,
        new_moments,
        summary_norms,
    )


def solution(mesh):
    in_specs = (
        P(("dp", "fsdp"), None, None),
        P(("dp", "fsdp"), None, None),
        P(("dp", "fsdp")),
        P("dp", "fsdp", None),
        P(),
        P(),
        P("dp", "fsdp", None),
        P("dp", "fsdp", None),
        P("dp", "fsdp", None),
        P("dp", "fsdp", None),
        P("dp", None),
    )
    out_specs = (
        P(("dp", "fsdp"), None, None),
        P(("dp", "fsdp"), None, None),
        P("dp", "fsdp", None),
        P("dp", "fsdp", None),
        P("dp", "fsdp", None),
        P("dp", "fsdp", None),
        P(),
        P(),
        P(),
    )
    return jax.shard_map(local, mesh=mesh, in_specs=in_specs, out_specs=out_specs, check_vma=False)
```

time: 611 us -> 414 us (0.68)
  matrix products: 119 us -> 0 us
  waiting for transfers between devices: 276 us -> 162 us
  Pallas kernels: 0 us -> 110 us
  local copies, waits for them, and re-layouts: 115 us -> 25.1 us
  starting transfers between devices: 0.29 us -> 84.3 us
  blocking collectives: 52.8 us -> 0 us
  between operations: 17.5 us -> 2.85 us
    ppermute x0 -> x59, waiting for transfers between devices: none -> 162 us  [the longest x39 109 us: toward(): return lax.ppermute(x, 'fsdp', [(i, move(i)) for i in range(GROUPS)])]
    reduce_scatter x2 -> x0, waiting for transfers between devices: 143 us -> none  [the longest x1 102 us: local(): lax.psum_scatter(all_terms.astype(jnp.bfloat16), 'fsdp', scatter_dimensio...]
    all_gather x5 -> x0, waiting for transfers between devices: 133 us -> none  [the longest x2 55 us: widen(): return lax.all_gather(tile_part, 'fsdp', axis=1, tiled=True)]
    dot_general x34 -> x0, matrix products: 119 us -> none  [the longest x6 24.5 us: gradient_tiles(): jnp.einsum('snic,snjd->ijcd', left_shaped, right_shaped, preferred_elemen...]
    pallas_call x0 -> x7, Pallas kernels: none -> 110 us  [call(): pl.pallas_call(kernel, out_shape=outs, in_specs=in_specs, out_specs=out_s...]
    ppermute x0 -> x59, starting transfers between devices: none -> 84.3 us  [the longest x20 45.6 us: along(): return lax.ppermute(x, 'dp', pairs)]
    psum x2 -> x0, blocking collectives: 52.8 us -> none  [the longest x1 40.1 us: local(): lax.psum((local_vectors, local_norms), ('dp', 'fsdp'))]
    reshape x14 -> x1, local copies, waits for them, and re-layouts: 35.5 us -> 0.13 us  [local(): decays.reshape(-1)]
  transfers between devices with their start and end apart: 7 -> 59, of which waited for: 6 -> 29; matrix products, arithmetic and copies ran while one was open for 10% -> 7% of each run, Pallas kernels for 0% -> 7%
where the time goes in v1:
time: 414 us; the launch traced here: 408 us
  waiting for transfers between devices  162 us (39%)
  Pallas kernels  110 us (27%)
  starting transfers between devices  84.3 us (20%)
  local copies, waits for them, and re-layouts  25.1 us (6%)
  other arithmetic  24.1 us (6%)
    pallas_call x7, Pallas kernels, call(): pl.pallas_call(kernel, out_shape=outs, in_specs=in_specs, out_specs=out_s...  110 us
    ppermute x39, waiting for transfers between devices, toward(): return lax.ppermute(x, 'fsdp', [(i, move(i)) for i in range(GROUPS)])  109 us
    ppermute x20, waiting for transfers between devices, along(): return lax.ppermute(x, 'dp', pairs)  52.7 us
    ppermute x20, starting transfers between devices, along(): return lax.ppermute(x, 'dp', pairs)  45.6 us
    ppermute x39, starting transfers between devices, toward(): return lax.ppermute(x, 'fsdp', [(i, move(i)) for i in range(GROUPS)])  38.6 us
    squeeze x6, local copies, waits for them, and re-layouts, plane_gather(): return [own, a, b, c] + [d[i] for i in range(4)]  13.6 us
    unnamed x165, local copies, waits for them, and re-layouts  11.1 us
    another operation x7, other arithmetic, plane_gather(): d = sibling(jnp.stack([own, a, b, c]))  8.85 us
  transfers between devices with their start and end apart: 59, of which 29 were waited for; matrix products, arithmetic and copies ran while one was open for 7% of the time, Pallas kernels for 7%

profile of v1, /device:TPU:0, one launch (start us, length us, event | category | flops | bytes accessed | tf_op | source)
XLA Modules:
  0.0 407.9 jit_solution(15971673156041267377)
XLA Ops:
  3.0 4.9 %collective-permute-start.4 = (bf16[110,16,128]{2,1,0:T(8,128)(2,1)S(1)}, bf16[110,16,128]{2,1,0:T(8,128)(2,1)S(1)}, u32[]{:S(2)}, u32[]{:S(2)}) collective-permute-start(bf16[110,16,128]{2,1,0:T(8,128)(2,1)S(1)} %get-tuple-element.124.rest_0_), channel_id=1, source_target_pairs={{0,8},{8,16},{16,24},{1,9},{9,17},{17,25},{2,10},{10,18},{18,26},{... | collective-permute-start | bytes 1351688 | tf_op jit(solution)/shard_map/ppermute | solution.py:391
  9.2 8.3 %collective-permute-done.4 = bf16[110,16,128]{2,1,0:T(8,128)(2,1)S(1)} collective-permute-done((bf16[110,16,128]{2,1,0:T(8,128)(2,1)S(1)}, bf16[110,16,128]{2,1,0:T(8,128)(2,1)S(1)}, u32[]{:S(2)}, u32[]{:S(2)}) %collective-permute-start.4) | collective-permute-done | bytes 450592 | tf_op jit(solution)/shard_map/ppermute | solution.py:391
  17.5 4.4 %collective-permute-start.5 = (bf16[110,16,128]{2,1,0:T(8,128)(2,1)S(1)}, bf16[110,16,128]{2,1,0:T(8,128)(2,1)S(1)}, u32[]{:S(2)}, u32[]{:S(2)}) collective-permute-start(bf16[110,16,128]{2,1,0:T(8,128)(2,1)S(1)} %collective-permute-done.4), channel_id=1, source_target_pairs={{0,8},{8,16},{16,24},{1,9},{9,17},{17,25},{2,10},{10,18},{18,26},{... | collective-permute-start | bytes 1351688 | tf_op jit(solution)/shard_map/ppermute | solution.py:391
  23.2 7.4 %collective-permute-done.5 = bf16[110,16,128]{2,1,0:T(8,128)(2,1)S(1)} collective-permute-done((bf16[110,16,128]{2,1,0:T(8,128)(2,1)S(1)}, bf16[110,16,128]{2,1,0:T(8,128)(2,1)S(1)}, u32[]{:S(2)}, u32[]{:S(2)}) %collective-permute-start.5) | collective-permute-done | bytes 450592 | tf_op jit(solution)/shard_map/ppermute | solution.py:391
  30.6 5.2 %collective-permute-start.11 = (bf16[110,16,128]{2,1,0:T(8,128)(2,1)S(1)}, bf16[110,16,128]{2,1,0:T(8,128)(2,1)}, u32[]{:S(2)}, u32[]{:S(2)}) collective-permute-start(bf16[110,16,128]{2,1,0:T(8,128)(2,1)S(1)} %collective-permute-done.5), channel_id=1, source_target_pairs={{0,8},{8,16},{16,24},{1,9},{9,17},{17,25},{2,10},{10,18},{18,26},{... | collective-permute-start | bytes 1351688 | tf_op jit(solution)/shard_map/ppermute | solution.py:391
  42.8 5.0 %collective-permute-done.17 = bf16[110,16,128]{2,1,0:T(8,128)(2,1)} collective-permute-done((bf16[110,16,128]{2,1,0:T(8,128)(2,1)S(1)}, bf16[110,16,128]{2,1,0:T(8,128)(2,1)}, u32[]{:S(2)}, u32[]{:S(2)}) %collective-permute-start.17) | collective-permute-done | bytes 450592 | tf_op jit(solution)/shard_map/ppermute | solution.py:391
  54.9 7.7 %collective-permute-done.13.rest_17_ = bf16[110,16,128]{2,1,0:T(8,128)(2,1)S(1)} collective-permute-done((bf16[110,16,128]{2,1,0:T(8,128)(2,1)S(1)}, bf16[110,16,128]{2,1,0:T(8,128)(2,1)S(1)}, u32[]{:S(2)}, u32[]{:S(2)}) %collective-permute-start.13) | collective-permute-done | bytes 450592 | tf_op jit(solution)/shard_map/ppermute | solution.py:375
  65.6 6.6 %collective-permute-done.7.rest_9_ = bf16[110,16,128]{2,1,0:T(8,128)(2,1)S(1)} collective-permute-done((bf16[110,16,128]{2,1,0:T(8,128)(2,1)S(1)}, bf16[110,16,128]{2,1,0:T(8,128)(2,1)S(1)}, u32[]{:S(2)}, u32[]{:S(2)}) %collective-permute-start.7) | collective-permute-done | bytes 450592 | tf_op jit(solution)/shard_map/ppermute | solution.py:375
  75.2 6.7 %collective-permute-done.18.rest_25_ = bf16[110,16,128]{2,1,0:T(8,128)(2,1)S(1)} collective-permute-done((bf16[110,16,128]{2,1,0:T(8,128)(2,1)S(1)}, bf16[110,16,128]{2,1,0:T(8,128)(2,1)S(1)}, u32[]{:S(2)}, u32[]{:S(2)}) %collective-permute-start.18) | collective-permute-done | bytes 450592 | tf_op jit(solution)/shard_map/ppermute | solution.py:375
  92.2 4.8 %collective-permute-done.20.rest_27_ = bf16[110,16,128]{2,1,0:T(8,128)(2,1)S(1)} collective-permute-done((bf16[110,16,128]{2,1,0:T(8,128)(2,1)S(1)}, bf16[110,16,128]{2,1,0:T(8,128)(2,1)S(1)}, u32[]{:S(2)}, u32[]{:S(2)}) %collective-permute-start.20) | collective-permute-done | bytes 450592 | tf_op jit(solution)/shard_map/ppermute | solution.py:375
  107.1 3.4 slice_bitcast_fusion.8
  110.8 19.0 %shard_map.214 = (bf16[512,768]{1,0:T(8,128)(2,1)S(1)}, bf16[512,768]{1,0:T(8,128)(2,1)S(1)}, bf16[512,768]{1,0:T(8,128)(2,1)S(1)}, bf16[256,768]{1,0:T(8,128)(2...) custom-call(s32[15]{0:T(128)S(1)} %concatenate.12.sc, ...), custom_call_target="tpu_custom_call" | custom-call | flops 5000000000 | bytes 10000000 | tf_op jit(solution)/shard_map/pallas_call | solution.py:355
  134.7 31.8 %shard_map.215 = (bf16[512,768]{1,0:T(8,128)(2,1)}, f32[512,768]{1,0:T(8,128)}, bf16[512,768]{1,0:T(8,128)(2,1)}, f32[512,3072]{1,0:T(8,128)}, bf16[512,768]{1,0...) custom-call(s32[15]{0:T(128)} %copy-done.42, ...), custom_call_target="tpu_custom_call" | custom-call | flops 8000000000 | bytes 30000000 | tf_op jit(solution)/shard_map/pallas_call | solution.py:355
  169.1 13.7 %shard_map.216 = (bf16[512,3072]{1,0:T(8,128)(2,1)}, f32[512,768]{1,0:T(8,128)S(1)}, bf16[512,768]{1,0:T(8,128)(2,1)S(1)}, bf16[512,768]{1,0:T(8,128)(2,1)S(1)}, f32[7,768]{1,0:T(8,128)S(1)}) custom-call(f32[512,768]{1,0:T(8,128)S(1)} %copy-done.47, bf16[512,768]{1,0:T(8,128)(2,1)S(1)} %copy-done.49, f32[512,3072]{1,0:T(8,128)} %get-tuple-element.62.slope, ...), custom_call_target="tpu_custom_call" | custom-call | flops 6000000000 | bytes 20000000 | tf_op jit(solution)/shard_map/pallas_call | solution.py:355
  184.7 3.4 shard_map.219
  188.7 5.5 %shard_map.217 = (bf16[512,768]{1,0:T(8,128)(2,1)S(1)}, bf16[256,768]{1,0:T(8,128)(2,1)S(1)}, bf16[256,768]{1,0:T(8,128)(2,1)S(1)}) custom-call(bf16[512,768]{1,0:T(8,128)(2,1)S(1)} %copy-done.59, bf16[256,768]{1,0:T(8,128)(2,1)S(1)} %copy-done.62, bf16[256,768]{1,0:T(8,128)(2,1)S(1)} %copy-done.64, f32[12,512]{1,0:T(8,128)S(1)} %get-tuple-element.59.lse, ...), custom_call_target="tpu_custom_call" | custom-call | flops 4000000000 | bytes 4000000 | tf_op jit(solution)/shard_map/pallas_call | solution.py:355
  194.3 7.4 %shard_map.218 = (bf16[512,768]{1,0:T(8,128)(2,1)}, bf16[4,152,16,128]{3,2,1,0:T(8,128)(2,1)S(1)}, bf16[4,152,16,128]{3,2,1,0:T(8,128)(2,1)}, f32[3,768]{1,0:T(4,128)S(1)}) custom-call(s32[15]{0:T(128)S(1)} %copy-done.43, bf16[512,768]{1,0:T(8,128)(2,1)S(1)} %bitcast.124, bf16[512,768]{1,0:T(8,128)(2,1)S(1)} %copy-done.54, bf16[512,768]{1,0:T(8,128)(2,1)S(1)} %copy-done.56, ...), custom_call_target="tpu_custom_call" | custom-call | flops 5000000000 | bytes 20000000 | tf_op jit(solution)/shard_map/pallas_call | solution.py:355
  207.7 12.0 %collective-permute-done.23 = bf16[2,144,16,128]{3,2,1,0:T(8,128)(2,1)S(1)} collective-permute-done((bf16[2,144,16,128]{3,2,1,0:T(8,128)(2,1)S(1)}, bf16[2,144,16,128]{3,2,1,0:T(8,128)(2,1)S(1)}, u32[]{:S(2)}, u32[]{:S(2)}) %collective-permute-start.23) | collective-permute-done | bytes 1179680 | tf_op jit(solution)/shard_map/ppermute | solution.py:375
  222.5 16.1 %collective-permute-done.28 = bf16[2,144,16,128]{3,2,1,0:T(8,128)(2,1)S(1)} collective-permute-done((bf16[2,144,16,128]{3,2,1,0:T(8,128)(2,1)S(1)}, bf16[2,144,16,128]{3,2,1,0:T(8,128)(2,1)S(1)}, u32[]{:S(2)}, u32[]{:S(2)}) %collective-permute-start.28) | collective-permute-done | bytes 1179680 | tf_op jit(solution)/shard_map/ppermute | solution.py:375
  241.1 21.6 %collective-permute-done.35 = bf16[2,152,16,128]{3,2,1,0:T(8,128)(2,1)S(1)} collective-permute-done((bf16[2,152,16,128]{3,2,1,0:T(8,128)(2,1)S(1)}, bf16[2,152,16,128]{3,2,1,0:T(8,128)(2,1)S(1)}, u32[]{:S(2)}, u32[]{:S(2)}) %collective-permute-start.35) | collective-permute-done | bytes 1245216 | tf_op jit(solution)/shard_map/ppermute | solution.py:375
  267.6 4.6 %collective-permute-start.25 = (bf16[110,16,128]{2,1,0:T(8,128)(2,1)S(1)}, bf16[110,16,128]{2,1,0:T(8,128)(2,1)S(1)}, u32[]{:S(2)}, u32[]{:S(2)}) collective-permute-start(bf16[110,16,128]{2,1,0:T(8,128)(2,1)S(1)} %slice.249), channel_id=1, source_target_pairs={{0,8},{16,24},{1,9},{17,25},{2,10},{18,26},{3,11},{19,27},{4,12},{... | collective-permute-start | bytes 1351688 | tf_op jit(solution)/shard_map/ppermute | solution.py:391
  273.5 4.6 %collective-permute-start.39 = (bf16[68,16,128]{2,1,0:T(8,128)(2,1)S(1)}, bf16[68,16,128]{2,1,0:T(8,128)(2,1)S(1)}, u32[]{:S(2)}, u32[]{:S(2)}) collective-permute-start(bf16[68,16,128]{2,1,0:T(8,128)(2,1)S(1)} %slice.263), channel_id=1, source_target_pairs={{0,8},{16,24},{1,9},{17,25},{2,10},{18,26},{3,11},{19,27},{4,12},{... | collective-permute-start | bytes 835592 | tf_op jit(solution)/shard_map/ppermute | solution.py:391
  278.2 4.1 %collective-permute-start.33 = (bf16[34,16,128]{2,1,0:T(8,128)(2,1)S(1)}, bf16[34,16,128]{2,1,0:T(8,128)(2,1)S(1)}, u32[]{:S(2)}, u32[]{:S(2)}) collective-permute-start(bf16[34,16,128]{2,1,0:T(8,128)(2,1)S(1)} %add_convert_fusion.17), channel_id=1, source_target_pairs={{0,16},{1,17},{2,18},{3,19},{4,20},{5,21},{6,22},{7,23}} | collective-permute-start | bytes 417800 | tf_op jit(solution)/shard_map/ppermute | solution.py:391
  282.7 4.2 %collective-permute-done.39 = bf16[68,16,128]{2,1,0:T(8,128)(2,1)S(1)} collective-permute-done((bf16[68,16,128]{2,1,0:T(8,128)(2,1)S(1)}, bf16[68,16,128]{2,1,0:T(8,128)(2,1)S(1)}, u32[]{:S(2)}, u32[]{:S(2)}) %collective-permute-start.39) | collective-permute-done | bytes 278560 | tf_op jit(solution)/shard_map/ppermute | solution.py:391
  286.9 4.4 %collective-permute-start.37 = (bf16[42,16,128]{2,1,0:T(8,128)(2,1)S(1)}, bf16[42,16,128]{2,1,0:T(8,128)(2,1)S(1)}, u32[]{:S(2)}, u32[]{:S(2)}) collective-permute-start(bf16[42,16,128]{2,1,0:T(8,128)(2,1)S(1)} %slice.262), channel_id=1, source_target_pairs={{0,8},{16,24},{1,9},{17,25},{2,10},{18,26},{3,11},{19,27},{4,12},{... | collective-permute-start | bytes 516104 | tf_op jit(solution)/shard_map/ppermute | solution.py:391
  298.4 7.5 %collective-permute-done.41 = bf16[110,16,128]{2,1,0:T(8,128)(2,1)S(1)} collective-permute-done((bf16[110,16,128]{2,1,0:T(8,128)(2,1)S(1)}, bf16[110,16,128]{2,1,0:T(8,128)(2,1)S(1)}, u32[]{:S(2)}, u32[]{:S(2)}) %collective-permute-start.41) | collective-permute-done | bytes 450592 | tf_op jit(solution)/shard_map/ppermute | solution.py:391
  307.7 9.6 %collective-permute-done.42 = bf16[110,16,128]{2,1,0:T(8,128)(2,1)S(1)} collective-permute-done((bf16[110,16,128]{2,1,0:T(8,128)(2,1)S(1)}, bf16[110,16,128]{2,1,0:T(8,128)(2,1)S(1)}, u32[]{:S(2)}, u32[]{:S(2)}) %collective-permute-start.42) | collective-permute-done | bytes 450592 | tf_op jit(solution)/shard_map/ppermute | solution.py:391
  321.8 9.2 %collective-permute-done.43.rest_1_ = bf16[110,16,128]{2,1,0:T(8,128)(2,1)S(1)} collective-permute-done((bf16[110,16,128]{2,1,0:T(8,128)(2,1)S(1)}, bf16[110,16,128]{2,1,0:T(8,128)(2,1)S(1)}, u32[]{:S(2)}, u32[]{:S(2)}) %collective-permute-start.43) | collective-permute-done | bytes 450592 | tf_op jit(solution)/shard_map/ppermute | solution.py:375
  336.4 4.8 %collective-permute-done.45.rest_3_ = bf16[110,16,128]{2,1,0:T(8,128)(2,1)S(1)} collective-permute-done((bf16[110,16,128]{2,1,0:T(8,128)(2,1)S(1)}, bf16[110,16,128]{2,1,0:T(8,128)(2,1)S(1)}, u32[]{:S(2)}, u32[]{:S(2)}) %collective-permute-start.45) | collective-permute-done | bytes 450592 | tf_op jit(solution)/shard_map/ppermute | solution.py:375
  347.6 2.7 collective-permute-done.55
  354.9 3.8 collective-permute-done.57
  366.3 29.3 %shard_map.220 = (f32[110,16,128]{2,1,0:T(8,128)}, f32[110,16,128]{2,1,0:T(8,128)}, f32[110,16,128]{2,1,0:T(8,128)S(1)}, f32[110,128]{1,0:T(8,128)S(1)}) custom-call(s32[15]{0:T(128)S(1)} %copy-done.43, f32[220]{0:T(256)S(1)} %reshape.112.dec, f32[110,16,128]{2,1,0:T(8,128)S(1)} %get-tuple-element.98.own, f32[110,16,128]{2,1,0:T(8,128)S(1)} %copy-done.10, ...), custom_call_target="tpu_custom_call" | custom-call | flops 1000000000 | bytes 10000000 | tf_op jit(solution)/shard_map/pallas_call | solution.py:355
  (324 shorter events, 121.4 us)
Async XLA Ops:
  3.0 14.5 %collective-permute-start.4 = (bf16[110,16,128]{2,1,0:T(8,128)(2,1)S(1)}, bf16[110,16,128]{2,1,0:T(8,128)(2,1)S(1)}, u32[]{:S(2)}, u32[]{:S(2)}) collective-permute-start(bf16[110,16,128]{2,1,0:T(8,128)(2,1)S(1)} %get-tuple-element.124.rest_0_), channel_id=1, source_target_pairs={{0,8},{8,16},{16,24},{1,9},{9,17},{17,25},{2,10},{10,18},{18,26},{... | collective-permute-start | bytes 1351688 | tf_op jit(solution)/shard_map/ppermute | solution.py:391
  7.9 14.0 %collective-permute-start.6 = (bf16[110,16,128]{2,1,0:T(8,128)(2,1)S(1)}, bf16[110,16,128]{2,1,0:T(8,128)(2,1)S(1)}, u32[]{:S(2)}, u32[]{:S(2)}) collective-permute-start(bf16[110,16,128]{2,1,0:T(8,128)(2,1)S(1)} %get-tuple-element.124.rest_0_), channel_id=1, source_target_pairs={{24,16},{16,8},{8,0},{25,17},{17,9},{9,1},{26,18},{18,10},{10,2},{... | collective-permute-start | bytes 1351688 | tf_op jit(solution)/shard_map/ppermute | solution.py:391
  21.9 13.8 %collective-permute-start.12 = (bf16[110,16,128]{2,1,0:T(8,128)(2,1)S(1)}, bf16[110,16,128]{2,1,0:T(8,128)(2,1)S(1)}, u32[]{:S(2)}, u32[]{:S(2)}) collective-permute-start(bf16[110,16,128]{2,1,0:T(8,128)(2,1)S(1)} %collective-permute-done.6), channel_id=1, source_target_pairs={{24,16},{16,8},{8,0},{25,17},{17,9},{9,1},{26,18},{18,10},{10,2},{... | collective-permute-start | bytes 1351688 | tf_op jit(solution)/shard_map/ppermute | solution.py:391
  37.0 13.8 %collective-permute-start = (bf16[110,16,128]{2,1,0:T(8,128)(2,1)S(1)}, bf16[110,16,128]{2,1,0:T(8,128)(2,1)S(1)}, u32[]{:S(2)}, u32[]{:S(2)}) collective-permute-start(bf16[110,16,128]{2,1,0:T(8,128)(2,1)S(1)} %get-tuple-element.124.rest_0_), channel_id=1, source_target_pairs={{0,2},{1,5},{2,0},{3,7},{4,6},{5,1},{6,4},{7,3},{8,10},{9,13},{10,... | collective-permute-start | bytes 1351688 | tf_op jit(solution)/shard_map/ppermute | solution.py:375
  38.6 14.8 %collective-permute-start.1 = (bf16[110,16,128]{2,1,0:T(8,128)(2,1)S(1)}, bf16[110,16,128]{2,1,0:T(8,128)(2,1)S(1)}, u32[]{:S(2)}, u32[]{:S(2)}) collective-permute-start(bf16[110,16,128]{2,1,0:T(8,128)(2,1)S(1)} %get-tuple-element.124.rest_0_), channel_id=1, source_target_pairs={{0,4},{1,3},{2,6},{3,1},{4,0},{5,7},{6,2},{7,5},{8,12},{9,11},{10,... | collective-permute-start | bytes 1351688 | tf_op jit(solution)/shard_map/ppermute | solution.py:375
  52.4 19.9 %collective-permute-start.7 = (bf16[110,16,128]{2,1,0:T(8,128)(2,1)S(1)}, bf16[110,16,128]{2,1,0:T(8,128)(2,1)S(1)}, u32[]{:S(2)}, u32[]{:S(2)}) collective-permute-start(bf16[110,16,128]{2,1,0:T(8,128)(2,1)S(1)} %get-tuple-element.127.rest_8_), channel_id=1, source_target_pairs={{0,2},{1,5},{2,0},{3,7},{4,6},{5,1},{6,4},{7,3},{8,10},{9,13},{10,... | collective-permute-start | bytes 1351688 | tf_op jit(solution)/shard_map/ppermute | solution.py:375
  52.9 22.3 %collective-permute-start.14 = (bf16[110,16,128]{2,1,0:T(8,128)(2,1)S(1)}, bf16[110,16,128]{2,1,0:T(8,128)(2,1)S(1)}, u32[]{:S(2)}, u32[]{:S(2)}) collective-permute-start(bf16[110,16,128]{2,1,0:T(8,128)(2,1)S(1)} %get-tuple-element.126.rest_16_), channel_id=1, source_target_pairs={{0,4},{1,3},{2,6},{3,1},{4,0},{5,7},{6,2},{7,5},{8,12},{9,11},{10,... | collective-permute-start | bytes 1351688 | tf_op jit(solution)/shard_map/ppermute | solution.py:375
  53.4 28.5 %collective-permute-start.18 = (bf16[110,16,128]{2,1,0:T(8,128)(2,1)S(1)}, bf16[110,16,128]{2,1,0:T(8,128)(2,1)S(1)}, u32[]{:S(2)}, u32[]{:S(2)}) collective-permute-start(bf16[110,16,128]{2,1,0:T(8,128)(2,1)S(1)} %get-tuple-element.125.rest_24_), channel_id=1, source_target_pairs={{0,2},{1,5},{2,0},{3,7},{4,6},{5,1},{6,4},{7,3},{8,10},{9,13},{10,... | collective-permute-start | bytes 1351688 | tf_op jit(solution)/shard_map/ppermute | solution.py:375
  62.6 20.8 %collective-permute-start.15 = (bf16[110,16,128]{2,1,0:T(8,128)(2,1)S(1)}, bf16[110,16,128]{2,1,0:T(8,128)(2,1)S(1)}, u32[]{:S(2)}, u32[]{:S(2)}) collective-permute-start(bf16[110,16,128]{2,1,0:T(8,128)(2,1)S(1)} %collective-permute-done.13.rest_17_), channel_id=1, source_target_pairs={{0,4},{1,3},{2,6},{3,1},{4,0},{5,7},{6,2},{7,5},{8,12},{9,11},{10,... | collective-permute-start | bytes 1351688 | tf_op jit(solution)/shard_map/ppermute | solution.py:375
  64.1 21.3 %collective-permute-start.8 = (bf16[110,16,128]{2,1,0:T(8,128)(2,1)S(1)}, bf16[110,16,128]{2,1,0:T(8,128)(2,1)S(1)}, u32[]{:S(2)}, u32[]{:S(2)}) collective-permute-start(bf16[110,16,128]{2,1,0:T(8,128)(2,1)S(1)} %get-tuple-element.127.rest_8_), channel_id=1, source_target_pairs={{0,4},{1,3},{2,6},{3,1},{4,0},{5,7},{6,2},{7,5},{8,12},{9,11},{10,... | collective-permute-start | bytes 1351688 | tf_op jit(solution)/shard_map/ppermute | solution.py:375
  72.3 15.1 %collective-permute-start.9 = (bf16[110,16,128]{2,1,0:T(8,128)(2,1)S(1)}, bf16[110,16,128]{2,1,0:T(8,128)(2,1)S(1)}, u32[]{:S(2)}, u32[]{:S(2)}) collective-permute-start(bf16[110,16,128]{2,1,0:T(8,128)(2,1)S(1)} %collective-permute-done.7.rest_9_), channel_id=1, source_target_pairs={{0,4},{1,3},{2,6},{3,1},{4,0},{5,7},{6,2},{7,5},{8,12},{9,11},{10,... | collective-permute-start | bytes 1351688 | tf_op jit(solution)/shard_map/ppermute | solution.py:375
  75.2 25.2 %collective-permute-start.3 = (bf16[4,110,16,128]{3,2,1,0:T(8,128)(2,1)}, bf16[4,110,16,128]{3,2,1,0:T(8,128)(2,1)}, u32[]{:S(2)}, u32[]{:S(2)}) collective-permute-start(bf16[4,110,16,128]{3,2,1,0:T(8,128)(2,1)} %pad_maximum_fusion), channel_id=1, source_target_pairs={{0,1},{1,0},{2,3},{3,2},{4,5},{5,4},{6,7},{7,6},{8,9},{9,8},{10,11... | collective-permute-start | bytes 5406728 | tf_op jit(solution)/shard_map/ppermute | solution.py:375
  83.5 13.6 %collective-permute-start.20 = (bf16[110,16,128]{2,1,0:T(8,128)(2,1)S(1)}, bf16[110,16,128]{2,1,0:T(8,128)(2,1)S(1)}, u32[]{:S(2)}, u32[]{:S(2)}) collective-permute-start(bf16[110,16,128]{2,1,0:T(8,128)(2,1)S(1)} %collective-permute-done.18.rest_25_), channel_id=1, source_target_pairs={{0,4},{1,3},{2,6},{3,1},{4,0},{5,7},{6,2},{7,5},{8,12},{9,11},{10,... | collective-permute-start | bytes 1351688 | tf_op jit(solution)/shard_map/ppermute | solution.py:375
  85.4 16.8 %collective-permute-start.16 = (bf16[4,110,16,128]{3,2,1,0:T(8,128)(2,1)}, bf16[4,110,16,128]{3,2,1,0:T(8,128)(2,1)}, u32[]{:S(2)}, u32[]{:S(2)}) collective-permute-start(bf16[4,110,16,128]{3,2,1,0:T(8,128)(2,1)} %pad_maximum_fusion.2), channel_id=1, source_target_pairs={{0,1},{1,0},{2,3},{3,2},{4,5},{5,4},{6,7},{7,6},{8,9},{9,8},{10,11... | collective-permute-start | bytes 5406728 | tf_op jit(solution)/shard_map/ppermute | solution.py:375
  88.9 15.8 %collective-permute-start.10 = (bf16[4,110,16,128]{3,2,1,0:T(8,128)(2,1)}, bf16[4,110,16,128]{3,2,1,0:T(8,128)(2,1)}, u32[]{:S(2)}, u32[]{:S(2)}) collective-permute-start(bf16[4,110,16,128]{3,2,1,0:T(8,128)(2,1)} %pad_maximum_fusion.1), channel_id=1, source_target_pairs={{0,1},{1,0},{2,3},{3,2},{4,5},{5,4},{6,7},{7,6},{8,9},{9,8},{10,11... | collective-permute-start | bytes 5406728 | tf_op jit(solution)/shard_map/ppermute | solution.py:375
  166.5 35.3 %collective-permute-start.22 = (bf16[4,144,16,128]{3,2,1,0:T(8,128)(2,1)}, bf16[4,144,16,128]{3,2,1,0:T(8,128)(2,1)}, u32[]{:S(2)}, u32[]{:S(2)}) collective-permute-start(bf16[4,144,16,128]{3,2,1,0:T(8,128)(2,1)} %get-tuple-element.80), channel_id=1, source_target_pairs={{0,1},{1,0},{2,3},{3,2},{4,5},{5,4},{6,7},{7,6},{8,9},{9,8},{10,11... | collective-permute-start | bytes 7077896 | tf_op jit(solution)/shard_map/ppermute | solution.py:375
  188.1 16.3 %collective-permute-start.27 = (bf16[4,144,16,128]{3,2,1,0:T(8,128)(2,1)S(1)}, bf16[4,144,16,128]{3,2,1,0:T(8,128)(2,1)S(1)}, u32[]{:S(2)}, u32[]{:S(2)}) collective-permute-start(bf16[4,144,16,128]{3,2,1,0:T(8,128)(2,1)S(1)} %get-tuple-element.84), channel_id=1, source_target_pairs={{0,1},{1,0},{2,3},{3,2},{4,5},{5,4},{6,7},{7,6},{8,9},{9,8},{10,11... | collective-permute-start | bytes 7077896 | tf_op jit(solution)/shard_map/ppermute | solution.py:375
  203.4 16.3 %collective-permute-start.23 = (bf16[2,144,16,128]{3,2,1,0:T(8,128)(2,1)S(1)}, bf16[2,144,16,128]{3,2,1,0:T(8,128)(2,1)S(1)}, u32[]{:S(2)}, u32[]{:S(2)}) collective-permute-start(bf16[2,144,16,128]{3,2,1,0:T(8,128)(2,1)S(1)} %add_convert_fusion.2), channel_id=1, source_target_pairs={{0,4},{1,3},{2,6},{3,1},{4,0},{5,7},{6,2},{7,5},{8,12},{9,11},{10,... | collective-permute-start | bytes 3538952 | tf_op jit(solution)/shard_map/ppermute | solution.py:375
  204.7 33.9 %collective-permute-start.28 = (bf16[2,144,16,128]{3,2,1,0:T(8,128)(2,1)S(1)}, bf16[2,144,16,128]{3,2,1,0:T(8,128)(2,1)S(1)}, u32[]{:S(2)}, u32[]{:S(2)}) collective-permute-start(bf16[2,144,16,128]{3,2,1,0:T(8,128)(2,1)S(1)} %add_convert_fusion.1), channel_id=1, source_target_pairs={{0,4},{1,3},{2,6},{3,1},{4,0},{5,7},{6,2},{7,5},{8,12},{9,11},{10,... | collective-permute-start | bytes 3538952 | tf_op jit(solution)/shard_map/ppermute | solution.py:375
  207.0 55.7 %collective-permute-start.35 = (bf16[2,152,16,128]{3,2,1,0:T(8,128)(2,1)S(1)}, bf16[2,152,16,128]{3,2,1,0:T(8,128)(2,1)S(1)}, u32[]{:S(2)}, u32[]{:S(2)}) collective-permute-start(bf16[2,152,16,128]{3,2,1,0:T(8,128)(2,1)S(1)} %add_convert_fusion), channel_id=1, source_target_pairs={{0,4},{1,3},{2,6},{3,1},{4,0},{5,7},{6,2},{7,5},{8,12},{9,11},{10,... | collective-permute-start | bytes 3735560 | tf_op jit(solution)/shard_map/ppermute | solution.py:375
  220.9 43.6 %collective-permute-start.24 = (bf16[144,16,128]{2,1,0:T(8,128)(2,1)S(1)}, bf16[144,16,128]{2,1,0:T(8,128)(2,1)S(1)}, u32[]{:S(2)}, u32[]{:S(2)}) collective-permute-start(bf16[144,16,128]{2,1,0:T(8,128)(2,1)S(1)} %fusion.6), channel_id=1, source_target_pairs={{0,2},{1,5},{2,0},{3,7},{4,6},{5,1},{6,4},{7,3},{8,10},{9,13},{10,... | collective-permute-start | bytes 1769480 | tf_op jit(solution)/shard_map/ppermute | solution.py:375
  238.8 28.4 %collective-permute-start.29 = (bf16[144,16,128]{2,1,0:T(8,128)(2,1)S(1)}, bf16[144,16,128]{2,1,0:T(8,128)(2,1)S(1)}, u32[]{:S(2)}, u32[]{:S(2)}) collective-permute-start(bf16[144,16,128]{2,1,0:T(8,128)(2,1)S(1)} %fusion.7), channel_id=1, source_target_pairs={{0,2},{1,5},{2,0},{3,7},{4,6},{5,1},{6,4},{7,3},{8,10},{9,13},{10,... | collective-permute-start | bytes 1769480 | tf_op jit(solution)/shard_map/ppermute | solution.py:375
  240.5 79.2 %collective-permute-start.47 = (bf16[110,16,128]{2,1,0:T(8,128)(2,1)S(1)}, bf16[110,16,128]{2,1,0:T(8,128)(2,1)S(1)}, u32[]{:S(2)}, u32[]{:S(2)}) collective-permute-start(bf16[110,16,128]{2,1,0:T(8,128)(2,1)S(1)} %convert_element_type.391.rest_8_), channel_id=1, source_target_pairs={{0,2},{1,5},{2,0},{3,7},{4,6},{5,1},{6,4},{7,3},{8,10},{9,13},{10,... | collective-permute-start | bytes 1351688 | tf_op jit(solution)/shard_map/ppermute | solution.py:375
  263.0 15.2 %collective-permute-start.36 = (bf16[152,16,128]{2,1,0:T(8,128)(2,1)S(1)}, bf16[152,16,128]{2,1,0:T(8,128)(2,1)S(1)}, u32[]{:S(2)}, u32[]{:S(2)}) collective-permute-start(bf16[152,16,128]{2,1,0:T(8,128)(2,1)S(1)} %fusion.5), channel_id=1, source_target_pairs={{0,2},{1,5},{2,0},{3,7},{4,6},{5,1},{6,4},{7,3},{8,10},{9,13},{10,... | collective-permute-start | bytes 1867784 | tf_op jit(solution)/shard_map/ppermute | solution.py:375
  267.6 29.2 %collective-permute-start.25 = (bf16[110,16,128]{2,1,0:T(8,128)(2,1)S(1)}, bf16[110,16,128]{2,1,0:T(8,128)(2,1)S(1)}, u32[]{:S(2)}, u32[]{:S(2)}) collective-permute-start(bf16[110,16,128]{2,1,0:T(8,128)(2,1)S(1)} %slice.249), channel_id=1, source_target_pairs={{0,8},{16,24},{1,9},{17,25},{2,10},{18,26},{3,11},{19,27},{4,12},{... | collective-permute-start | bytes 1351688 | tf_op jit(solution)/shard_map/ppermute | solution.py:391
  272.2 20.5 %collective-permute-start.30 = (bf16[76,16,128]{2,1,0:T(8,128)(2,1)S(1)}, bf16[76,16,128]{2,1,0:T(8,128)(2,1)S(1)}, u32[]{:S(2)}, u32[]{:S(2)}) collective-permute-start(bf16[76,16,128]{2,1,0:T(8,128)(2,1)S(1)} %slice.255), channel_id=1, source_target_pairs={{8,0},{24,16},{9,1},{25,17},{10,2},{26,18},{11,3},{27,19},{12,4},{... | collective-permute-start | bytes 933896 | tf_op jit(solution)/shard_map/ppermute | solution.py:391
  273.5 13.4 %collective-permute-start.39 = (bf16[68,16,128]{2,1,0:T(8,128)(2,1)S(1)}, bf16[68,16,128]{2,1,0:T(8,128)(2,1)S(1)}, u32[]{:S(2)}, u32[]{:S(2)}) collective-permute-start(bf16[68,16,128]{2,1,0:T(8,128)(2,1)S(1)} %slice.263), channel_id=1, source_target_pairs={{0,8},{16,24},{1,9},{17,25},{2,10},{18,26},{3,11},{19,27},{4,12},{... | collective-permute-start | bytes 835592 | tf_op jit(solution)/shard_map/ppermute | solution.py:391
  291.4 14.5 %collective-permute-start.41 = (bf16[110,16,128]{2,1,0:T(8,128)(2,1)S(1)}, bf16[110,16,128]{2,1,0:T(8,128)(2,1)S(1)}, u32[]{:S(2)}, u32[]{:S(2)}) collective-permute-start(bf16[110,16,128]{2,1,0:T(8,128)(2,1)S(1)} %slice.264), channel_id=1, source_target_pairs={{8,0},{24,16},{9,1},{25,17},{10,2},{26,18},{11,3},{27,19},{12,4},{... | collective-permute-start | bytes 1351688 | tf_op jit(solution)/shard_map/ppermute | solution.py:391
  318.4 13.9 %collective-permute-start.48 = (bf16[110,16,128]{2,1,0:T(8,128)(2,1)S(1)}, bf16[110,16,128]{2,1,0:T(8,128)(2,1)S(1)}, u32[]{:S(2)}, u32[]{:S(2)}) collective-permute-start(bf16[110,16,128]{2,1,0:T(8,128)(2,1)S(1)} %convert_element_type.391.rest_8_), channel_id=1, source_target_pairs={{0,4},{1,3},{2,6},{3,1},{4,0},{5,7},{6,2},{7,5},{8,12},{9,11},{10,... | collective-permute-start | bytes 1351688 | tf_op jit(solution)/shard_map/ppermute | solution.py:375
  320.5 16.0 %collective-permute-start.44 = (bf16[110,16,128]{2,1,0:T(8,128)(2,1)S(1)}, bf16[110,16,128]{2,1,0:T(8,128)(2,1)S(1)}, u32[]{:S(2)}, u32[]{:S(2)}) collective-permute-start(bf16[110,16,128]{2,1,0:T(8,128)(2,1)S(1)} %get-tuple-element.97.rest_0_), channel_id=1, source_target_pairs={{0,4},{1,3},{2,6},{3,1},{4,0},{5,7},{6,2},{7,5},{8,12},{9,11},{10,... | collective-permute-start | bytes 1351688 | tf_op jit(solution)/shard_map/ppermute | solution.py:375
  333.8 25.8 %collective-permute-start.50 = (bf16[4,110,16,128]{3,2,1,0:T(8,128)(2,1)}, bf16[4,110,16,128]{3,2,1,0:T(8,128)(2,1)}, u32[]{:S(2)}, u32[]{:S(2)}) collective-permute-start(bf16[4,110,16,128]{3,2,1,0:T(8,128)(2,1)} %pad_maximum_fusion.5), channel_id=1, source_target_pairs={{0,1},{1,0},{2,3},{3,2},{4,5},{5,4},{6,7},{7,6},{8,9},{9,8},{10,11... | collective-permute-start | bytes 5406728 | tf_op jit(solution)/shard_map/ppermute | solution.py:375
  342.7 21.2 %collective-permute-start.46 = (bf16[4,110,16,128]{3,2,1,0:T(8,128)(2,1)}, bf16[4,110,16,128]{3,2,1,0:T(8,128)(2,1)}, u32[]{:S(2)}, u32[]{:S(2)}) collective-permute-start(bf16[4,110,16,128]{3,2,1,0:T(8,128)(2,1)} %pad_maximum_fusion.4), channel_id=1, source_target_pairs={{0,1},{1,0},{2,3},{3,2},{4,5},{5,4},{6,7},{7,6},{8,9},{9,8},{10,11... | collective-permute-start | bytes 5406728 | tf_op jit(solution)/shard_map/ppermute | solution.py:375
  (109 other events, 1346.9 us)

commit v2 on v1

v2 whole, which is shorter than its diff:
```python
import functools

import jax
import jax.numpy as jnp
from jax import lax
from jax.experimental import pallas as pl
from jax.experimental.pallas import tpu as pltpu
from jax.sharding import PartitionSpec as P

D = 768
H = 12
HD = 64
FF = 3072
K = 256
NMAX = 512
TB = 128
LANES = 128
PART = 110
GROUPS = 8

EPS_NORM = 1e-05
EPS_STEP = 1e-06
STEP_RATE = 0.25
MOMENT_DECAY = 0.9
SQRT_HALF = 0.7071067811865476
INV_SQRT_TWO_PI = 0.3989422804014327
SCALE = HD ** (-0.5)

QUARTER = (D // TB) ** 2
ATT = 4 * QUARTER + NMAX // TB * (K // TB)
HID = D // TB * (FF // TB)
NBLK = ATT + 2 * HID
BF = jnp.bfloat16
F32 = jnp.float32

ANY = pl.BlockSpec(memory_space=pl.ANY)
VM = pl.BlockSpec(memory_space=pltpu.VMEM)
SM = pl.BlockSpec(memory_space=pltpu.SMEM)


def sds(shape, dtype):
    return jax.ShapeDtypeStruct(shape, dtype)


def nn(a, b):
    return lax.dot_general(a, b, (((1,), (0,)), ((), ())), preferred_element_type=F32)


def nt(a, b):
    return lax.dot_general(a, b, (((1,), (1,)), ((), ())), preferred_element_type=F32)


def tn(a, b):
    return lax.dot_general(a, b, (((0,), (0,)), ((), ())), preferred_element_type=F32)


def layer_norm(value):
    centre = jnp.mean(value, axis=-1, keepdims=True)
    shifted = value - centre
    spread = jnp.mean(shifted * shifted, axis=-1, keepdims=True)
    inverse = lax.rsqrt(spread + EPS_NORM)
    return shifted * inverse, inverse


def norm_backward(grad_out, normed, inverse, gain):
    scaled = grad_out * gain
    centred = scaled - jnp.mean(scaled, axis=-1, keepdims=True)
    return inverse * (centred - normed * jnp.mean(scaled * normed, axis=-1, keepdims=True))


def column_sum(value):
    return jnp.sum(value.astype(F32), axis=0, keepdims=True)


def valid_rows(length, width):
    return lax.broadcasted_iota(jnp.int32, (NMAX, width), 0) < length


HELD = GROUPS // 2
SET = 2


def piece_at(pieces, s):
    return pieces[s // HELD].at[s % HELD]


def fetch(sc, pieces, steps, parts, raw, sem):
    for step in range(steps):
        for at, part in enumerate(parts):

            @pl.when(sc[8 + part] == step)
            def _():
                for s in range(GROUPS):
                    source = piece_at(pieces[step * SET : (step + 1) * SET], s)
                    pltpu.make_async_copy(source, raw.at[at, s], sem.at[at, s]).start()


def fetched(pieces, raw, sem, at):
    for s in range(GROUPS):
        pltpu.make_async_copy(piece_at(pieces, s), raw.at[at, s], sem.at[at, s]).wait()


def lay_out(slots, raw, at, first, count, dst, dst_first, per_row):
    for n in range(count):
        i, j = divmod(n + dst_first, per_row)
        for r in range(GROUPS):
            dst[i * TB + 16 * r : i * TB + 16 * r + 16, j * TB : (j + 1) * TB] = raw[at, slots[r], first + n]


def splitter(sc):
    even = sc[13] == 0
    mine = [jnp.where(even, sc[2 * m], sc[2 * m + 1]) for m in range(4)]
    other = [jnp.where(even, sc[2 * m + 1], sc[2 * m]) - 4 for m in range(4)]

    def put(keep, send, b, value):
        low = value.astype(BF)
        for m in range(4):
            first = low[32 * m : 32 * m + 16]
            second = low[32 * m + 16 : 32 * m + 32]
            keep[mine[m], b] = jnp.where(even, first, second)
            send[other[m], b] = jnp.where(even, second, first)

    return put


STEP = 256


def tiles(raw, slots, block):
    part, b = divmod(block, PART)
    return [raw[part, slots[r], b] for r in range(GROUPS)]


def hidden_columns(raw, slots, g):
    count = STEP // TB
    rows = []
    for i in range(D // TB):
        blocks = [tiles(raw, slots, ATT + i * (FF // TB) + g * count + c) for c in range(count)]
        rows += [jnp.concatenate([block[r] for block in blocks], axis=1) for r in range(GROUPS)]
    return jnp.concatenate(rows, axis=0)


def return_rows(raw, slots, g):
    count = STEP // TB
    rows = []
    for i in range(count):
        blocks = [tiles(raw, slots, ATT + HID + (g * count + i) * (D // TB) + j) for j in range(D // TB)]
        rows += [jnp.concatenate([block[r] for block in blocks], axis=1) for r in range(GROUPS)]
    return jnp.concatenate(rows, axis=0)


KEPT = 10


def layer(sc, tok, cot, vec, *rest):
    pieces, rest = rest[: 4 * SET], rest[4 * SET :]
    stored, rest = rest[:KEPT], rest[KEPT:]
    (ks_o, vs_o, lse_o, norm_o, out_o, gr_o, gb_o, gm_o, keep_o, send_o, sums_o) = rest[:11]
    (raw, q_o, k_o, v_o, mixt_o, wq_o, wk_o, wv_o, wo_o, cm_o, mix_o, fl_o, gh_o, slope, act, gsl, acc, sem, osem) = rest[11:]
    fetch(sc, pieces, 4, range(4), raw, sem)
    slots = [sc[r] for r in range(GROUPS)]
    put = splitter(sc)
    nb = nd = D // TB
    copies = []

    def store(*refs):
        for ref in refs:
            copy = pltpu.make_async_copy(ref, stored[len(copies)], osem.at[len(copies)])
            copy.start()
            copies.append(copy)

    for at in (0, 1):
        fetched(pieces, raw, sem, at)
    for m, dst in enumerate((wq_o, wk_o, wv_o)):
        lay_out(slots, raw, 0, m * QUARTER, QUARTER, dst, 0, nb)
    head = PART - 3 * QUARTER
    lay_out(slots, raw, 0, 3 * QUARTER, head, wo_o, 0, nb)
    lay_out(slots, raw, 1, 0, QUARTER - head, wo_o, head, nb)
    lay_out(slots, raw, 1, QUARTER - head, ATT - 4 * QUARTER, cm_o, 0, K // TB)
    store(wq_o, wk_o, wv_o, cm_o)
    x = tok[...]
    q_o[...] = (nn(x, wq_o[...]) + vec[0:1]).astype(BF)
    k_o[...] = (nn(x, wk_o[...]) + vec[1:2]).astype(BF)
    v_o[...] = (nn(x, wv_o[...]) + vec[2:3]).astype(BF)
    store(q_o, k_o, v_o)
    masked = jnp.where(valid_rows(sc[12], K), cm_o[...], jnp.zeros((), BF))
    ks_o[...] = tn(masked, k_o[...]).astype(BF)
    vs_o[...] = tn(masked, v_o[...]).astype(BF)
    for n, ref in enumerate((ks_o, vs_o)):
        square = jnp.square(ref[...].astype(F32))
        total = jnp.sum(jnp.sum(square, axis=0, keepdims=True), axis=1, keepdims=True)
        norm_o[n : n + 1, :] = jnp.broadcast_to(jnp.sqrt(total), (1, LANES))
    lane = lax.broadcasted_iota(jnp.int32, (K, LANES), 1) < HD
    for p in range(H // 2):
        cols = slice(p * LANES, (p + 1) * LANES)
        q_p, ks_p, vs_p = q_o[:, cols], ks_o[:, cols], vs_o[:, cols]
        zero = jnp.zeros((), BF)
        parts, values = [], []
        for half in range(2):
            sel = lane if half == 0 else jnp.logical_not(lane)
            scores = nt(jnp.where(sel, ks_p, zero), q_p) * SCALE
            peak = jnp.max(scores, axis=0, keepdims=True)
            raised = jnp.exp(scores - peak)
            total = jnp.sum(raised, axis=0, keepdims=True)
            lse_o[2 * p + half : 2 * p + half + 1, :] = peak + jnp.log(total)
            parts.append((raised * (1.0 / total)).astype(BF))
            values.append(jnp.where(sel, vs_p, zero))
        mixt = tn(jnp.concatenate(values, axis=0), jnp.concatenate(parts, axis=0)).astype(BF)
        mixt_o[cols, :] = mixt
        mix_o[:, cols] = mixt.T
    store(mixt_o)
    branch = nn(mix_o[...], wo_o[...]) + vec[3:4]
    normed, inverse = layer_norm(x.astype(F32) + branch)
    first = normed * vec[4:5] + vec[5:6]
    fl_o[...] = first.astype(BF)
    store(fl_o)
    acc[...] = first + vec[10:11]
    for at in (2, 3):
        fetched(pieces, raw, sem, at)
    for g in range(FF // STEP):
        cols = slice(g * STEP, (g + 1) * STEP)
        row, off = 6 + (g * STEP) // D, (g * STEP) % D
        hidden = nn(fl_o[...], hidden_columns(raw, slots, g)) + vec[row : row + 1, off : off + STEP]
        phi = 0.5 * (1.0 + lax.erf(hidden * SQRT_HALF))
        low = (hidden * phi).astype(BF)
        act[:, cols] = low
        slope[:, cols] = phi + hidden * INV_SQRT_TWO_PI * jnp.exp(-0.5 * hidden * hidden)
        acc[...] += nn(low, return_rows(raw, slots, g))
    valid = valid_rows(sc[12], D)
    normed2, inverse2 = layer_norm(acc[...])
    result = normed2 * vec[11:12] + vec[12:13]
    out_o[...] = jnp.where(valid, result, 0.0).astype(BF)
    grad_result = jnp.where(valid, cot[...].astype(F32), 0.0)
    sums_o[8:9, :] = column_sum(grad_result * normed2)
    sums_o[9:10, :] = column_sum(grad_result)
    grad_second = norm_backward(grad_result, normed2, inverse2, vec[11:12])
    acc[...] = grad_second
    gsl[...] = grad_second.astype(BF)
    sums_o[7:8, :] = column_sum(gsl[...])
    for g in range(FF // STEP):
        cols = slice(g * STEP, (g + 1) * STEP)
        gh = (nt(gsl[...], return_rows(raw, slots, g)) * slope[:, cols]).astype(BF)
        gh_o[:, cols] = gh
        row, off = (g * STEP) // D, (g * STEP) % D
        sums_o[3 + row : 4 + row, off : off + STEP] = column_sum(gh)
        acc[...] += nt(gh, hidden_columns(raw, slots, g))
        terms = tn(act[:, cols], gsl[...])
        for i in range(STEP // TB):
            for j in range(nd):
                put(keep_o, send_o, (g * (STEP // TB) + i) * nd + j, terms[i * TB : (i + 1) * TB, j * TB : (j + 1) * TB])
    store(gh_o)
    grad_first = acc[...]
    normed, inverse = layer_norm(tok[...].astype(F32) + (nn(mix_o[...], wo_o[...]) + vec[3:4]))
    sums_o[1:2, :] = column_sum(grad_first * normed)
    sums_o[2:3, :] = column_sum(grad_first)
    grad_resid = norm_backward(grad_first, normed, inverse, vec[4:5])
    gr_o[...] = grad_resid
    low = grad_resid.astype(BF)
    gb_o[...] = low
    sums_o[0:1, :] = column_sum(low)
    gm_o[...] = nt(low, wo_o[...]).astype(BF)
    for copy in copies:
        copy.wait()


def attention_backward(sc, tok, q, ks, vs, lse, gm, k, v, gb, mixt, cm, *rest):
    gq_o, gk_o, gv_o, keep_o, send_o, sums_o, gks_o, gvs_o, *held, sem = rest[-15:]
    copies = [
        pltpu.make_async_copy(source, target, sem.at[n])
        for n, (source, target) in enumerate(zip((q, tok, mixt, cm, k, v), held))
    ]
    for copy in copies:
        copy.start()
    q, tok, mixt, cm, k, v = held
    copies[0].wait()
    lane = lax.broadcasted_iota(jnp.int32, (K, LANES), 1) < HD
    zero = jnp.zeros((), BF)
    for p in range(H // 2):
        cols = slice(p * LANES, (p + 1) * LANES)
        q_p, ks_p, vs_p, gm_p = q[:, cols], ks[:, cols], vs[:, cols], gm[:, cols]
        keys, grads, gvs, gks = [], [], [], []
        for half in range(2):
            sel = lane if half == 0 else jnp.logical_not(lane)
            key = jnp.where(sel, ks_p, zero)
            attend = jnp.exp(nt(key, q_p) * SCALE - lse[2 * p + half : 2 * p + half + 1, :])
            grad_attend = nt(jnp.where(sel, vs_p, zero), gm_p)
            mean = jnp.sum(grad_attend * attend, axis=0, keepdims=True)
            grad_scores = (attend * (grad_attend - mean)).astype(BF)
            gvs.append(nn(attend.astype(BF), gm_p))
            gks.append(nn(grad_scores, q_p))
            keys.append(key)
            grads.append(grad_scores)
        gvs_o[:, cols] = jnp.where(lane, gvs[0], gvs[1]).astype(BF)
        gks_o[:, cols] = (jnp.where(lane, gks[0], gks[1]) * SCALE).astype(BF)
        gqt = tn(jnp.concatenate(keys, axis=0), jnp.concatenate(grads, axis=0)) * SCALE
        gq_o[:, cols] = gqt.astype(BF).T
    put = splitter(sc)
    nd, nk = D // TB, K // TB
    for copy in copies[1:]:
        copy.wait()
    masked = jnp.where(valid_rows(sc[12], K), cm[...], zero)
    gk_o[...] = nn(masked, gks_o[...]).astype(BF)
    gv_o[...] = nn(masked, gvs_o[...]).astype(BF)
    tokt = tok[...].T
    lhs = (tokt, tokt, tokt, mixt[...])
    for m, grad in enumerate((gq_o, gk_o, gv_o, gb)):
        if m < 3:
            sums_o[m : m + 1, :] = column_sum(grad[...])
        terms = nn(lhs[m], grad[...])
        for i in range(nd):
            for j in range(nd):
                put(keep_o, send_o, m * QUARTER + i * nd + j, terms[i * TB : (i + 1) * TB, j * TB : (j + 1) * TB])
    comp = nt(k[...], gks_o[...]) + nt(v[...], gvs_o[...])
    comp = jnp.where(valid_rows(sc[12], K), comp, 0.0)
    for i in range(NMAX // TB):
        for j in range(nk):
            put(keep_o, send_o, 4 * QUARTER + i * nk + j, comp[i * TB : (i + 1) * TB, j * TB : (j + 1) * TB])


def closing(sc, fl, gh, gr, gq, gk, gv, wq, wk, wv, *rest):
    keep_o, send_o, in_o, *held, sem = rest[-9:]
    copies = [
        pltpu.make_async_copy(source, target, sem.at[n])
        for n, (source, target) in enumerate(zip((fl, gh, wq, wk, wv), held))
    ]
    for copy in copies:
        copy.start()
    fl, gh, wq, wk, wv = held
    put = splitter(sc)
    for copy in copies[:2]:
        copy.wait()
    nh, nd = FF // TB, D // TB
    flt = fl[...].T
    for g in range(FF // STEP):
        terms = nn(flt, gh[:, g * STEP : (g + 1) * STEP])
        for i in range(nd):
            for j in range(STEP // TB):
                put(keep_o, send_o, i * nh + g * (STEP // TB) + j, terms[i * TB : (i + 1) * TB, j * TB : (j + 1) * TB])
    for copy in copies[2:]:
        copy.wait()
    total = gr[...] + nt(gq[...], wq[...])
    total = total + nt(gk[...], wk[...])
    total = total + nt(gv[...], wv[...])
    in_o[...] = total.astype(BF)


def assemble(at, wide_a, wide_r, wide_x, slim_x, h_half, h_x, *rest):
    rows_o, low_o, scale = rest[-2], rest[-1], at[1].astype(F32)
    upper = at[0] >= 2
    end = at[0] % 3 == 0
    size, slim, late = wide_a.shape[0], slim_x.shape[0], h_half.shape[0]

    def emit(first, count, value):
        low = (value * (1.0 / scale))
        rows_o[first : first + count] = low
        low_o[first : first + count] = low.astype(BF)

    @pl.when(end)
    def _():
        emit(0, size, jnp.where(upper, wide_r[...], wide_a[...]).astype(F32) + wide_x[...].astype(F32))

    @pl.when(at[0] == 1)
    def _():
        emit(0, slim, wide_a[size - slim :].astype(F32) + slim_x[...].astype(F32))
        emit(slim, size - slim, h_half[: size - slim].astype(F32) + h_x[: size - slim].astype(F32))

    @pl.when(at[0] == 2)
    def _():
        emit(0, late, h_half[...].astype(F32) + h_x[...].astype(F32))
        emit(late, size - late, wide_r[: size - late].astype(F32) + slim_x[: size - late].astype(F32))


BATCH = 10


def halves(value):
    high = value.astype(BF)
    return high, (value - high.astype(F32)).astype(BF)


def step_kernel(sc, dec, own, lroot, lstat, rstat, g0, g1, r0, r1, nl_o, nr_o, pre_o, sq_o):
    slots = [sc[r] for r in range(GROUPS)]
    even = sc[13] == 0
    mine = [jnp.where(even, slots[2 * m], slots[2 * m + 1]) for m in range(4)]
    other = [jnp.where(even, slots[2 * m + 1], slots[2 * m]) - HELD for m in range(4)]
    pick_row = lax.broadcasted_iota(jnp.int32, (16, TB), 0) + sc[14] * 16
    select = (lax.broadcasted_iota(jnp.int32, (16, TB), 1) == pick_row).astype(BF)
    start = pl.program_id(0) * BATCH

    def whole(here, there, n):
        rows = []
        for m in range(4):
            a, b = here[mine[m], n], there[other[m], n]
            rows += [jnp.where(even, a, b), jnp.where(even, b, a)]
        return jnp.concatenate(rows, axis=0)

    bs = range(BATCH)
    grads = [whole(g0, g1, n) for n in bs]
    across = [nt(jnp.concatenate([own[n].astype(BF), select], axis=0), g) for n, g in zip(bs, grads)]
    heads = [halves(lroot[n]) for n in bs]
    down = [nn(jnp.concatenate([*h, a[16:].astype(BF)], axis=0), g) for h, a, g in zip(heads, across, grads)]
    mids = [halves(d[:16] + d[16:32]) for d in down]
    last = [nn(jnp.concatenate(m, axis=0), whole(r0, r1, n)) for n, m in zip(bs, mids)]
    for n, a, d, p in zip(bs, across, down, last):
        decay = dec[2 * (start + n)]
        nl_o[n] = decay * lstat[n] + (1.0 - decay) * a[:16]
        decay = dec[2 * (start + n) + 1]
        nr_o[n] = decay * rstat[n] + (1.0 - decay) * d[32:]
        pre = p[:16] + p[16:]
        pre_o[n] = pre
        sq_o[n] = jnp.sum(pre * pre, axis=0, keepdims=True)


def in_hbm(arrays):
    return [pltpu.with_memory_space_constraint(a, pltpu.HBM) for a in arrays]


def call(kernel, ins, outs, in_specs, out_specs=None, scratch=(), limit=60, deps=()):
    return pl.pallas_call(
        kernel,
        out_shape=outs,
        in_specs=in_specs + [ANY] * len(deps),
        out_specs=out_specs or [VM] * len(outs),
        scratch_shapes=list(scratch),
        compiler_params=pltpu.CompilerParams(vmem_limit_bytes=limit * 1024 * 1024),
        cost_estimate=pl.CostEstimate(flops=1, bytes_accessed=1, transcendentals=0),
    )(*ins, *deps)


SLOT_TABLE = (0, 4, 1, 6, 2, 5, 3, 7)


def slot_of(code, core):
    other, x, y = code & 1, (code >> 1) & 1, code >> 2
    return 4 * other + jnp.where((other ^ core) == 0, x + 2 * y, y + 2 * x)


def toward(x, move):
    return lax.ppermute(x, "fsdp", [(i, move(i)) for i in range(GROUPS)])


def near(x):
    return toward(x, lambda i: i ^ 2 if i % 2 == 0 else i ^ 4)


def far(x):
    return toward(x, lambda i: i ^ 4 if i % 2 == 0 else i ^ 2)


def sibling(x):
    return toward(x, lambda i: i ^ 1)


def along(x, pairs):
    return lax.ppermute(x, "dp", pairs)


def gate(index, options, copies, deps=()):
    flat, plan = [], []
    for entry in copies:
        group = entry if isinstance(entry, list) else [entry]
        plan.append((len(flat), len(group) if isinstance(entry, list) else 0))
        flat += group
    count = len(options)
    outs = [sds(options[0].shape, options[0].dtype)] if count else []
    for entry in copies:
        if isinstance(entry, list):
            outs.append(pltpu.HBM((len(entry),) + entry[0].shape, BF))
        else:
            outs.append(pltpu.HBM(entry.shape, BF) if entry.ndim == 4 else sds(entry.shape, BF))

    def kernel(at, *refs):
        sem = refs[-1]
        out = refs[-1 - len(outs) : -1]
        given = refs[count : count + len(flat)]
        started = []
        for n, (first, size) in enumerate(plan):
            target = out[n + (1 if count else 0)]
            for m in range(max(size, 1)):
                copy = pltpu.make_async_copy(
                    given[first + m], target.at[m] if size else target, sem.at[1 + first + m]
                )
                copy.start()
                started.append(copy)
        for n in range(count):

            @pl.when(at[0] == n)
            def _():
                pltpu.make_async_copy(refs[n], out[0], sem.at[0]).start()

        for copy in started:
            copy.wait()
        if count:
            pltpu.make_async_copy(refs[0], out[0], sem.at[0]).wait()

    return pl.pallas_call(
        kernel,
        out_shape=outs,
        in_specs=[SM] + [ANY] * (count + len(flat) + len(deps)),
        out_specs=[ANY] * len(outs),
        scratch_shapes=[pltpu.SemaphoreType.DMA((1 + len(flat),))],
        compiler_params=pltpu.CompilerParams(vmem_limit_bytes=2**20),
        cost_estimate=pl.CostEstimate(flops=1, bytes_accessed=1, transcendentals=0),
    )(index[None], *options, *flat, *deps)


def tie(x, deps):
    def kernel(*refs):
        pass

    return pl.pallas_call(
        kernel,
        out_shape=sds(x.shape, x.dtype),
        in_specs=[ANY] * (1 + len(deps)),
        out_specs=ANY,
        input_output_aliases={0: 0},
        compiler_params=pltpu.CompilerParams(vmem_limit_bytes=2**20),
        cost_estimate=pl.CostEstimate(flops=1, bytes_accessed=1, transcendentals=0),
    )(x, *deps)


def plane_gather(own):
    a = near(own)
    b = far(own)
    c = far(a)
    four = jnp.stack([own, a, b, c])
    return [four, sibling(four)]


def chosen(index, options):
    value = options[0]
    for i in range(1, len(options)):
        value = jnp.where(index == i, options[i], value)
    return value


EDGE = [(0, 1), (1, 0), (2, 3), (3, 2)]
INNER = [(0, 0), (1, 2), (2, 1), (3, 3)]


def gather_weights(narrow):
    z = lax.axis_index("dp")
    e, o = along(narrow, EDGE), along(narrow, INNER)
    a0, b0 = near(narrow), far(narrow)
    t1, a0 = gate(z, [e, e, o, e], [a0], (b0,))
    eo, oe = along(o, EDGE), along(e, INNER)
    a1, b1, c0 = near(t1), far(t1), far(a0)
    t2, a1, four0 = gate(z, [eo, o, oe, eo], [a1, [narrow, a0, b0, c0]], (b1,))
    eoe, d0 = along(oe, EDGE), sibling(four0)
    a2, b2, c1 = near(t2), far(t2), far(a1)
    t3, a2, four1, d0 = gate(z, [eoe, oe, e, eoe], [a2, [t1, a1, b1, c1], d0], (b2,))
    a3, b3, c2, d1 = near(t3), far(t3), far(a2), sibling(four1)
    a3, four2, d1 = gate(z, [], [a3, [t2, a2, b2, c2], d1], (b3,))
    c3, d2 = far(a3), sibling(four2)
    four3, d2 = gate(z, [], [[t3, a3, b3, c3], d2])
    d3 = sibling(four3)
    steps = chosen(z, [jnp.array(row, jnp.int32) for row in ((0, 1, 2, 3), (1, 0, 2, 3), (2, 1, 0, 3), (3, 2, 1, 0))])
    return [four0, d0, four1, d1, four2, d2, four3, d3], steps


def added(a, b, deps=()):
    def kernel(x, y, *rest):
        rest[-1][...] = (x[...].astype(F32) + y[...].astype(F32)).astype(BF)

    return call(kernel, [a, b], [sds(a.shape, BF)], [VM, VM], limit=8, deps=deps)[0]


def core_sum(keep, send, deps=()):
    got = sibling(send)

    def kernel(x, y, *rest):
        own, first, pair = rest[-3:]
        for n, (ref, at) in enumerate(((own, None), (first, None), (pair, 0), (pair, 1))):
            value = (x[n].astype(F32) + y[n].astype(F32)).astype(BF)
            if at is None:
                ref[...] = value
            else:
                ref[at] = value

    one = keep.shape[1:]
    return call(
        kernel, [keep, got], [sds(one, BF), sds(one, BF), sds((2,) + one, BF)], [VM, VM], limit=14,
        deps=deps,
    )


def last_sum(own, back, last, deps=()):
    def kernel(x, y, w, *rest):
        rest[-1][...] = (x[...].astype(F32) + y[0].astype(F32) + w[...].astype(F32)).astype(BF)

    return call(kernel, [own, back, last], [sds(own.shape, BF)], [VM] * 3, limit=8, deps=deps)[0]


def first_sum(first, back, deps=()):
    def kernel(x, y, *rest):
        rest[-1][...] = (x[...].astype(F32) + y[1].astype(F32)).astype(BF)

    return call(kernel, [first, back], [sds(first.shape, BF)], [VM] * 2, limit=8, deps=deps)[0]


CROSS = [(0, 2), (1, 3), (2, 0), (3, 1)]
SKIP = [(0, 1), (1, 3), (2, 0), (3, 2)]
TURN = [(0, 2), (1, 0), (2, 3), (3, 1)]


def pair_parts(odd, rows, cut):
    size = max(cut, rows.shape[0] - cut)
    even_at, odd_at = 0, rows.shape[0] - size
    stay = lax.dynamic_slice_in_dim(rows, jnp.where(odd, odd_at, even_at), size, 0)
    leave = lax.dynamic_slice_in_dim(rows, jnp.where(odd, even_at, odd_at), size, 0)
    return stay, leave


def plane_sum(x):
    for bit in (1, 2, 4):
        x = x + toward(x, lambda i, bit=bit: i ^ bit)
    return x


def local(
    tokens,
    cotangent,
    lengths,
    weights,
    vectors,
    moments,
    left_stats,
    right_stats,
    left_root,
    right_root,
    decays,
):
    dp, fsdp = lax.axis_size("dp"), lax.axis_size("fsdp")
    assert tokens.shape[0] == 1
    staged = (dp, fsdp) == (4, GROUPS)
    seq_total = tokens.shape[0] * dp * fsdp
    tok, cot = tokens[0], cotangent[0]
    narrow = weights.astype(BF)
    if staged:
        me = lax.axis_index("fsdp")
        core = lax.rem(me, 2)
        slots = slot_of(jnp.arange(GROUPS, dtype=jnp.int32) ^ me, core)
        pieces, steps = gather_weights(narrow)
    else:
        me = jnp.int32(0)
        core = jnp.int32(0)
        slots = slot_of(jnp.arange(GROUPS, dtype=jnp.int32), core)
        full = lax.all_gather(lax.all_gather(narrow, "dp", axis=0, tiled=True), "fsdp", axis=1, tiled=True)
        full = full.reshape(NBLK // PART, PART, GROUPS, TB // GROUPS, TB)
        place = [SLOT_TABLE.index(s) for s in range(GROUPS)]
        pieces = []
        for t in range(NBLK // PART):
            every = [full[t, :, place[s]] for s in range(GROUPS)]
            pieces += [jnp.stack(every[:HELD]), jnp.stack(every[HELD:])]
        steps = jnp.arange(4, dtype=jnp.int32)
    scalars = jnp.concatenate([slots, steps, lengths, core[None], me[None]]).astype(jnp.int32)

    row16 = TB // GROUPS
    act = sds((NMAX, D), BF)
    wide = sds((NMAX, D), F32)
    summary = sds((K, D), BF)
    shape = (NMAX, D)
    square = (D, D)
    r_terms = sds((4, HID, row16, TB), BF)
    a_terms = sds((4, ATT, row16, TB), BF)
    held = [square, square, square, (NMAX, K), shape, shape, shape, (D, NMAX), shape, (NMAX, FF)]
    (wq, wk, wv, cm, q, k, v, mixt, fl, gh,
     ks, vs, lse, norms, out, gr, gb, gm, r_keep, r_send, sums_b) = call(
        layer,
        [scalars, tok, cot, vectors] + in_hbm(pieces),
        [pltpu.HBM(one, BF) for one in held]
        + [summary, summary, sds((H, NMAX), F32), sds((2, LANES), F32), act, wide, act, act, r_terms, r_terms, sds((10, D), F32)],
        [SM, VM, VM, VM] + [ANY] * (4 * SET),
        [ANY] * KEPT + [VM] * 11,
        scratch=[
            pltpu.VMEM((4, GROUPS, PART, row16, TB), BF),
            *[pltpu.VMEM(one, BF) for one in (shape, shape, shape, (D, NMAX), square, square, square, square, (NMAX, K), shape, shape, (NMAX, FF))],
            pltpu.VMEM((NMAX, FF), F32),
            pltpu.VMEM((NMAX, FF), BF),
            pltpu.VMEM(shape, BF),
            pltpu.VMEM(shape, F32),
            pltpu.SemaphoreType.DMA((4, GROUPS)),
            pltpu.SemaphoreType.DMA((KEPT,)),
        ],
        limit=58,
    )
    deps = ()
    if staged:
        r_here, r_first, r_pair = core_sum(r_keep, r_send)
        r_back = far(r_pair)
        deps = (r_pair,)
    gq, gk, gv, a_keep, a_send, sums_a = call(
        attention_backward,
        [scalars, *in_hbm([tok, q]), ks, vs, lse, gm, *in_hbm([k, v]), gb, *in_hbm([mixt, cm])],
        [act, act, act, a_terms, a_terms, sds((3, D), F32)],
        [SM, ANY, ANY] + [VM] * 4 + [ANY, ANY, VM, ANY, ANY],
        scratch=[
            *[pltpu.VMEM(one, BF) for one in ((K, D), (K, D), shape, shape, (D, NMAX), (NMAX, K), shape, shape)],
            pltpu.SemaphoreType.DMA((6,)),
        ],
        limit=28, deps=deps,
    )
    if staged:
        r_first = first_sum(r_first, r_back)
        r_last = near(r_first)
        a_here, a_first, a_pair = core_sum(a_keep, tie(a_send, (r_first,)), (r_last,))
        r_rows = last_sum(r_here, r_back, r_last)
        r_stay, r_leave = pair_parts(lax.axis_index("dp") % 2 == 1, r_rows, 3 * PART - (ATT + HID))
        a_back = far(a_pair)
        r_came = along(r_leave, EDGE)
        deps = (a_pair, r_leave)
    h_keep, h_send, in_grads = call(
        closing,
        [scalars, *in_hbm([fl, gh]), gr, gq, gk, gv, *in_hbm([wq, wk, wv])],
        [r_terms, r_terms, act],
        [SM, ANY, ANY] + [VM] * 4 + [ANY] * 3,
        scratch=[
            *[pltpu.VMEM(one, BF) for one in (shape, (NMAX, FF), square, square, square)],
            pltpu.SemaphoreType.DMA((5,)),
        ],
        limit=28, deps=deps,
    )
    local_vectors = jnp.concatenate([sums_a, sums_b], axis=0)
    local_norms = norms[:, 0]
    if staged:
        z = lax.axis_index("dp")
        odd = z % 2 == 1
        cut_r = 3 * PART - (ATT + HID)
        cut_h = 2 * PART - ATT
        rest_a, rest_h = ATT - PART, HID - cut_h
        packed = jnp.concatenate([local_vectors, jnp.pad(local_norms[None], ((0, 0), (0, D - 2)))], axis=0)
        packed = packed + sibling(packed)
        a_first = first_sum(a_first, a_back, (r_came, packed))
        r_half = added(r_stay, r_came, (a_back,))
        a_last = near(a_first)
        packed = packed + toward(packed, lambda i: i ^ 2)
        h_here, h_first, h_pair = core_sum(h_keep, tie(h_send, (a_first,)), (a_last, packed))
        a_rows = last_sum(a_here, a_back, a_last)
        h_back = far(h_pair)
        a_stay, a_leave = pair_parts(odd, a_rows, PART)
        a_came = along(a_leave, EDGE)
        packed = packed + toward(packed, lambda i: i ^ 4)
        h_first = first_sum(h_first, h_back, (a_came, packed))
        a_half = added(a_stay, a_came, (h_back,))
        h_last = near(h_first)
        upper = z >= 2
        wide_cross = along(jnp.where(upper, a_half, r_half), SKIP)
        slim_cross = along(jnp.where(upper, a_half[PART - rest_a :], r_half[:rest_a]), TURN)
        packed = packed + along(packed, EDGE)
        h_rows = last_sum(h_here, h_back, h_last, (wide_cross, slim_cross, packed))
        h_stay = lax.dynamic_slice_in_dim(h_rows, jnp.where(odd, 0, cut_h), rest_h, 0)
        h_leave = lax.dynamic_slice_in_dim(h_rows, jnp.where(odd, cut_h, 0), rest_h, 0)
        h_came = along(h_leave, EDGE)
        root = right_root.astype(BF)
        root_near, root_far = near(root), far(root)
        packed = packed + along(packed, CROSS)
        h_half = added(h_stay, h_came, (root_near, root_far, packed))
        h_cross = along(h_half, TURN)
        root_diag = far(root_near)
        grad_rows, low_rows = call(
            assemble,
            [jnp.stack([z, jnp.int32(seq_total)]), a_half, r_half, wide_cross, slim_cross, h_half, h_cross],
            [sds(weights.shape, F32), sds(weights.shape, BF)],
            [SM] + [VM] * 6,
            limit=8, deps=(root_diag,),
        )
        vector_total, norm_totals = packed[:-1], packed[-1, :2]
        root_four = jnp.stack([root, root_near, root_far, root_diag])
        blocks = plane_gather(low_rows) + [root_four, sibling(root_four)]
        rows = sds(weights.shape, F32)
        one = pl.BlockSpec((BATCH, row16, TB), lambda n: (n, 0, 0))
        four = pl.BlockSpec((HELD, BATCH, row16, TB), lambda n: (0, n, 0, 0))
        new_left, new_right, precond, squares = pl.pallas_call(
            step_kernel,
            grid=(PART // BATCH,),
            out_shape=[rows, rows, rows, sds((PART, 1, LANES), F32)],
            in_specs=[SM, SM] + [one] * 4 + [four] * 4,
            out_specs=[one, one, one, pl.BlockSpec((BATCH, 1, LANES), lambda n: (n, 0, 0))],
            compiler_params=pltpu.CompilerParams(vmem_limit_bytes=16 * 1024 * 1024),
            cost_estimate=pl.CostEstimate(flops=1, bytes_accessed=1, transcendentals=0),
        )(scalars, decays.reshape(-1), grad_rows, left_root, left_stats, right_stats, *blocks)
        squares = squares[:, 0]
        both = jnp.stack([jnp.sum(squares, axis=1), jnp.sum(weights * weights, axis=(1, 2))])
        precond_squares, weight_squares = plane_sum(both)
    else:
        def join(keep, send):
            both = jnp.concatenate([keep, send], axis=0)
            return jnp.stack([both[s] for s in SLOT_TABLE], axis=1).reshape(-1, TB, TB)

        every = jnp.concatenate([join(a_keep, a_send), join(h_keep, h_send), join(r_keep, r_send)], axis=0)
        inner = lax.psum_scatter(every, "fsdp", scatter_dimension=1, tiled=True)
        total = lax.psum_scatter(inner, "dp", scatter_dimension=0, tiled=True).astype(F32)
        grad_rows = total / seq_total
        vector_total, norm_totals = lax.psum((local_vectors, local_norms), ("dp", "fsdp"))
        high = lax.Precision.HIGHEST
        whole = lax.all_gather(grad_rows.astype(BF), "fsdp", axis=1, tiled=True).astype(F32)
        count = grad_rows.shape[1]
        slab = lax.dynamic_slice_in_dim(whole, lax.axis_index("fsdp") * count, count, 2)
        gram_left = jnp.einsum("brc,bsc->brs", grad_rows, whole, precision=high)
        gram_right = jnp.einsum("bic,bis->bcs", slab, whole, precision=high)
        decay_left = decays[:, 0][:, None, None]
        decay_right = decays[:, 1][:, None, None]
        new_left = decay_left * left_stats + (1.0 - decay_left) * gram_left
        new_right = decay_right * right_stats + (1.0 - decay_right) * gram_right
        columns = jnp.einsum("bis,bcs->bic", whole, right_root, precision=high)
        applied = lax.all_gather(columns.astype(BF), "fsdp", axis=2, tiled=True).astype(F32)
        precond = jnp.einsum("brs,bsc->brc", left_root, applied, precision=high)
        precond_squares, weight_squares = lax.psum(
            (jnp.sum(precond * precond, axis=(1, 2)), jnp.sum(weights * weights, axis=(1, 2))), "fsdp"
        )
    vector_grad = vector_total / seq_total
    summary_norms = norm_totals / seq_total
    tile_area = TB * TB
    weight_scale = jnp.sqrt(weight_squares / tile_area)
    precond_scale = lax.rsqrt(precond_squares / tile_area + EPS_STEP)
    new_weights = weights - STEP_RATE * (weight_scale * precond_scale)[:, None, None] * precond
    new_moments = MOMENT_DECAY * moments + (1.0 - MOMENT_DECAY) * vector_grad
    row_scale = jnp.sqrt(jnp.mean(jnp.square(vectors), axis=1, keepdims=True))
    moment_scale = lax.rsqrt(jnp.mean(jnp.square(new_moments), axis=1, keepdims=True) + EPS_STEP)
    new_vectors = vectors - STEP_RATE * row_scale * new_moments * moment_scale
    return (
        out[None],
        in_grads[None],
        new_weights,
        grad_rows,
        new_left,
        new_right,
        new_vectors,
        new_moments,
        summary_norms,
    )


def solution(mesh):
    in_specs = (
        P(("dp", "fsdp"), None, None),
        P(("dp", "fsdp"), None, None),
        P(("dp", "fsdp")),
        P("dp", "fsdp", None),
        P(),
        P(),
        P("dp", "fsdp", None),
        P("dp", "fsdp", None),
        P("dp", "fsdp", None),
        P("dp", "fsdp", None),
        P("dp", None),
    )
    out_specs = (
        P(("dp", "fsdp"), None, None),
        P(("dp", "fsdp"), None, None),
        P("dp", "fsdp", None),
        P("dp", "fsdp", None),
        P("dp", "fsdp", None),
        P("dp", "fsdp", None),
        P(),
        P(),
        P(),
    )
    return jax.shard_map(local, mesh=mesh, in_specs=in_specs, out_specs=out_specs, check_vma=False)
```

time: 414 us -> 324 us (0.78)
  starting transfers between devices: 84.3 us -> 52.3 us
  Pallas kernels: 110 us -> 88.6 us
  waiting for transfers between devices: 162 us -> 143 us
  other arithmetic: 24.1 us -> 12.7 us
    ppermute x20 -> x13, starting transfers between devices: 45.6 us -> 18.5 us  [along(): return lax.ppermute(x, 'dp', pairs)]
    ppermute x20 -> x13, waiting for transfers between devices: 52.7 us -> 27.2 us  [along(): return lax.ppermute(x, 'dp', pairs)]
    pallas_call x7 -> x24, Pallas kernels: 110 us -> 88.6 us  [the longest x16 69.5 us: call(): pl.pallas_call(kernel, out_shape=outs, in_specs=in_specs + [ANY] * len(de...]
    squeeze x6 -> x0, local copies, waits for them, and re-layouts: 13.6 us -> none  [plane_gather(): return [own, a, b, c] + [d[i] for i in range(4)]]
    unnamed x165 -> x97, local copies, waits for them, and re-layouts: 11.1 us -> 18.8 us
    ppermute x39, waiting for transfers between devices: 109 us -> 116 us  [toward(): return lax.ppermute(x, 'fsdp', [(i, move(i)) for i in range(GROUPS)])]
    convert_element_type x17 -> x1, other arithmetic: 6.93 us -> 0.82 us  [local(): root = right_root.astype(BF)]
    another operation x7 -> x4, other arithmetic: 8.85 us -> 2.81 us  [the longest x1 1.43 us: plane_gather(): four = jnp.stack([own, a, b, c])]
  transfers between devices with their start and end apart: 59 -> 52, of which waited for: 29 -> 30; matrix products, arithmetic and copies ran while one was open for 7% -> 3% of each run, Pallas kernels for 7% -> 8%
where the time goes in v2:
time: 324 us; the launch traced here: 320 us
  waiting for transfers between devices  143 us (44%)
  Pallas kernels  88.6 us (27%)
  starting transfers between devices  52.3 us (16%)
  local copies, waits for them, and re-layouts  21.1 us (7%)
  other arithmetic  12.7 us (4%)
    ppermute x39, waiting for transfers between devices, toward(): return lax.ppermute(x, 'fsdp', [(i, move(i)) for i in range(GROUPS)])  116 us
    pallas_call x16, Pallas kernels, call(): pl.pallas_call(kernel, out_shape=outs, in_specs=in_specs + [ANY] * len(de...  69.5 us
    ppermute x39, starting transfers between devices, toward(): return lax.ppermute(x, 'fsdp', [(i, move(i)) for i in range(GROUPS)])  33.8 us
    ppermute x13, waiting for transfers between devices, along(): return lax.ppermute(x, 'dp', pairs)  27.2 us
    unnamed x97, local copies, waits for them, and re-layouts  18.8 us
    ppermute x13, starting transfers between devices, along(): return lax.ppermute(x, 'dp', pairs)  18.5 us
    pallas_call x1, Pallas kernels, local(): pl.pallas_call(step_kernel, grid=(PART // BATCH,), out_shape=[rows, rows,...  10.4 us
    pallas_call x5, Pallas kernels, gate(): pl.pallas_call(kernel, out_shape=outs, in_specs=[SM] + [ANY] * (count + l...  8.7 us
  transfers between devices with their start and end apart: 52, of which 30 were waited for; matrix products, arithmetic and copies ran while one was open for 3% of the time, Pallas kernels for 8%

profile of v2, /device:TPU:0, one launch (start us, length us, event | category | flops | bytes accessed | tf_op | source)
XLA Modules:
  0.0 320.3 jit_solution(2731660064952602270)
XLA Ops:
  0.6 2.4 multiply_reduce_fusion
  3.7 5.9 %collective-permute-start.2 = (bf16[110,16,128]{2,1,0:T(8,128)(2,1)S(1)}, bf16[110,16,128]{2,1,0:T(8,128)(2,1)S(1)}, u32[]{:S(2)}, u32[]{:S(2)}) collective-permute-start(bf16[110,16,128]{2,1,0:T(8,128)(2,1)S(1)} %get-tuple-element.130.refs_5_), channel_id=1, source_target_pairs={{0,8},{8,0},{16,24},{24,16},{1,9},{9,1},{17,25},{25,17},{2,10},{10... | collective-permute-start | bytes 1351688 | tf_op jit(solution)/shard_map/ppermute | solution.py:455
  12.6 7.0 %collective-permute-done.2.refs_0_.refs_1_.refs_3_.refs_2_ = bf16[110,16,128]{2,1,0:T(8,128)(2,1)S(1)} collective-permute-done((bf16[110,16,128]{2,1,0:T(8,128)(2,1)S(1)}, bf16[110,16,128]{2,1,0:T(8,128)(2,1)S(1)}, u32[]{:S(2)}, u32[]{:S(2)}) %collective-permute-start.2) | collective-permute-done | bytes 450592 | tf_op jit(solution)/shard_map/ppermute | solution.py:455
  19.7 2.7 collective-permute-done.5.refs_5_.refs_7_
  28.3 6.7 %collective-permute-done.8.refs_9_.refs_7_ = bf16[110,16,128]{2,1,0:T(8,128)(2,1)S(1)} collective-permute-done((bf16[110,16,128]{2,1,0:T(8,128)(2,1)S(1)}, bf16[110,16,128]{2,1,0:T(8,128)(2,1)S(1)}, u32[]{:S(2)}, u32[]{:S(2)}) %collective-permute-start.8) | collective-permute-done | bytes 450592 | tf_op jit(solution)/shard_map/ppermute | solution.py:439
  35.0 2.8 collective-permute-done.6.refs_4_
  45.6 8.3 %collective-permute-done.13.refs_10_.refs_3_ = bf16[110,16,128]{2,1,0:T(8,128)(2,1)S(1)} collective-permute-done((bf16[110,16,128]{2,1,0:T(8,128)(2,1)S(1)}, bf16[110,16,128]{2,1,0:T(8,128)(2,1)S(1)}, u32[]{:S(2)}, u32[]{:S(2)}) %collective-permute-start.13) | collective-permute-done | bytes 450592 | tf_op jit(solution)/shard_map/ppermute | solution.py:439
  53.9 2.4 collective-permute-done.10.refs_4_
  56.3 3.2 %collective-permute-done.11.refs_8_ = bf16[110,16,128]{2,1,0:T(8,128)(2,1)S(1)} collective-permute-done((bf16[110,16,128]{2,1,0:T(8,128)(2,1)S(1)}, bf16[110,16,128]{2,1,0:T(8,128)(2,1)S(1)}, u32[]{:S(2)}, u32[]{:S(2)}) %collective-permute-start.11) | collective-permute-done | bytes 450592 | tf_op jit(solution)/shard_map/ppermute | solution.py:439
  65.1 9.3 %collective-permute-done.14.refs_0_ = bf16[110,16,128]{2,1,0:T(8,128)(2,1)S(1)} collective-permute-done((bf16[110,16,128]{2,1,0:T(8,128)(2,1)S(1)}, bf16[110,16,128]{2,1,0:T(8,128)(2,1)S(1)}, u32[]{:S(2)}, u32[]{:S(2)}) %collective-permute-start.14) | collective-permute-done | bytes 450592 | tf_op jit(solution)/shard_map/ppermute | solution.py:439
  74.6 4.8 %collective-permute-done.17.refs_6_.refs_2_ = bf16[110,16,128]{2,1,0:T(8,128)(2,1)S(1)} collective-permute-done((bf16[110,16,128]{2,1,0:T(8,128)(2,1)S(1)}, bf16[110,16,128]{2,1,0:T(8,128)(2,1)S(1)}, u32[]{:S(2)}, u32[]{:S(2)}) %collective-permute-start.17) | collective-permute-done | bytes 450592 | tf_op jit(solution)/shard_map/ppermute | solution.py:439
  79.4 2.6 shard_map.217
  83.7 7.1 %collective-permute-done.18.refs_3_ = bf16[110,16,128]{2,1,0:T(8,128)(2,1)S(1)} collective-permute-done((bf16[110,16,128]{2,1,0:T(8,128)(2,1)S(1)}, bf16[110,16,128]{2,1,0:T(8,128)(2,1)S(1)}, u32[]{:S(2)}, u32[]{:S(2)}) %collective-permute-start.18) | collective-permute-done | bytes 450592 | tf_op jit(solution)/shard_map/ppermute | solution.py:439
  94.2 2.5 collective-permute-done.20.rest_7_
  97.9 38.6 %shard_map.219 = (bf16[768,768]{1,0:T(8,128)(2,1)}, bf16[768,768]{1,0:T(8,128)(2,1)}, bf16[768,768]{1,0:T(8,128)(2,1)}, bf16[512,256]{1,0:T(8,128)(2,1)}, bf16[5...) custom-call(s32[15]{0:T(128)} %concatenate.6.sc, ...), custom_call_target="tpu_custom_call" | custom-call | flops 1 | bytes 1 | tf_op jit(solution)/shard_map/pallas_call | solution.py:419
  136.8 4.6 %collective-permute-done.21.y = bf16[4,144,16,128]{3,2,1,0:T(8,128)(2,1)S(1)} collective-permute-done((bf16[4,144,16,128]{3,2,1,0:T(8,128)(2,1)}, bf16[4,144,16,128]{3,2,1,0:T(8,128)(2,1)S(1)}, u32[]{:S(2)}, u32[]{:S(2)}) %collective-permute-start.21) | collective-permute-done | bytes 2359328 | tf_op jit(solution)/shard_map/ppermute | solution.py:439
  145.8 11.1 %shard_map.221 = (bf16[512,768]{1,0:T(8,128)(2,1)S(1)}, bf16[512,768]{1,0:T(8,128)(2,1)S(1)}, bf16[512,768]{1,0:T(8,128)(2,1)S(1)}, bf16[4,152,16,128]{3,2,1,0:T...) custom-call(s32[15]{0:T(128)S(1)} %copy-done.35, bf16[512,768]{1,0:T(8,128)(2,1)} %bitcast.27, ...), custom_call_target="tpu_custom_call" | custom-call | flops 1 | bytes 1 | tf_op jit(solution)/shard_map/pallas_call | solution.py:419
  157.0 3.7 %collective-permute-done.22.y = bf16[2,144,16,128]{3,2,1,0:T(8,128)(2,1)S(1)} collective-permute-done((bf16[2,144,16,128]{3,2,1,0:T(8,128)(2,1)S(1)}, bf16[2,144,16,128]{3,2,1,0:T(8,128)(2,1)S(1)}, u32[]{:S(2)}, u32[]{:S(2)}) %collective-permute-start.22) | collective-permute-done | bytes 1179680 | tf_op jit(solution)/shard_map/ppermute | solution.py:439
  162.2 8.7 %collective-permute-done.24.rest_0_.w = bf16[144,16,128]{2,1,0:T(8,128)(2,1)S(1)} collective-permute-done((bf16[144,16,128]{2,1,0:T(8,128)(2,1)S(1)}, bf16[144,16,128]{2,1,0:T(8,128)(2,1)S(1)}, u32[]{:S(2)}, u32[]{:S(2)}) %collective-permute-start.24) | collective-permute-done | bytes 589856 | tf_op jit(solution)/shard_map/ppermute | solution.py:439
  179.1 9.8 %shard_map.226 = (bf16[4,144,16,128]{3,2,1,0:T(8,128)(2,1)S(1)}, bf16[4,144,16,128]{3,2,1,0:T(8,128)(2,1)S(1)}, bf16[512,768]{1,0:T(8,128)(2,1)}) custom-call(s32[15]{0:T(128)S(1)} %copy-done.35, bf16[512,768]{1,0:T(8,128)(2,1)} %get-tuple-element.83.fl, bf16[512,3072]{1,0:T(8,128)(2,1)} %get-tuple-element.84.gh, f32[512,768]{1,0:T(8,128)S(1)} %copy-done.7, ...), custom_call_target="tpu_custom_call" | custom-call | flops 1 | bytes 1 | tf_op jit(solution)/shard_map/pallas_call | solution.py:419
  189.0 2.3 collective-permute-done.25.y.rest_0_
  193.6 9.3 %collective-permute-done.31 = f32[14,768]{1,0:T(8,128)S(1)} collective-permute-done((f32[14,768]{1,0:T(8,128)S(1)}, f32[14,768]{1,0:T(8,128)S(1)}, u32[]{:S(2)}, u32[]{:S(2)}) %collective-permute-start.31) | collective-permute-done | bytes 43040 | tf_op jit(solution)/shard_map/ppermute | solution.py:439
  211.1 12.5 %collective-permute-done.35 = f32[14,768]{1,0:T(8,128)S(1)} collective-permute-done((f32[14,768]{1,0:T(8,128)S(1)}, f32[14,768]{1,0:T(8,128)S(1)}, u32[]{:S(2)}, u32[]{:S(2)}) %collective-permute-start.35) | collective-permute-done | bytes 43040 | tf_op jit(solution)/shard_map/ppermute | solution.py:439
  230.6 2.4 collective-permute-start.34
  235.8 7.6 %collective-permute-done.37 = f32[14,768]{1,0:T(8,128)S(1)} collective-permute-done((f32[14,768]{1,0:T(8,128)S(1)}, f32[14,768]{1,0:T(8,128)S(1)}, u32[]{:S(2)}, u32[]{:S(2)}) %collective-permute-start.37) | collective-permute-done | bytes 43040 | tf_op jit(solution)/shard_map/ppermute | solution.py:455
  252.8 3.7 %collective-permute-done.41 = f32[14,768]{1,0:T(8,128)S(1)} collective-permute-done((f32[14,768]{1,0:T(8,128)S(1)}, f32[14,768]{1,0:T(8,128)S(1)}, u32[]{:S(2)}, u32[]{:S(2)}) %collective-permute-start.41) | collective-permute-done | bytes 43040 | tf_op jit(solution)/shard_map/ppermute | solution.py:455
  260.1 6.6 %collective-permute-done.42.h_x = bf16[76,16,128]{2,1,0:T(8,128)(2,1)S(1)} collective-permute-done((bf16[76,16,128]{2,1,0:T(8,128)(2,1)S(1)}, bf16[76,16,128]{2,1,0:T(8,128)(2,1)S(1)}, u32[]{:S(2)}, u32[]{:S(2)}) %collective-permute-start.42) | collective-permute-done | bytes 311328 | tf_op jit(solution)/shard_map/ppermute | solution.py:455
  269.5 9.7 %collective-permute-done.44 = bf16[110,16,128]{2,1,0:T(8,128)(2,1)S(1)} collective-permute-done((bf16[110,16,128]{2,1,0:T(8,128)(2,1)S(1)}, bf16[110,16,128]{2,1,0:T(8,128)(2,1)S(1)}, u32[]{:S(2)}, u32[]{:S(2)}) %collective-permute-start.44) | collective-permute-done | bytes 450592 | tf_op jit(solution)/shard_map/ppermute | solution.py:439
  282.6 5.0 %collective-permute-done.46 = bf16[110,16,128]{2,1,0:T(8,128)(2,1)S(1)} collective-permute-done((bf16[110,16,128]{2,1,0:T(8,128)(2,1)S(1)}, bf16[110,16,128]{2,1,0:T(8,128)(2,1)S(1)}, u32[]{:S(2)}, u32[]{:S(2)}) %collective-permute-start.46) | collective-permute-done | bytes 450592 | tf_op jit(solution)/shard_map/ppermute | solution.py:439
  289.6 3.5 %collective-permute-done.47.g1 = bf16[4,110,16,128]{3,2,1,0:T(8,128)(2,1)} collective-permute-done((bf16[4,110,16,128]{3,2,1,0:T(8,128)(2,1)}, bf16[4,110,16,128]{3,2,1,0:T(8,128)(2,1)}, u32[]{:S(2)}, u32[]{:S(2)}) %collective-permute-start.47) | collective-permute-done | bytes 1802272 | tf_op jit(solution)/shard_map/ppermute | solution.py:439
  296.7 10.4 %shard_map.237 = (f32[110,16,128]{2,1,0:T(8,128)}, f32[110,16,128]{2,1,0:T(8,128)}, f32[110,16,128]{2,1,0:T(8,128)S(1)}, f32[110,1,128]{2,1,0:T(1,128)S(1)}) custom-call(s32[15]{0:T(128)S(1)} %copy-done.35, f32[220]{0:T(256)S(1)} %reshape.64.dec, f32[110,16,128]{2,1,0:T(8,128)S(1)} %copy-done.11, f32[110,16,128]{2,1,0:T(8,128)S(1)} %copy-done.8, ...), custom_call_target="tpu_custom_call" | custom-call | flops 1 | bytes 1 | tf_op jit(solution)/shard_map/pallas_call | solution.py:773
  317.4 2.5 multiply_subtract_fusion
  (228 shorter events, 98.1 us)
Async XLA Ops:
  3.7 15.9 %collective-permute-start.2 = (bf16[110,16,128]{2,1,0:T(8,128)(2,1)S(1)}, bf16[110,16,128]{2,1,0:T(8,128)(2,1)S(1)}, u32[]{:S(2)}, u32[]{:S(2)}) collective-permute-start(bf16[110,16,128]{2,1,0:T(8,128)(2,1)S(1)} %get-tuple-element.130.refs_5_), channel_id=1, source_target_pairs={{0,8},{8,0},{16,24},{24,16},{1,9},{9,1},{17,25},{25,17},{2,10},{10... | collective-permute-start | bytes 1351688 | tf_op jit(solution)/shard_map/ppermute | solution.py:455
  9.6 12.7 %collective-permute-start.5 = (bf16[110,16,128]{2,1,0:T(8,128)(2,1)S(1)}, bf16[110,16,128]{2,1,0:T(8,128)(2,1)S(1)}, u32[]{:S(2)}, u32[]{:S(2)}) collective-permute-start(bf16[110,16,128]{2,1,0:T(8,128)(2,1)S(1)} %get-tuple-element.130.refs_5_), channel_id=1, source_target_pairs={{0,4},{1,3},{2,6},{3,1},{4,0},{5,7},{6,2},{7,5},{8,12},{9,11},{10,... | collective-permute-start | bytes 1351688 | tf_op jit(solution)/shard_map/ppermute | solution.py:439
  11.1 11.2 %collective-permute-start.4 = (bf16[110,16,128]{2,1,0:T(8,128)(2,1)S(1)}, bf16[110,16,128]{2,1,0:T(8,128)(2,1)S(1)}, u32[]{:S(2)}, u32[]{:S(2)}) collective-permute-start(bf16[110,16,128]{2,1,0:T(8,128)(2,1)S(1)} %get-tuple-element.130.refs_5_), channel_id=1, source_target_pairs={{0,2},{1,5},{2,0},{3,7},{4,6},{5,1},{6,4},{7,3},{8,10},{9,13},{10,... | collective-permute-start | bytes 1351688 | tf_op jit(solution)/shard_map/ppermute | solution.py:439
  22.9 12.1 %collective-permute-start.8 = (bf16[110,16,128]{2,1,0:T(8,128)(2,1)S(1)}, bf16[110,16,128]{2,1,0:T(8,128)(2,1)S(1)}, u32[]{:S(2)}, u32[]{:S(2)}) collective-permute-start(bf16[110,16,128]{2,1,0:T(8,128)(2,1)S(1)} %get-tuple-element.68.refs_5_), channel_id=1, source_target_pairs={{0,4},{1,3},{2,6},{3,1},{4,0},{5,7},{6,2},{7,5},{8,12},{9,11},{10,... | collective-permute-start | bytes 1351688 | tf_op jit(solution)/shard_map/ppermute | solution.py:439
  24.5 13.3 %collective-permute-start.6 = (bf16[110,16,128]{2,1,0:T(8,128)(2,1)S(1)}, bf16[110,16,128]{2,1,0:T(8,128)(2,1)S(1)}, u32[]{:S(2)}, u32[]{:S(2)}) collective-permute-start(bf16[110,16,128]{2,1,0:T(8,128)(2,1)S(1)} %get-tuple-element.68.refs_5_), channel_id=1, source_target_pairs={{0,2},{1,5},{2,0},{3,7},{4,6},{5,1},{6,4},{7,3},{8,10},{9,13},{10,... | collective-permute-start | bytes 1351688 | tf_op jit(solution)/shard_map/ppermute | solution.py:439
  25.0 14.8 %collective-permute-start.7 = (bf16[110,16,128]{2,1,0:T(8,128)(2,1)S(1)}, bf16[110,16,128]{2,1,0:T(8,128)(2,1)S(1)}, u32[]{:S(2)}, u32[]{:S(2)}) collective-permute-start(bf16[110,16,128]{2,1,0:T(8,128)(2,1)S(1)} %get-tuple-element.69.refs_6_), channel_id=1, source_target_pairs={{0,4},{1,3},{2,6},{3,1},{4,0},{5,7},{6,2},{7,5},{8,12},{9,11},{10,... | collective-permute-start | bytes 1351688 | tf_op jit(solution)/shard_map/ppermute | solution.py:439
  25.5 14.3 %collective-permute-start.3 = (bf16[110,16,128]{2,1,0:T(8,128)(2,1)S(1)}, bf16[110,16,128]{2,1,0:T(8,128)(2,1)S(1)}, u32[]{:S(2)}, u32[]{:S(2)}) collective-permute-start(bf16[110,16,128]{2,1,0:T(8,128)(2,1)S(1)} %collective-permute-done.2.refs_0_.refs_1_.refs_3_.refs_2_), channel_id=1, source_target_pairs={{0,0},{8,16},{16,8},{24,24},{1,1},{9,17},{17,9},{25,25},{2,2},{10,... | collective-permute-start | bytes 1351688 | tf_op jit(solution)/shard_map/ppermute | solution.py:455
  26.2 13.6 %collective-permute-start.1 = (bf16[110,16,128]{2,1,0:T(8,128)(2,1)S(1)}, bf16[110,16,128]{2,1,0:T(8,128)(2,1)S(1)}, u32[]{:S(2)}, u32[]{:S(2)}) collective-permute-start(bf16[110,16,128]{2,1,0:T(8,128)(2,1)S(1)} %collective-permute-done.refs_2_.refs_1_), channel_id=1, source_target_pairs={{0,8},{8,0},{16,24},{24,16},{1,9},{9,1},{17,25},{25,17},{2,10},{10... | collective-permute-start | bytes 1351688 | tf_op jit(solution)/shard_map/ppermute | solution.py:455
  41.4 18.2 %collective-permute-start.12 = (bf16[4,110,16,128]{3,2,1,0:T(8,128)(2,1)}, bf16[4,110,16,128]{3,2,1,0:T(8,128)(2,1)S(1)}, u32[]{:S(2)}, u32[]{:S(2)}) collective-permute-start(bf16[4,110,16,128]{3,2,1,0:T(8,128)(2,1)} %get-tuple-element.70.rest_0_), channel_id=1, source_target_pairs={{0,1},{1,0},{2,3},{3,2},{4,5},{5,4},{6,7},{7,6},{8,9},{9,8},{10,11... | collective-permute-start | bytes 5406728 | tf_op jit(solution)/shard_map/ppermute | solution.py:439
  41.5 12.4 %collective-permute-start.13 = (bf16[110,16,128]{2,1,0:T(8,128)(2,1)S(1)}, bf16[110,16,128]{2,1,0:T(8,128)(2,1)S(1)}, u32[]{:S(2)}, u32[]{:S(2)}) collective-permute-start(bf16[110,16,128]{2,1,0:T(8,128)(2,1)S(1)} %get-tuple-element.71.refs_1_), channel_id=1, source_target_pairs={{0,4},{1,3},{2,6},{3,1},{4,0},{5,7},{6,2},{7,5},{8,12},{9,11},{10,... | collective-permute-start | bytes 1351688 | tf_op jit(solution)/shard_map/ppermute | solution.py:439
  43.0 13.3 %collective-permute-start.10 = (bf16[110,16,128]{2,1,0:T(8,128)(2,1)S(1)}, bf16[110,16,128]{2,1,0:T(8,128)(2,1)S(1)}, u32[]{:S(2)}, u32[]{:S(2)}) collective-permute-start(bf16[110,16,128]{2,1,0:T(8,128)(2,1)S(1)} %get-tuple-element.71.refs_1_), channel_id=1, source_target_pairs={{0,2},{1,5},{2,0},{3,7},{4,6},{5,1},{6,4},{7,3},{8,10},{9,13},{10,... | collective-permute-start | bytes 1351688 | tf_op jit(solution)/shard_map/ppermute | solution.py:439
  44.7 14.9 %collective-permute-start.11 = (bf16[110,16,128]{2,1,0:T(8,128)(2,1)S(1)}, bf16[110,16,128]{2,1,0:T(8,128)(2,1)S(1)}, u32[]{:S(2)}, u32[]{:S(2)}) collective-permute-start(bf16[110,16,128]{2,1,0:T(8,128)(2,1)S(1)} %get-tuple-element.72.refs_6_), channel_id=1, source_target_pairs={{0,4},{1,3},{2,6},{3,1},{4,0},{5,7},{6,2},{7,5},{8,12},{9,11},{10,... | collective-permute-start | bytes 1351688 | tf_op jit(solution)/shard_map/ppermute | solution.py:439
  45.2 14.4 %collective-permute-start.9 = (bf16[110,16,128]{2,1,0:T(8,128)(2,1)S(1)}, bf16[110,16,128]{2,1,0:T(8,128)(2,1)S(1)}, u32[]{:S(2)}, u32[]{:S(2)}) collective-permute-start(bf16[110,16,128]{2,1,0:T(8,128)(2,1)S(1)} %collective-permute-done.3.refs_2_.refs_1_), channel_id=1, source_target_pairs={{0,8},{8,0},{16,24},{24,16},{1,9},{9,1},{17,25},{25,17},{2,10},{10... | collective-permute-start | bytes 1351688 | tf_op jit(solution)/shard_map/ppermute | solution.py:455
  61.8 17.7 %collective-permute-start.16 = (bf16[4,110,16,128]{3,2,1,0:T(8,128)(2,1)}, bf16[4,110,16,128]{3,2,1,0:T(8,128)(2,1)S(1)}, u32[]{:S(2)}, u32[]{:S(2)}) collective-permute-start(bf16[4,110,16,128]{3,2,1,0:T(8,128)(2,1)} %get-tuple-element.74.rest_2_), channel_id=1, source_target_pairs={{0,1},{1,0},{2,3},{3,2},{4,5},{5,4},{6,7},{7,6},{8,9},{9,8},{10,11... | collective-permute-start | bytes 5406728 | tf_op jit(solution)/shard_map/ppermute | solution.py:439
  61.8 12.6 %collective-permute-start.14 = (bf16[110,16,128]{2,1,0:T(8,128)(2,1)S(1)}, bf16[110,16,128]{2,1,0:T(8,128)(2,1)S(1)}, u32[]{:S(2)}, u32[]{:S(2)}) collective-permute-start(bf16[110,16,128]{2,1,0:T(8,128)(2,1)S(1)} %get-tuple-element.75.refs_0_), channel_id=1, source_target_pairs={{0,2},{1,5},{2,0},{3,7},{4,6},{5,1},{6,4},{7,3},{8,10},{9,13},{10,... | collective-permute-start | bytes 1351688 | tf_op jit(solution)/shard_map/ppermute | solution.py:439
  63.1 11.5 %collective-permute-start.15 = (bf16[110,16,128]{2,1,0:T(8,128)(2,1)S(1)}, bf16[110,16,128]{2,1,0:T(8,128)(2,1)S(1)}, u32[]{:S(2)}, u32[]{:S(2)}) collective-permute-start(bf16[110,16,128]{2,1,0:T(8,128)(2,1)S(1)} %get-tuple-element.76.refs_2_), channel_id=1, source_target_pairs={{0,4},{1,3},{2,6},{3,1},{4,0},{5,7},{6,2},{7,5},{8,12},{9,11},{10,... | collective-permute-start | bytes 1351688 | tf_op jit(solution)/shard_map/ppermute | solution.py:439
  64.6 14.8 %collective-permute-start.17 = (bf16[110,16,128]{2,1,0:T(8,128)(2,1)S(1)}, bf16[110,16,128]{2,1,0:T(8,128)(2,1)S(1)}, u32[]{:S(2)}, u32[]{:S(2)}) collective-permute-start(bf16[110,16,128]{2,1,0:T(8,128)(2,1)S(1)} %get-tuple-element.75.refs_0_), channel_id=1, source_target_pairs={{0,4},{1,3},{2,6},{3,1},{4,0},{5,7},{6,2},{7,5},{8,12},{9,11},{10,... | collective-permute-start | bytes 1351688 | tf_op jit(solution)/shard_map/ppermute | solution.py:439
  144.5 16.2 %collective-permute-start.22 = (bf16[2,144,16,128]{3,2,1,0:T(8,128)(2,1)S(1)}, bf16[2,144,16,128]{3,2,1,0:T(8,128)(2,1)S(1)}, u32[]{:S(2)}, u32[]{:S(2)}) collective-permute-start(bf16[2,144,16,128]{3,2,1,0:T(8,128)(2,1)S(1)} %get-tuple-element.98.rest_0_), channel_id=1, source_target_pairs={{0,4},{1,3},{2,6},{3,1},{4,0},{5,7},{6,2},{7,5},{8,12},{9,11},{10,... | collective-permute-start | bytes 3538952 | tf_op jit(solution)/shard_map/ppermute | solution.py:439
  174.2 17.1 %collective-permute-start.25 = (bf16[2,152,16,128]{3,2,1,0:T(8,128)(2,1)}, bf16[2,152,16,128]{3,2,1,0:T(8,128)(2,1)S(1)}, u32[]{:S(2)}, u32[]{:S(2)}) collective-permute-start(bf16[2,152,16,128]{3,2,1,0:T(8,128)(2,1)} %get-tuple-element.108.rest_0_), channel_id=1, source_target_pairs={{0,4},{1,3},{2,6},{3,1},{4,0},{5,7},{6,2},{7,5},{8,12},{9,11},{10,... | collective-permute-start | bytes 3735560 | tf_op jit(solution)/shard_map/ppermute | solution.py:439
  177.0 12.0 %collective-permute-start.26 = (bf16[110,16,128]{2,1,0:T(8,128)(2,1)S(1)}, bf16[110,16,128]{2,1,0:T(8,128)(2,1)S(1)}, u32[]{:S(2)}, u32[]{:S(2)}) collective-permute-start(bf16[110,16,128]{2,1,0:T(8,128)(2,1)S(1)} %get-tuple-element.136.rest_1_), channel_id=1, source_target_pairs={{0,8},{8,0},{16,24},{24,16},{1,9},{9,1},{17,25},{25,17},{2,10},{10... | collective-permute-start | bytes 1351688 | tf_op jit(solution)/shard_map/ppermute | solution.py:455
  191.4 11.4 %collective-permute-start.30 = (bf16[4,144,16,128]{3,2,1,0:T(8,128)(2,1)S(1)}, bf16[4,144,16,128]{3,2,1,0:T(8,128)(2,1)S(1)}, u32[]{:S(2)}, u32[]{:S(2)}) collective-permute-start(bf16[4,144,16,128]{3,2,1,0:T(8,128)(2,1)S(1)} %shard_map.229), channel_id=1, source_target_pairs={{0,1},{1,0},{2,3},{3,2},{4,5},{5,4},{6,7},{7,6},{8,9},{9,8},{10,11... | collective-permute-start | bytes 7077896 | tf_op jit(solution)/shard_map/ppermute | solution.py:439
  191.5 11.4 %collective-permute-start.28 = (bf16[152,16,128]{2,1,0:T(8,128)(2,1)S(1)}, bf16[152,16,128]{2,1,0:T(8,128)(2,1)S(1)}, u32[]{:S(2)}, u32[]{:S(2)}) collective-permute-start(bf16[152,16,128]{2,1,0:T(8,128)(2,1)S(1)} %shard_map.227.refs_1_), channel_id=1, source_target_pairs={{0,2},{1,5},{2,0},{3,7},{4,6},{5,1},{6,4},{7,3},{8,10},{9,13},{10,... | collective-permute-start | bytes 1867784 | tf_op jit(solution)/shard_map/ppermute | solution.py:439
  206.1 18.7 %collective-permute-start.32 = (bf16[2,144,16,128]{3,2,1,0:T(8,128)(2,1)}, bf16[2,144,16,128]{3,2,1,0:T(8,128)(2,1)S(1)}, u32[]{:S(2)}, u32[]{:S(2)}) collective-permute-start(bf16[2,144,16,128]{3,2,1,0:T(8,128)(2,1)} %get-tuple-element.118), channel_id=1, source_target_pairs={{0,4},{1,3},{2,6},{3,1},{4,0},{5,7},{6,2},{7,5},{8,12},{9,11},{10,... | collective-permute-start | bytes 3538952 | tf_op jit(solution)/shard_map/ppermute | solution.py:439
  209.7 15.0 %collective-permute-start.29 = (bf16[110,16,128]{2,1,0:T(8,128)(2,1)}, bf16[110,16,128]{2,1,0:T(8,128)(2,1)}, u32[]{:S(2)}, u32[]{:S(2)}) collective-permute-start(bf16[110,16,128]{2,1,0:T(8,128)(2,1)} %get-tuple-element.131), channel_id=1, source_target_pairs={{0,8},{8,0},{16,24},{24,16},{1,9},{9,1},{17,25},{25,17},{2,10},{10... | collective-permute-start | bytes 1351688 | tf_op jit(solution)/shard_map/ppermute | solution.py:455
  210.3 13.3 %collective-permute-start.35 = (f32[14,768]{1,0:T(8,128)S(1)}, f32[14,768]{1,0:T(8,128)S(1)}, u32[]{:S(2)}, u32[]{:S(2)}) collective-permute-start(f32[14,768]{1,0:T(8,128)S(1)} %add.73.rest_1_), channel_id=1, source_target_pairs={{0,4},{1,5},{2,6},{3,7},{4,0},{5,1},{6,2},{7,3},{8,12},{9,13},{10,... | collective-permute-start | bytes 129032 | tf_op jit(solution)/shard_map/ppermute | solution.py:439
  226.8 18.9 %collective-permute-start.36 = (bf16[144,16,128]{2,1,0:T(8,128)(2,1)}, bf16[144,16,128]{2,1,0:T(8,128)(2,1)}, u32[]{:S(2)}, u32[]{:S(2)}) collective-permute-start(bf16[144,16,128]{2,1,0:T(8,128)(2,1)} %shard_map.233), channel_id=1, source_target_pairs={{0,2},{1,5},{2,0},{3,7},{4,6},{5,1},{6,4},{7,3},{8,10},{9,13},{10,... | collective-permute-start | bytes 1769480 | tf_op jit(solution)/shard_map/ppermute | solution.py:439
  230.0 14.9 %collective-permute-start.33 = (bf16[110,16,128]{2,1,0:T(8,128)(2,1)}, bf16[110,16,128]{2,1,0:T(8,128)(2,1)S(1)}, u32[]{:S(2)}, u32[]{:S(2)}) collective-permute-start(bf16[110,16,128]{2,1,0:T(8,128)(2,1)} %broadcast_select_fusion), channel_id=1, source_target_pairs={{0,8},{8,24},{16,0},{24,16},{1,9},{9,25},{17,1},{25,17},{2,10},{10... | collective-permute-start | bytes 1351688 | tf_op jit(solution)/shard_map/ppermute | solution.py:455
  230.6 14.3 %collective-permute-start.34 = (bf16[42,16,128]{2,1,0:T(8,128)(2,1)S(1)}, bf16[42,16,128]{2,1,0:T(8,128)(2,1)S(1)}, u32[]{:S(2)}, u32[]{:S(2)}) collective-permute-start(bf16[42,16,128]{2,1,0:T(8,128)(2,1)S(1)} %slice_select_fusion), channel_id=1, source_target_pairs={{0,16},{8,0},{16,24},{24,8},{1,17},{9,1},{17,25},{25,9},{2,18},{10... | collective-permute-start | bytes 516104 | tf_op jit(solution)/shard_map/ppermute | solution.py:455
  233.9 15.5 %collective-permute-start.39 = (bf16[110,16,128]{2,1,0:T(8,128)(2,1)}, bf16[110,16,128]{2,1,0:T(8,128)(2,1)S(1)}, u32[]{:S(2)}, u32[]{:S(2)}) collective-permute-start(bf16[110,16,128]{2,1,0:T(8,128)(2,1)} %convert_element_type.9), channel_id=1, source_target_pairs={{0,2},{1,5},{2,0},{3,7},{4,6},{5,1},{6,4},{7,3},{8,10},{9,13},{10,... | collective-permute-start | bytes 1351688 | tf_op jit(solution)/shard_map/ppermute | solution.py:439
  243.4 13.1 %collective-permute-start.40 = (bf16[110,16,128]{2,1,0:T(8,128)(2,1)}, bf16[110,16,128]{2,1,0:T(8,128)(2,1)}, u32[]{:S(2)}, u32[]{:S(2)}) collective-permute-start(bf16[110,16,128]{2,1,0:T(8,128)(2,1)} %convert_element_type.9), channel_id=1, source_target_pairs={{0,4},{1,3},{2,6},{3,1},{4,0},{5,7},{6,2},{7,5},{8,12},{9,11},{10,... | collective-permute-start | bytes 1351688 | tf_op jit(solution)/shard_map/ppermute | solution.py:439
  249.3 10.8 %collective-permute-start.43 = (bf16[110,16,128]{2,1,0:T(8,128)(2,1)S(1)}, bf16[110,16,128]{2,1,0:T(8,128)(2,1)S(1)}, u32[]{:S(2)}, u32[]{:S(2)}) collective-permute-start(bf16[110,16,128]{2,1,0:T(8,128)(2,1)S(1)} %collective-permute-done.39.rest_0_), channel_id=1, source_target_pairs={{0,4},{1,3},{2,6},{3,1},{4,0},{5,7},{6,2},{7,5},{8,12},{9,11},{10,... | collective-permute-start | bytes 1351688 | tf_op jit(solution)/shard_map/ppermute | solution.py:439
  268.7 13.9 %collective-permute-start.45 = (bf16[110,16,128]{2,1,0:T(8,128)(2,1)S(1)}, bf16[110,16,128]{2,1,0:T(8,128)(2,1)S(1)}, u32[]{:S(2)}, u32[]{:S(2)}) collective-permute-start(bf16[110,16,128]{2,1,0:T(8,128)(2,1)S(1)} %get-tuple-element.122), channel_id=1, source_target_pairs={{0,4},{1,3},{2,6},{3,1},{4,0},{5,7},{6,2},{7,5},{8,12},{9,11},{10,... | collective-permute-start | bytes 1351688 | tf_op jit(solution)/shard_map/ppermute | solution.py:439
  (68 other events, 336.5 us)

commit v3 on v2

--- a/solution.py
+++ b/solution.py
@@ -77,27 +77,29 @@
 
 
 HELD = GROUPS // 2
-SET = 2
-
-
-def piece_at(pieces, s):
-    return pieces[s // HELD].at[s % HELD]
-
-
-def fetch(sc, pieces, steps, parts, raw, sem):
-    for step in range(steps):
-        for at, part in enumerate(parts):
+ARRAYS = 10
+
+
+def piece_at(pieces, step, s):
+    if step < 3:
+        return pieces[2 * step + s // HELD].at[s % HELD]
+    trio, last = pieces[6 + 2 * (s // HELD)], pieces[7 + 2 * (s // HELD)]
+    return last if s % HELD == HELD - 1 else trio.at[s % HELD]
+
+
+def fetch(sc, pieces, raw, sem):
+    for part in range(4):
+        for step in range(4):
 
             @pl.when(sc[8 + part] == step)
             def _():
                 for s in range(GROUPS):
-                    source = piece_at(pieces[step * SET : (step + 1) * SET], s)
-                    pltpu.make_async_copy(source, raw.at[at, s], sem.at[at, s]).start()
-
-
-def fetched(pieces, raw, sem, at):
+                    pltpu.make_async_copy(piece_at(pieces, step, s), raw.at[part, s], sem.at[part, s]).start()
+
+
+def fetched(pieces, raw, sem, part):
     for s in range(GROUPS):
-        pltpu.make_async_copy(piece_at(pieces, s), raw.at[at, s], sem.at[at, s]).wait()
+        pltpu.make_async_copy(piece_at(pieces, 0, s), raw.at[part, s], sem.at[part, s]).wait()
 
 
 def lay_out(slots, raw, at, first, count, dst, dst_first, per_row):
@@ -123,6 +125,22 @@
     return put
 
 
+SHIPPED = 5
+
+
+def shipped(keep, send, outs, span, sem):
+    cuts = [(keep, pl.ds(0, 2)), (keep, pl.ds(2, 2)), (send, pl.ds(0, 2)), (send, 2), (send, 3)]
+    return [
+        pltpu.make_async_copy(source.at[at, span], out.at[span] if isinstance(at, int) else out.at[:, span], sem.at[n])
+        for n, ((source, at), out) in enumerate(zip(cuts, outs))
+    ]
+
+
+def shipped_shapes(count):
+    one = (count, TB // GROUPS, TB)
+    return [pltpu.HBM((2,) + one, BF)] * 3 + [pltpu.HBM(one, BF)] * 2
+
+
 STEP = 256
 
 
@@ -149,15 +167,18 @@
     return jnp.concatenate(rows, axis=0)
 
 
-KEPT = 10
+KEPT = 19
 
 
 def layer(sc, tok, cot, vec, *rest):
-    pieces, rest = rest[: 4 * SET], rest[4 * SET :]
+    pieces, rest = rest[:ARRAYS], rest[ARRAYS:]
     stored, rest = rest[:KEPT], rest[KEPT:]
-    (ks_o, vs_o, lse_o, norm_o, out_o, gr_o, gb_o, gm_o, keep_o, send_o, sums_o) = rest[:11]
-    (raw, q_o, k_o, v_o, mixt_o, wq_o, wk_o, wv_o, wo_o, cm_o, mix_o, fl_o, gh_o, slope, act, gsl, acc, sem, osem) = rest[11:]
-    fetch(sc, pieces, 4, range(4), raw, sem)
+    ks_o, vs_o, lse_o, norm_o, sums_o = rest[:5]
+    (raw, q_o, k_o, v_o, mixt_o, wq_o, wk_o, wv_o, wo_o, cm_o, mix_o, fl_o, gh_o, slope, act, gsl, acc, nf, ni,
+     cot_v, out_o, gr_o, gb_o, gm_o, keep_o, send_o, sem, osem, csem, tsem) = rest[5:]
+    fetch(sc, pieces, raw, sem)
+    cot_copy = pltpu.make_async_copy(cot, cot_v, csem)
+    cot_copy.start()
     slots = [sc[r] for r in range(GROUPS)]
     put = splitter(sc)
     nb = nd = D // TB
@@ -169,20 +190,19 @@
             copy.start()
             copies.append(copy)
 
-    for at in (0, 1):
-        fetched(pieces, raw, sem, at)
+    fetched(pieces, raw, sem, 0)
     for m, dst in enumerate((wq_o, wk_o, wv_o)):
         lay_out(slots, raw, 0, m * QUARTER, QUARTER, dst, 0, nb)
     head = PART - 3 * QUARTER
     lay_out(slots, raw, 0, 3 * QUARTER, head, wo_o, 0, nb)
-    lay_out(slots, raw, 1, 0, QUARTER - head, wo_o, head, nb)
-    lay_out(slots, raw, 1, QUARTER - head, ATT - 4 * QUARTER, cm_o, 0, K // TB)
-    store(wq_o, wk_o, wv_o, cm_o)
     x = tok[...]
     q_o[...] = (nn(x, wq_o[...]) + vec[0:1]).astype(BF)
     k_o[...] = (nn(x, wk_o[...]) + vec[1:2]).astype(BF)
     v_o[...] = (nn(x, wv_o[...]) + vec[2:3]).astype(BF)
-    store(q_o, k_o, v_o)
+    fetched(pieces, raw, sem, 1)
+    lay_out(slots, raw, 1, 0, QUARTER - head, wo_o, head, nb)
+    lay_out(slots, raw, 1, QUARTER - head, ATT - 4 * QUARTER, cm_o, 0, K // TB)
+    store(wq_o, wk_o, wv_o, cm_o, q_o, k_o, v_o)
     masked = jnp.where(valid_rows(sc[12], K), cm_o[...], jnp.zeros((), BF))
     ks_o[...] = tn(masked, k_o[...]).astype(BF)
     vs_o[...] = tn(masked, v_o[...]).astype(BF)
@@ -211,6 +231,8 @@
     store(mixt_o)
     branch = nn(mix_o[...], wo_o[...]) + vec[3:4]
     normed, inverse = layer_norm(x.astype(F32) + branch)
+    nf[...] = normed
+    ni[...] = jnp.broadcast_to(inverse, (NMAX, LANES))
     first = normed * vec[4:5] + vec[5:6]
     fl_o[...] = first.astype(BF)
     store(fl_o)
@@ -230,7 +252,9 @@
     normed2, inverse2 = layer_norm(acc[...])
     result = normed2 * vec[11:12] + vec[12:13]
     out_o[...] = jnp.where(valid, result, 0.0).astype(BF)
-    grad_result = jnp.where(valid, cot[...].astype(F32), 0.0)
+    store(out_o)
+    cot_copy.wait()
+    grad_result = jnp.where(valid, cot_v[...].astype(F32), 0.0)
     sums_o[8:9, :] = column_sum(grad_result * normed2)
     sums_o[9:10, :] = column_sum(grad_result)
     grad_second = norm_backward(grad_result, normed2, inverse2, vec[11:12])
@@ -248,9 +272,12 @@
         for i in range(STEP // TB):
             for j in range(nd):
                 put(keep_o, send_o, (g * (STEP // TB) + i) * nd + j, terms[i * TB : (i + 1) * TB, j * TB : (j + 1) * TB])
+        span = pl.ds(g * (STEP // TB) * nd, (STEP // TB) * nd)
+        for copy in shipped(keep_o, send_o, stored[-SHIPPED:], span, tsem.at[g]):
+            copy.start()
     store(gh_o)
     grad_first = acc[...]
-    normed, inverse = layer_norm(tok[...].astype(F32) + (nn(mix_o[...], wo_o[...]) + vec[3:4]))
+    normed, inverse = nf[...], ni[:, 0:1]
     sums_o[1:2, :] = column_sum(grad_first * normed)
     sums_o[2:3, :] = column_sum(grad_first)
     grad_resid = norm_backward(grad_first, normed, inverse, vec[4:5])
@@ -258,21 +285,36 @@
     low = grad_resid.astype(BF)
     gb_o[...] = low
     sums_o[0:1, :] = column_sum(low)
+    store(gr_o, gb_o)
     gm_o[...] = nt(low, wo_o[...]).astype(BF)
+    store(gm_o)
     for copy in copies:
         copy.wait()
+    for g in range(FF // STEP):
+        span = pl.ds(g * (STEP // TB) * nd, (STEP // TB) * nd)
+        for copy in shipped(keep_o, send_o, stored[-SHIPPED:], span, tsem.at[g]):
+            copy.wait()
 
 
 def attention_backward(sc, tok, q, ks, vs, lse, gm, k, v, gb, mixt, cm, *rest):
-    gq_o, gk_o, gv_o, keep_o, send_o, sums_o, gks_o, gvs_o, *held, sem = rest[-15:]
+    gq_o, gk_o, gv_o, sums_o, *outs = rest[-23:-14]
+    gks_o, gvs_o, keep_o, send_o, *held, sem, tsem = rest[-14:]
+    ships = []
+
+    def ship(n, first, count):
+        for copy in shipped(keep_o, send_o, outs, pl.ds(first, count), tsem.at[n]):
+            copy.start()
+            ships.append(copy)
+
     copies = [
         pltpu.make_async_copy(source, target, sem.at[n])
-        for n, (source, target) in enumerate(zip((q, tok, mixt, cm, k, v), held))
+        for n, (source, target) in enumerate(zip((q, gm, tok, mixt, cm, k, v, gb), held))
     ]
     for copy in copies:
         copy.start()
-    q, tok, mixt, cm, k, v = held
-    copies[0].wait()
+    q, gm, tok, mixt, cm, k, v, gb = held
+    for copy in copies[:2]:
+        copy.wait()
     lane = lax.broadcasted_iota(jnp.int32, (K, LANES), 1) < HD
     zero = jnp.zeros((), BF)
     for p in range(H // 2):
@@ -296,7 +338,7 @@
         gq_o[:, cols] = gqt.astype(BF).T
     put = splitter(sc)
     nd, nk = D // TB, K // TB
-    for copy in copies[1:]:
+    for copy in copies[2:]:
         copy.wait()
     masked = jnp.where(valid_rows(sc[12], K), cm[...], zero)
     gk_o[...] = nn(masked, gks_o[...]).astype(BF)
@@ -310,18 +352,23 @@
         for i in range(nd):
             for j in range(nd):
                 put(keep_o, send_o, m * QUARTER + i * nd + j, terms[i * TB : (i + 1) * TB, j * TB : (j + 1) * TB])
+        ship(m, m * QUARTER, QUARTER)
     comp = nt(k[...], gks_o[...]) + nt(v[...], gvs_o[...])
     comp = jnp.where(valid_rows(sc[12], K), comp, 0.0)
     for i in range(NMAX // TB):
         for j in range(nk):
             put(keep_o, send_o, 4 * QUARTER + i * nk + j, comp[i * TB : (i + 1) * TB, j * TB : (j + 1) * TB])
+    ship(4, 4 * QUARTER, ATT - 4 * QUARTER)
+    for copy in ships:
+        copy.wait()
 
 
 def closing(sc, fl, gh, gr, gq, gk, gv, wq, wk, wv, *rest):
-    keep_o, send_o, in_o, *held, sem = rest[-9:]
+    in_o, *outs = rest[-16:-10]
+    keep_o, send_o, *held, gr_v, sem, tsem = rest[-10:]
     copies = [
         pltpu.make_async_copy(source, target, sem.at[n])
-        for n, (source, target) in enumerate(zip((fl, gh, wq, wk, wv), held))
+        for n, (source, target) in enumerate(zip((fl, gh, wq, wk, wv, gr), (*held, gr_v)))
     ]
     for copy in copies:
         copy.start()
@@ -336,41 +383,51 @@
         for i in range(nd):
             for j in range(STEP // TB):
                 put(keep_o, send_o, i * nh + g * (STEP // TB) + j, terms[i * TB : (i + 1) * TB, j * TB : (j + 1) * TB])
+    ships = shipped(keep_o, send_o, outs, pl.ds(0, HID), tsem)
+    for copy in ships:
+        copy.start()
     for copy in copies[2:]:
         copy.wait()
-    total = gr[...] + nt(gq[...], wq[...])
+    total = gr_v[...] + nt(gq[...], wq[...])
     total = total + nt(gk[...], wk[...])
     total = total + nt(gv[...], wv[...])
     in_o[...] = total.astype(BF)
-
-
-def assemble(at, wide_a, wide_r, wide_x, slim_x, h_half, h_x, *rest):
+    for copy in ships:
+        copy.wait()
+
+
+def assemble(at, wide_a, wide_r, wide_x, slim_x, h_stay, h_x, h_y, h_z, *rest):
     rows_o, low_o, scale = rest[-2], rest[-1], at[1].astype(F32)
     upper = at[0] >= 2
-    end = at[0] % 3 == 0
-    size, slim, late = wide_a.shape[0], slim_x.shape[0], h_half.shape[0]
+    size, slim, late = wide_a.shape[0], slim_x.shape[0], h_stay.shape[0]
 
     def emit(first, count, value):
-        low = (value * (1.0 / scale))
-        rows_o[first : first + count] = low
-        low_o[first : first + count] = low.astype(BF)
-
-    @pl.when(end)
+        value = value * (1.0 / scale)
+        rows_o[first : first + count] = value
+        low_o[first : first + count] = value.astype(BF)
+
+    def hidden(count):
+        value = h_stay[:count].astype(F32)
+        for ref in (h_x, h_y, h_z):
+            value = value + ref[:count].astype(F32)
+        return value
+
+    @pl.when(at[0] % 3 == 0)
     def _():
         emit(0, size, jnp.where(upper, wide_r[...], wide_a[...]).astype(F32) + wide_x[...].astype(F32))
 
     @pl.when(at[0] == 1)
     def _():
         emit(0, slim, wide_a[size - slim :].astype(F32) + slim_x[...].astype(F32))
-        emit(slim, size - slim, h_half[: size - slim].astype(F32) + h_x[: size - slim].astype(F32))
+        emit(slim, size - slim, hidden(size - slim))
 
     @pl.when(at[0] == 2)
     def _():
-        emit(0, late, h_half[...].astype(F32) + h_x[...].astype(F32))
+        emit(0, late, hidden(late))
         emit(late, size - late, wide_r[: size - late].astype(F32) + slim_x[: size - late].astype(F32))
 
 
-BATCH = 10
+BATCH = 22
 
 
 def halves(value):
@@ -378,7 +435,10 @@
     return high, (value - high.astype(F32)).astype(BF)
 
 
-def step_kernel(sc, dec, own, lroot, lstat, rstat, g0, g1, r0, r1, nl_o, nr_o, pre_o, sq_o):
+def step_kernel(sc, dec, size, own, lroot, lstat, rstat, weight, *rest):
+    here, there, lefts, rights = (rest[n * HELD : (n + 1) * HELD] for n in (0, 1, 2, 4))
+    other_lefts, other_rights = rest[3 * HELD : 4 * HELD], rest[5 * HELD : 6 * HELD]
+    nw_o, nl_o, nr_o = rest[6 * HELD :]
     slots = [sc[r] for r in range(GROUPS)]
     even = sc[13] == 0
     mine = [jnp.where(even, slots[2 * m], slots[2 * m + 1]) for m in range(4)]
@@ -387,28 +447,39 @@
     select = (lax.broadcasted_iota(jnp.int32, (16, TB), 1) == pick_row).astype(BF)
     start = pl.program_id(0) * BATCH
 
-    def whole(here, there, n):
+    def ordered(pairs):
         rows = []
-        for m in range(4):
-            a, b = here[mine[m], n], there[other[m], n]
+        for a, b in pairs:
             rows += [jnp.where(even, a, b), jnp.where(even, b, a)]
         return jnp.concatenate(rows, axis=0)
 
+    def tile(refs, slot, n):
+        value = refs[0][n]
+        for at in range(1, HELD):
+            value = jnp.where(slot == at, refs[at][n], value)
+        return value
+
+    def whole(here, there, n):
+        return ordered([(tile(here, mine[m], n), tile(there, other[m], n)) for m in range(4)])
+
     bs = range(BATCH)
-    grads = [whole(g0, g1, n) for n in bs]
+    grads = [whole(here, there, n) for n in bs]
     across = [nt(jnp.concatenate([own[n].astype(BF), select], axis=0), g) for n, g in zip(bs, grads)]
-    heads = [halves(lroot[n]) for n in bs]
-    down = [nn(jnp.concatenate([*h, a[16:].astype(BF)], axis=0), g) for h, a, g in zip(heads, across, grads)]
-    mids = [halves(d[:16] + d[16:32]) for d in down]
-    last = [nn(jnp.concatenate(m, axis=0), whole(r0, r1, n)) for n, m in zip(bs, mids)]
+    left = [jnp.concatenate([whole(lefts, other_lefts, n), *halves(lroot[n])], axis=0) for n in bs]
+    down = [nn(jnp.concatenate([f, a[16:].astype(BF)], axis=0), g) for f, a, g in zip(left, across, grads)]
+    mids = [
+        jnp.concatenate([d[:TB].astype(BF), *halves(d[TB : TB + 16] + d[TB + 16 : TB + 32])], axis=0) for d in down
+    ]
+    last = [nn(m, whole(rights, other_rights, n)) for n, m in zip(bs, mids)]
     for n, a, d, p in zip(bs, across, down, last):
         decay = dec[2 * (start + n)]
         nl_o[n] = decay * lstat[n] + (1.0 - decay) * a[:16]
         decay = dec[2 * (start + n) + 1]
-        nr_o[n] = decay * rstat[n] + (1.0 - decay) * d[32:]
-        pre = p[:16] + p[16:]
-        pre_o[n] = pre
-        sq_o[n] = jnp.sum(pre * pre, axis=0, keepdims=True)
+        nr_o[n] = decay * rstat[n] + (1.0 - decay) * d[TB + 32 :]
+        full = p[:TB]
+        squares = jnp.sum(jnp.sum(full * full, axis=0, keepdims=True), axis=1, keepdims=True)
+        scale = size[start + n] * lax.rsqrt(squares * (1.0 / (TB * TB)) + EPS_STEP)
+        nw_o[n] = weight[n] - STEP_RATE * scale * (p[TB : TB + 16] + p[TB + 16 :])
 
 
 def in_hbm(arrays):
@@ -516,15 +587,7 @@
         input_output_aliases={0: 0},
         compiler_params=pltpu.CompilerParams(vmem_limit_bytes=2**20),
         cost_estimate=pl.CostEstimate(flops=1, bytes_accessed=1, transcendentals=0),
-    )(x, *deps)
-
-
-def plane_gather(own):
-    a = near(own)
-    b = far(own)
-    c = far(a)
-    four = jnp.stack([own, a, b, c])
-    return [four, sibling(four)]
+    )(*in_hbm([x]), *deps)
 
 
 def chosen(index, options):
@@ -536,6 +599,11 @@
 
 EDGE = [(0, 1), (1, 0), (2, 3), (3, 2)]
 INNER = [(0, 0), (1, 2), (2, 1), (3, 3)]
+
+
+CROSS = [(0, 2), (1, 3), (2, 0), (3, 1)]
+SKIP = [(0, 1), (1, 3), (2, 0), (3, 2)]
+TURN = [(0, 2), (1, 0), (2, 3), (3, 1)]
 
 
 def gather_weights(narrow):
@@ -548,67 +616,53 @@
     t2, a1, four0 = gate(z, [eo, o, oe, eo], [a1, [narrow, a0, b0, c0]], (b1,))
     eoe, d0 = along(oe, EDGE), sibling(four0)
     a2, b2, c1 = near(t2), far(t2), far(a1)
-    t3, a2, four1, d0 = gate(z, [eoe, oe, e, eoe], [a2, [t1, a1, b1, c1], d0], (b2,))
+    t3, a2, four1 = gate(z, [eoe, oe, e, eoe], [a2, [t1, a1, b1, c1]], (b2, d0))
     a3, b3, c2, d1 = near(t3), far(t3), far(a2), sibling(four1)
-    a3, four2, d1 = gate(z, [], [a3, [t2, a2, b2, c2], d1], (b3,))
-    c3, d2 = far(a3), sibling(four2)
-    four3, d2 = gate(z, [], [[t3, a3, b3, c3], d2])
-    d3 = sibling(four3)
+    a3, four2, trio = gate(z, [], [a3, [t2, a2, b2, c2], [t3, a3, b3]], (d1,))
+    c3, d2, d3 = far(a3), sibling(four2), sibling(trio)
+    last = sibling(c3)
     steps = chosen(z, [jnp.array(row, jnp.int32) for row in ((0, 1, 2, 3), (1, 0, 2, 3), (2, 1, 0, 3), (3, 2, 1, 0))])
-    return [four0, d0, four1, d1, four2, d2, four3, d3], steps
-
-
-def added(a, b, deps=()):
-    def kernel(x, y, *rest):
-        rest[-1][...] = (x[...].astype(F32) + y[...].astype(F32)).astype(BF)
-
-    return call(kernel, [a, b], [sds(a.shape, BF)], [VM, VM], limit=8, deps=deps)[0]
-
-
-def core_sum(keep, send, deps=()):
-    got = sibling(send)
-
-    def kernel(x, y, *rest):
-        own, first, pair = rest[-3:]
-        for n, (ref, at) in enumerate(((own, None), (first, None), (pair, 0), (pair, 1))):
-            value = (x[n].astype(F32) + y[n].astype(F32)).astype(BF)
-            if at is None:
-                ref[...] = value
-            else:
-                ref[at] = value
-
-    one = keep.shape[1:]
-    return call(
-        kernel, [keep, got], [sds(one, BF), sds(one, BF), sds((2,) + one, BF)], [VM, VM], limit=14,
-        deps=deps,
+    return [four0, d0, four1, d1, four2, d2, trio, c3, d3, last], steps
+
+
+def summed(sources, deps=(), windows=(), scalars=None, split=False):
+    shape, count = sources[0].shape, len(sources)
+
+    def kernel(sc, *refs):
+        outs = refs[count + len(deps) :]
+        value = refs[0][...].astype(F32)
+        for n in range(1, count):
+            value = value + refs[n][...].astype(F32)
+        value = value.astype(BF)
+        if windows:
+            outs[-1][...] = value
+            for out, (start, size) in zip(outs, windows):
+                out[...] = outs[-1][pl.ds(sc[start], size)]
+        elif split:
+            for n, out in enumerate(outs):
+                out[...] = value[n]
+        else:
+            outs[0][...] = value
+
+    shapes = [shape[1:]] * shape[0] if split else [(size,) + shape[1:] for _, size in windows] or [shape]
+    results = call(
+        kernel,
+        [jnp.zeros((1,), jnp.int32) if scalars is None else scalars, *sources],
+        [sds(one, BF) for one in shapes],
+        [SM] + [VM] * count,
+        scratch=[pltpu.VMEM(shape, BF)] if windows else [],
+        limit=12, deps=deps,
     )
-
-
-def last_sum(own, back, last, deps=()):
-    def kernel(x, y, w, *rest):
-        rest[-1][...] = (x[...].astype(F32) + y[0].astype(F32) + w[...].astype(F32)).astype(BF)
-
-    return call(kernel, [own, back, last], [sds(own.shape, BF)], [VM] * 3, limit=8, deps=deps)[0]
-
-
-def first_sum(first, back, deps=()):
-    def kernel(x, y, *rest):
-        rest[-1][...] = (x[...].astype(F32) + y[1].astype(F32)).astype(BF)
-
-    return call(kernel, [first, back], [sds(first.shape, BF)], [VM] * 2, limit=8, deps=deps)[0]
-
-
-CROSS = [(0, 2), (1, 3), (2, 0), (3, 1)]
-SKIP = [(0, 1), (1, 3), (2, 0), (3, 2)]
-TURN = [(0, 2), (1, 0), (2, 3), (3, 1)]
-
-
-def pair_parts(odd, rows, cut):
-    size = max(cut, rows.shape[0] - cut)
-    even_at, odd_at = 0, rows.shape[0] - size
-    stay = lax.dynamic_slice_in_dim(rows, jnp.where(odd, odd_at, even_at), size, 0)
-    leave = lax.dynamic_slice_in_dim(rows, jnp.where(odd, even_at, odd_at), size, 0)
-    return stay, leave
+    return results if len(shapes) > 1 else results[0]
+
+
+def pair_sum(keep, send, deps=()):
+    def kernel(x, y, z, *rest):
+        for n, ref in enumerate((y, z)):
+            rest[-1][n] = (x[n].astype(F32) + ref[...].astype(F32)).astype(BF)
+
+    got = [sibling(one) for one in send]
+    return call(kernel, [*in_hbm([keep]), *got], [sds(keep.shape, BF)], [VM] * 3, limit=12, deps=deps)[0]
 
 
 def plane_sum(x):
@@ -651,7 +705,10 @@
         pieces = []
         for t in range(NBLK // PART):
             every = [full[t, :, place[s]] for s in range(GROUPS)]
-            pieces += [jnp.stack(every[:HELD]), jnp.stack(every[HELD:])]
+            if t < 3:
+                pieces += [jnp.stack(every[:HELD]), jnp.stack(every[HELD:])]
+            else:
+                pieces += [jnp.stack(every[:3]), every[3], jnp.stack(every[4:7]), every[7]]
         steps = jnp.arange(4, dtype=jnp.int32)
     scalars = jnp.concatenate([slots, steps, lengths, core[None], me[None]]).astype(jnp.int32)
 
@@ -663,15 +720,16 @@
     square = (D, D)
     r_terms = sds((4, HID, row16, TB), BF)
     a_terms = sds((4, ATT, row16, TB), BF)
-    held = [square, square, square, (NMAX, K), shape, shape, shape, (D, NMAX), shape, (NMAX, FF)]
-    (wq, wk, wv, cm, q, k, v, mixt, fl, gh,
-     ks, vs, lse, norms, out, gr, gb, gm, r_keep, r_send, sums_b) = call(
+    held = [square, square, square, (NMAX, K), shape, shape, shape, (D, NMAX), shape, shape, (NMAX, FF)]
+    (wq, wk, wv, cm, q, k, v, mixt, fl, out, gh, gr, gb, gm, *r_ship, ks, vs, lse, norms, sums_b) = call(
         layer,
-        [scalars, tok, cot, vectors] + in_hbm(pieces),
+        [scalars, tok, *in_hbm([cot]), vectors] + in_hbm(pieces),
         [pltpu.HBM(one, BF) for one in held]
-        + [summary, summary, sds((H, NMAX), F32), sds((2, LANES), F32), act, wide, act, act, r_terms, r_terms, sds((10, D), F32)],
-        [SM, VM, VM, VM] + [ANY] * (4 * SET),
-        [ANY] * KEPT + [VM] * 11,
+        + [pltpu.HBM(shape, F32), pltpu.HBM(shape, BF), pltpu.HBM(shape, BF)]
+        + shipped_shapes(HID)
+        + [summary, summary, sds((H, NMAX), F32), sds((2, LANES), F32), sds((10, D), F32)],
+        [SM, VM, ANY, VM] + [ANY] * ARRAYS,
+        [ANY] * KEPT + [VM] * 5,
         scratch=[
             pltpu.VMEM((4, GROUPS, PART, row16, TB), BF),
             *[pltpu.VMEM(one, BF) for one in (shape, shape, shape, (D, NMAX), square, square, square, square, (NMAX, K), shape, shape, (NMAX, FF))],
@@ -679,115 +737,141 @@
             pltpu.VMEM((NMAX, FF), BF),
             pltpu.VMEM(shape, BF),
             pltpu.VMEM(shape, F32),
+            pltpu.VMEM(shape, F32),
+            pltpu.VMEM((NMAX, LANES), F32),
+            pltpu.VMEM(shape, BF),
+            pltpu.VMEM(shape, BF),
+            pltpu.VMEM(shape, F32),
+            pltpu.VMEM(shape, BF),
+            pltpu.VMEM(shape, BF),
+            pltpu.VMEM(r_terms.shape, BF),
+            pltpu.VMEM(r_terms.shape, BF),
             pltpu.SemaphoreType.DMA((4, GROUPS)),
-            pltpu.SemaphoreType.DMA((KEPT,)),
+            pltpu.SemaphoreType.DMA((KEPT - SHIPPED,)),
+            pltpu.SemaphoreType.DMA(()),
+            pltpu.SemaphoreType.DMA((FF // STEP, SHIPPED)),
         ],
-        limit=58,
+        limit=60,
     )
     deps = ()
     if staged:
-        r_here, r_first, r_pair = core_sum(r_keep, r_send)
+        z = lax.axis_index("dp")
+        odd = z % 2
+        cut_r = 3 * PART - (ATT + HID)
+        cut_h = 2 * PART - ATT
+        rest_a, rest_h = ATT - PART, HID - cut_h
+        ranges = jnp.stack([odd * cut_r, (1 - odd) * cut_r, odd * rest_a, (1 - odd) * rest_a, (1 - odd) * cut_h, odd * cut_h])
+        right, left = right_root.astype(BF), left_root.astype(BF)
+        roots = jnp.stack([left, right])
+        roots = [roots, near(roots), far(roots), toward(roots, lambda i: i ^ 6)]
+        r_rest, r_keep, send_rest, *send = r_ship
+        r_pair = pair_sum(r_keep, [tie(send[0], roots[1:]), send[1]])
         r_back = far(r_pair)
+        r_came = sibling(send_rest)
+        other_roots = [sibling(piece) for piece in roots]
         deps = (r_pair,)
-    gq, gk, gv, a_keep, a_send, sums_a = call(
+    gq, gk, gv, sums_a, *a_ship = call(
         attention_backward,
-        [scalars, *in_hbm([tok, q]), ks, vs, lse, gm, *in_hbm([k, v]), gb, *in_hbm([mixt, cm])],
-        [act, act, act, a_terms, a_terms, sds((3, D), F32)],
-        [SM, ANY, ANY] + [VM] * 4 + [ANY, ANY, VM, ANY, ANY],
+        [scalars, *in_hbm([tok, q]), ks, vs, lse, *in_hbm([gm, k, v, gb, mixt, cm])],
+        [act, act, act, sds((3, D), F32)] + shipped_shapes(ATT),
+        [SM, ANY, ANY] + [VM] * 3 + [ANY] * 6,
+        [VM] * 4 + [ANY] * SHIPPED,
         scratch=[
-            *[pltpu.VMEM(one, BF) for one in ((K, D), (K, D), shape, shape, (D, NMAX), (NMAX, K), shape, shape)],
-            pltpu.SemaphoreType.DMA((6,)),
-        ],
-        limit=28, deps=deps,
-    )
-    if staged:
-        r_first = first_sum(r_first, r_back)
-        r_last = near(r_first)
-        a_here, a_first, a_pair = core_sum(a_keep, tie(a_send, (r_first,)), (r_last,))
-        r_rows = last_sum(r_here, r_back, r_last)
-        r_stay, r_leave = pair_parts(lax.axis_index("dp") % 2 == 1, r_rows, 3 * PART - (ATT + HID))
-        a_back = far(a_pair)
-        r_came = along(r_leave, EDGE)
-        deps = (a_pair, r_leave)
-    h_keep, h_send, in_grads = call(
-        closing,
-        [scalars, *in_hbm([fl, gh]), gr, gq, gk, gv, *in_hbm([wq, wk, wv])],
-        [r_terms, r_terms, act],
-        [SM, ANY, ANY] + [VM] * 4 + [ANY] * 3,
-        scratch=[
-            *[pltpu.VMEM(one, BF) for one in (shape, (NMAX, FF), square, square, square)],
-            pltpu.SemaphoreType.DMA((5,)),
+            *[pltpu.VMEM(one, BF) for one in ((K, D), (K, D), a_terms.shape, a_terms.shape, shape, shape, shape, (D, NMAX), (NMAX, K), shape, shape, shape)],
+            pltpu.SemaphoreType.DMA((8,)),
+            pltpu.SemaphoreType.DMA((5, SHIPPED)),
         ],
         limit=28, deps=deps,
     )
     local_vectors = jnp.concatenate([sums_a, sums_b], axis=0)
     local_norms = norms[:, 0]
     if staged:
-        z = lax.axis_index("dp")
-        odd = z % 2 == 1
-        cut_r = 3 * PART - (ATT + HID)
-        cut_h = 2 * PART - ATT
-        rest_a, rest_h = ATT - PART, HID - cut_h
-        packed = jnp.concatenate([local_vectors, jnp.pad(local_norms[None], ((0, 0), (0, D - 2)))], axis=0)
+        weight_sums = jnp.sum(weights * weights, axis=(1, 2))
+        packed = jnp.concatenate([local_norms, weight_sums, jnp.zeros((D - 2 - PART,), F32)])
+        packed = jnp.concatenate([local_vectors, packed[None]], axis=0)
         packed = packed + sibling(packed)
-        a_first = first_sum(a_first, a_back, (r_came, packed))
-        r_half = added(r_stay, r_came, (a_back,))
+        r_own, r_first = summed([*in_hbm([r_rest]), r_came, r_back], other_roots, split=True)
+        r_last = near(r_first)
+        a_rest, a_keep, send_rest, *send = a_ship
+        a_pair = pair_sum(a_keep, [tie(send[0], (r_first,)), send[1]], (packed,))
+        a_back = far(a_pair)
+        a_came = sibling(send_rest)
+        r_stay, r_leave = summed([r_own, r_last], (), [(0, PART), (1, PART)], ranges)
+        r_edge = along(r_leave, EDGE)
+        deps = (a_pair,)
+    in_grads, *h_ship = call(
+        closing,
+        [scalars, *in_hbm([fl, gh, gr]), gq, gk, gv, *in_hbm([wq, wk, wv])],
+        [act] + shipped_shapes(HID),
+        [SM, ANY, ANY, ANY] + [VM] * 3 + [ANY] * 3,
+        [VM] + [ANY] * SHIPPED,
+        scratch=[
+            *[pltpu.VMEM(one, BF) for one in (r_terms.shape, r_terms.shape, shape, (NMAX, FF), square, square, square)],
+            pltpu.VMEM(shape, F32),
+            pltpu.SemaphoreType.DMA((6,)),
+            pltpu.SemaphoreType.DMA((SHIPPED,)),
+        ],
+        limit=28, deps=deps,
+    )
+    if staged:
+        packed = packed + toward(packed, lambda i: i ^ 2)
+        a_own, a_first = summed([*in_hbm([a_rest]), a_came, a_back], (r_leave, packed), split=True)
         a_last = near(a_first)
-        packed = packed + toward(packed, lambda i: i ^ 2)
-        h_here, h_first, h_pair = core_sum(h_keep, tie(h_send, (a_first,)), (a_last, packed))
-        a_rows = last_sum(a_here, a_back, a_last)
+        h_rest, h_keep, send_rest, *send = h_ship
+        h_pair = pair_sum(h_keep, send)
         h_back = far(h_pair)
-        a_stay, a_leave = pair_parts(odd, a_rows, PART)
-        a_came = along(a_leave, EDGE)
+        h_came = sibling(send_rest)
+        a_stay, a_leave = summed([a_own, a_last], (), [(2, PART), (3, PART)], ranges)
+        a_edge = along(a_leave, EDGE)
         packed = packed + toward(packed, lambda i: i ^ 4)
-        h_first = first_sum(h_first, h_back, (a_came, packed))
-        a_half = added(a_stay, a_came, (h_back,))
+        weight_squares = packed[-1, 2 : 2 + PART]
+        h_own, h_first = summed([*in_hbm([h_rest]), h_came, h_back], (r_edge, a_leave, packed), split=True)
         h_last = near(h_first)
+        r_half = summed([r_stay, r_edge], (h_first,))
+        a_half = summed([a_stay, a_edge], (h_first,))
         upper = z >= 2
         wide_cross = along(jnp.where(upper, a_half, r_half), SKIP)
         slim_cross = along(jnp.where(upper, a_half[PART - rest_a :], r_half[:rest_a]), TURN)
         packed = packed + along(packed, EDGE)
-        h_rows = last_sum(h_here, h_back, h_last, (wide_cross, slim_cross, packed))
-        h_stay = lax.dynamic_slice_in_dim(h_rows, jnp.where(odd, 0, cut_h), rest_h, 0)
-        h_leave = lax.dynamic_slice_in_dim(h_rows, jnp.where(odd, cut_h, 0), rest_h, 0)
-        h_came = along(h_leave, EDGE)
-        root = right_root.astype(BF)
-        root_near, root_far = near(root), far(root)
+        h_stay, h_leave = summed([h_own, h_last], (packed,), [(4, rest_h), (5, rest_h)], ranges)
+        h_edge, h_inner, h_turn = along(h_leave, EDGE), along(h_leave, INNER), along(h_stay, TURN)
         packed = packed + along(packed, CROSS)
-        h_half = added(h_stay, h_came, (root_near, root_far, packed))
-        h_cross = along(h_half, TURN)
-        root_diag = far(root_near)
         grad_rows, low_rows = call(
             assemble,
-            [jnp.stack([z, jnp.int32(seq_total)]), a_half, r_half, wide_cross, slim_cross, h_half, h_cross],
-            [sds(weights.shape, F32), sds(weights.shape, BF)],
-            [SM] + [VM] * 6,
-            limit=8, deps=(root_diag,),
+            [jnp.stack([z, jnp.int32(seq_total)])]
+            + [a_half, r_half, wide_cross, slim_cross, h_stay, h_edge, h_inner, h_turn],
+            [pltpu.HBM(weights.shape, F32), sds(weights.shape, BF)],
+            [SM] + [VM] * 8,
+            limit=10, deps=(packed,),
         )
         vector_total, norm_totals = packed[:-1], packed[-1, :2]
-        root_four = jnp.stack([root, root_near, root_far, root_diag])
-        blocks = plane_gather(low_rows) + [root_four, sibling(root_four)]
+        low_near, low_far = near(low_rows), far(low_rows)
+        low = [low_rows, low_near, low_far, far(low_near)]
         rows = sds(weights.shape, F32)
         one = pl.BlockSpec((BATCH, row16, TB), lambda n: (n, 0, 0))
-        four = pl.BlockSpec((HELD, BATCH, row16, TB), lambda n: (0, n, 0, 0))
-        new_left, new_right, precond, squares = pl.pallas_call(
+        halved = [pl.BlockSpec((None, BATCH, row16, TB), lambda n, at=at: (at, n, 0, 0)) for at in range(2)]
+        new_weights, new_left, new_right = pl.pallas_call(
             step_kernel,
             grid=(PART // BATCH,),
-            out_shape=[rows, rows, rows, sds((PART, 1, LANES), F32)],
-            in_specs=[SM, SM] + [one] * 4 + [four] * 4,
-            out_specs=[one, one, one, pl.BlockSpec((BATCH, 1, LANES), lambda n: (n, 0, 0))],
-            compiler_params=pltpu.CompilerParams(vmem_limit_bytes=16 * 1024 * 1024),
+            out_shape=[rows, rows, rows],
+            in_specs=[SM, SM, SM] + [one] * (5 + GROUPS) + [halved[0]] * GROUPS + [halved[1]] * GROUPS,
+            out_specs=[one, one, one],
+            compiler_params=pltpu.CompilerParams(vmem_limit_bytes=24 * 1024 * 1024),
             cost_estimate=pl.CostEstimate(flops=1, bytes_accessed=1, transcendentals=0),
-        )(scalars, decays.reshape(-1), grad_rows, left_root, left_stats, right_stats, *blocks)
-        squares = squares[:, 0]
-        both = jnp.stack([jnp.sum(squares, axis=1), jnp.sum(weights * weights, axis=(1, 2))])
-        precond_squares, weight_squares = plane_sum(both)
+        )(
+            scalars, decays.reshape(-1), jnp.sqrt(weight_squares / (TB * TB)),
+            *in_hbm([
+                grad_rows, left_root, left_stats, right_stats, weights,
+                *low, *(sibling(piece) for piece in low),
+                *roots, *other_roots, *roots, *other_roots,
+            ]),
+        )
     else:
-        def join(keep, send):
-            both = jnp.concatenate([keep, send], axis=0)
+        def join(ship):
+            both = jnp.concatenate(ship[:3] + [ship[3][None], ship[4][None]], axis=0)
             return jnp.stack([both[s] for s in SLOT_TABLE], axis=1).reshape(-1, TB, TB)
 
-        every = jnp.concatenate([join(a_keep, a_send), join(h_keep, h_send), join(r_keep, r_send)], axis=0)
+        every = jnp.concatenate([join(a_ship), join(h_ship), join(r_ship)], axis=0)
         inner = lax.psum_scatter(every, "fsdp", scatter_dimension=1, tiled=True)
         total = lax.psum_scatter(inner, "dp", scatter_dimension=0, tiled=True).astype(F32)
         grad_rows = total / seq_total
@@ -808,12 +892,12 @@
         precond_squares, weight_squares = lax.psum(
             (jnp.sum(precond * precond, axis=(1, 2)), jnp.sum(weights * weights, axis=(1, 2))), "fsdp"
         )
+        tile_area = TB * TB
+        weight_scale = jnp.sqrt(weight_squares / tile_area)
+        precond_scale = lax.rsqrt(precond_squares / tile_area + EPS_STEP)
+        new_weights = weights - STEP_RATE * (weight_scale * precond_scale)[:, None, None] * precond
     vector_grad = vector_total / seq_total
     summary_norms = norm_totals / seq_total
-    tile_area = TB * TB
-    weight_scale = jnp.sqrt(weight_squares / tile_area)
-    precond_scale = lax.rsqrt(precond_squares / tile_area + EPS_STEP)
-    new_weights = weights - STEP_RATE * (weight_scale * precond_scale)[:, None, None] * precond
     new_moments = MOMENT_DECAY * moments + (1.0 - MOMENT_DECAY) * vector_grad
     row_scale = jnp.sqrt(jnp.mean(jnp.square(vectors), axis=1, keepdims=True))
     moment_scale = lax.rsqrt(jnp.mean(jnp.square(new_moments), axis=1, keepdims=True) + EPS_STEP)

time: 324 us -> 292 us (0.901)
  waiting for transfers between devices: 143 us -> 123 us
  local copies, waits for them, and re-layouts: 21.1 us -> 5.24 us
  Pallas kernels: 88.6 us -> 96.1 us
  other arithmetic: 12.7 us -> 5.46 us
  starting transfers between devices: 52.3 us -> 57.3 us
    ppermute x39 -> x49, waiting for transfers between devices: 116 us -> 93.4 us  [toward(): return lax.ppermute(x, 'fsdp', [(i, move(i)) for i in range(GROUPS)])]
    unnamed x97 -> x81, local copies, waits for them, and re-layouts: 18.8 us -> 4.33 us
    pallas_call x16 -> x15, Pallas kernels: 69.5 us -> 78.6 us  [call(): pl.pallas_call(kernel, out_shape=outs, in_specs=in_specs + [ANY] * len(de...]
    ppermute x39 -> x49, starting transfers between devices: 33.8 us -> 37.2 us  [toward(): return lax.ppermute(x, 'fsdp', [(i, move(i)) for i in range(GROUPS)])]
    pallas_call x5 -> x4, Pallas kernels: 8.7 us -> 6.55 us  [gate(): pl.pallas_call(kernel, out_shape=outs, in_specs=[SM] + [ANY] * (count + l...]
    ppermute x13 -> x14, waiting for transfers between devices: 27.2 us -> 29.3 us  [along(): return lax.ppermute(x, 'dp', pairs)]
    ppermute x13 -> x14, starting transfers between devices: 18.5 us -> 20.1 us  [along(): return lax.ppermute(x, 'dp', pairs)]
  transfers between devices with their start and end apart: 52 -> 63, of which waited for: 30 -> 29; matrix products, arithmetic and copies ran while one was open for 3% -> 1% of each run, Pallas kernels for 8% -> 27%
where the time goes in v3:
time: 292 us; the launch traced here: 289 us
  waiting for transfers between devices  123 us (42%)
  Pallas kernels  96.1 us (33%)
  starting transfers between devices  57.3 us (20%)
  other arithmetic  5.46 us (2%)
  local copies, waits for them, and re-layouts  5.24 us (2%)
    ppermute x49, waiting for transfers between devices, toward(): return lax.ppermute(x, 'fsdp', [(i, move(i)) for i in range(GROUPS)])  93.4 us
    pallas_call x15, Pallas kernels, call(): pl.pallas_call(kernel, out_shape=outs, in_specs=in_specs + [ANY] * len(de...  78.6 us
    ppermute x49, starting transfers between devices, toward(): return lax.ppermute(x, 'fsdp', [(i, move(i)) for i in range(GROUPS)])  37.2 us
    ppermute x14, waiting for transfers between devices, along(): return lax.ppermute(x, 'dp', pairs)  29.3 us
    ppermute x14, starting transfers between devices, along(): return lax.ppermute(x, 'dp', pairs)  20.1 us
    pallas_call x1, Pallas kernels, local(): pl.pallas_call(step_kernel, grid=(PART // BATCH,), out_shape=[rows, rows,...  11 us
    pallas_call x4, Pallas kernels, gate(): pl.pallas_call(kernel, out_shape=outs, in_specs=[SM] + [ANY] * (count + l...  6.55 us
  transfers between devices with their start and end apart: 63, of which 29 were waited for; matrix products, arithmetic and copies ran while one was open for 1% of the time, Pallas kernels for 27%

profile of v3, /device:TPU:0, one launch (start us, length us, event | category | flops | bytes accessed | tf_op | source)
XLA Modules:
  0.0 289.0 jit_solution(4756983621868093632)
XLA Ops:
  0.6 2.4 multiply_reduce_fusion
  3.8 5.9 %collective-permute-start.2 = (bf16[110,16,128]{2,1,0:T(8,128)(2,1)S(1)}, bf16[110,16,128]{2,1,0:T(8,128)(2,1)S(1)}, u32[]{:S(2)}, u32[]{:S(2)}) collective-permute-start(bf16[110,16,128]{2,1,0:T(8,128)(2,1)S(1)} %get-tuple-element.146.refs_5_), channel_id=1, source_target_pairs={{0,8},{8,0},{16,24},{24,16},{1,9},{9,1},{17,25},{25,17},{2,10},{10... | collective-permute-start | bytes 1351688 | tf_op jit(solution)/shard_map/ppermute | solution.py:526
  12.7 7.0 %collective-permute-done.2.refs_0_.refs_1_.refs_3_.refs_2_ = bf16[110,16,128]{2,1,0:T(8,128)(2,1)S(1)} collective-permute-done((bf16[110,16,128]{2,1,0:T(8,128)(2,1)S(1)}, bf16[110,16,128]{2,1,0:T(8,128)(2,1)S(1)}, u32[]{:S(2)}, u32[]{:S(2)}) %collective-permute-start.2) | collective-permute-done | bytes 450592 | tf_op jit(solution)/shard_map/ppermute | solution.py:526
  19.7 2.7 collective-permute-done.5.refs_5_.refs_7_
  26.3 2.1 collective-permute-start.1
  28.4 6.7 %collective-permute-done.8.refs_9_.refs_7_ = bf16[110,16,128]{2,1,0:T(8,128)(2,1)S(1)} collective-permute-done((bf16[110,16,128]{2,1,0:T(8,128)(2,1)S(1)}, bf16[110,16,128]{2,1,0:T(8,128)(2,1)S(1)}, u32[]{:S(2)}, u32[]{:S(2)}) %collective-permute-start.8) | collective-permute-done | bytes 450592 | tf_op jit(solution)/shard_map/ppermute | solution.py:510
  35.0 2.8 collective-permute-done.6.refs_4_
  37.8 2.1 collective-permute-done.7.refs_8_
  45.7 8.3 %collective-permute-done.13.refs_9_.refs_3_ = bf16[110,16,128]{2,1,0:T(8,128)(2,1)S(1)} collective-permute-done((bf16[110,16,128]{2,1,0:T(8,128)(2,1)S(1)}, bf16[110,16,128]{2,1,0:T(8,128)(2,1)S(1)}, u32[]{:S(2)}, u32[]{:S(2)}) %collective-permute-start.13) | collective-permute-done | bytes 450592 | tf_op jit(solution)/shard_map/ppermute | solution.py:510
  54.0 2.4 collective-permute-done.11.refs_4_
  56.4 3.2 %collective-permute-done.12.refs_8_ = bf16[110,16,128]{2,1,0:T(8,128)(2,1)S(1)} collective-permute-done((bf16[110,16,128]{2,1,0:T(8,128)(2,1)S(1)}, bf16[110,16,128]{2,1,0:T(8,128)(2,1)S(1)}, u32[]{:S(2)}, u32[]{:S(2)}) %collective-permute-start.12) | collective-permute-done | bytes 450592 | tf_op jit(solution)/shard_map/ppermute | solution.py:510
  64.8 9.3 %collective-permute-done.15.refs_0_.refs_6_ = bf16[110,16,128]{2,1,0:T(8,128)(2,1)S(1)} collective-permute-done((bf16[110,16,128]{2,1,0:T(8,128)(2,1)S(1)}, bf16[110,16,128]{2,1,0:T(8,128)(2,1)S(1)}, u32[]{:S(2)}, u32[]{:S(2)}) %collective-permute-start.15) | collective-permute-done | bytes 450592 | tf_op jit(solution)/shard_map/ppermute | solution.py:510
  74.3 4.8 %collective-permute-done.17.refs_7_ = bf16[110,16,128]{2,1,0:T(8,128)(2,1)S(1)} collective-permute-done((bf16[110,16,128]{2,1,0:T(8,128)(2,1)S(1)}, bf16[110,16,128]{2,1,0:T(8,128)(2,1)S(1)}, u32[]{:S(2)}, u32[]{:S(2)}) %collective-permute-start.17) | collective-permute-done | bytes 450592 | tf_op jit(solution)/shard_map/ppermute | solution.py:510
  79.1 2.6 shard_map.217
  83.5 7.1 %collective-permute-done.19.rest_7_ = bf16[110,16,128]{2,1,0:T(8,128)(2,1)S(1)} collective-permute-done((bf16[110,16,128]{2,1,0:T(8,128)(2,1)S(1)}, bf16[110,16,128]{2,1,0:T(8,128)(2,1)S(1)}, u32[]{:S(2)}, u32[]{:S(2)}) %collective-permute-start.19) | collective-permute-done | bytes 450592 | tf_op jit(solution)/shard_map/ppermute | solution.py:510
  97.2 37.4 %shard_map.218 = (bf16[768,768]{1,0:T(8,128)(2,1)}, bf16[768,768]{1,0:T(8,128)(2,1)}, bf16[768,768]{1,0:T(8,128)(2,1)}, bf16[512,256]{1,0:T(8,128)(2,1)}, bf16[5...) custom-call(s32[15]{0:T(128)} %concatenate.9.sc, ...), custom_call_target="tpu_custom_call" | custom-call | flops 1 | bytes 1 | tf_op jit(solution)/shard_map/pallas_call | solution.py:490
  142.6 12.7 %shard_map.221 = (bf16[512,768]{1,0:T(8,128)(2,1)S(1)}, bf16[512,768]{1,0:T(8,128)(2,1)S(1)}, bf16[512,768]{1,0:T(8,128)(2,1)S(1)}, f32[3,768]{1,0:T(4,128)S(1)}...) custom-call(s32[15]{0:T(128)S(1)} %copy-done.18, ...), custom_call_target="tpu_custom_call" | custom-call | flops 1 | bytes 1 | tf_op jit(solution)/shard_map/pallas_call | solution.py:490
  163.9 10.0 %shard_map.225 = (bf16[512,768]{1,0:T(8,128)(2,1)}, bf16[2,144,16,128]{3,2,1,0:T(8,128)(2,1)}, bf16[2,144,16,128]{3,2,1,0:T(8,128)(2,1)}, bf16[2,144,16,128]{3,2...) custom-call(s32[15]{0:T(128)S(1)} %copy-done.18, ...), custom_call_target="tpu_custom_call" | custom-call | flops 1 | bytes 1 | tf_op jit(solution)/shard_map/pallas_call | solution.py:490
  177.5 2.6 shard_map.229
  180.1 8.6 %collective-permute-done.36 = f32[14,768]{1,0:T(8,128)S(1)} collective-permute-done((f32[14,768]{1,0:T(8,128)S(1)}, f32[14,768]{1,0:T(8,128)S(1)}, u32[]{:S(2)}, u32[]{:S(2)}) %collective-permute-start.36) | collective-permute-done | bytes 43040 | tf_op jit(solution)/shard_map/ppermute | solution.py:510
  192.1 2.1 shard_map.227
  196.1 9.3 %collective-permute-done.41.refs_1_ = bf16[152,16,128]{2,1,0:T(8,128)(2,1)S(1)} collective-permute-done((bf16[152,16,128]{2,1,0:T(8,128)(2,1)S(1)}, bf16[152,16,128]{2,1,0:T(8,128)(2,1)S(1)}, u32[]{:S(2)}, u32[]{:S(2)}) %collective-permute-start.41) | collective-permute-done | bytes 622624 | tf_op jit(solution)/shard_map/ppermute | solution.py:510
  208.2 4.5 %collective-permute-done.37 = f32[14,768]{1,0:T(8,128)S(1)} collective-permute-done((f32[14,768]{1,0:T(8,128)S(1)}, f32[14,768]{1,0:T(8,128)S(1)}, u32[]{:S(2)}, u32[]{:S(2)}) %collective-permute-start.37) | collective-permute-done | bytes 43040 | tf_op jit(solution)/shard_map/ppermute | solution.py:510
  212.8 2.4 shard_map.230
  221.0 2.4 collective-permute-start.55
  227.4 4.2 %collective-permute-start.54 = (bf16[76,16,128]{2,1,0:T(8,128)(2,1)S(1)}, bf16[76,16,128]{2,1,0:T(8,128)(2,1)S(1)}, u32[]{:S(2)}, u32[]{:S(2)}) collective-permute-start(bf16[76,16,128]{2,1,0:T(8,128)(2,1)S(1)} %get-tuple-element.136.h_stay), channel_id=1, source_target_pairs={{0,16},{8,0},{16,24},{24,8},{1,17},{9,1},{17,25},{25,9},{2,18},{10... | collective-permute-start | bytes 933896 | tf_op jit(solution)/shard_map/ppermute | solution.py:526
  231.6 5.0 %collective-permute-done.55 = f32[14,768]{1,0:T(8,128)S(1)} collective-permute-done((f32[14,768]{1,0:T(8,128)S(1)}, f32[14,768]{1,0:T(8,128)S(1)}, u32[]{:S(2)}, u32[]{:S(2)}) %collective-permute-start.55) | collective-permute-done | bytes 43040 | tf_op jit(solution)/shard_map/ppermute | solution.py:526
  236.7 15.4 %collective-permute-done.49.slim_x = bf16[42,16,128]{2,1,0:T(8,128)(2,1)S(1)} collective-permute-done((bf16[42,16,128]{2,1,0:T(8,128)(2,1)S(1)}, bf16[42,16,128]{2,1,0:T(8,128)(2,1)S(1)}, u32[]{:S(2)}, u32[]{:S(2)}) %collective-permute-start.49) | collective-permute-done | bytes 172064 | tf_op jit(solution)/shard_map/ppermute | solution.py:526
  252.2 2.0 shard_map.234
  257.5 9.3 %collective-permute-done.56.rest_1_ = bf16[110,16,128]{2,1,0:T(8,128)(2,1)S(1)} collective-permute-done((bf16[110,16,128]{2,1,0:T(8,128)(2,1)S(1)}, bf16[110,16,128]{2,1,0:T(8,128)(2,1)S(1)}, u32[]{:S(2)}, u32[]{:S(2)}) %collective-permute-start.56) | collective-permute-done | bytes 450592 | tf_op jit(solution)/shard_map/ppermute | solution.py:510
  270.0 5.2 %collective-permute-done.58.rest_3_ = bf16[110,16,128]{2,1,0:T(8,128)(2,1)S(1)} collective-permute-done((bf16[110,16,128]{2,1,0:T(8,128)(2,1)S(1)}, bf16[110,16,128]{2,1,0:T(8,128)(2,1)S(1)}, u32[]{:S(2)}, u32[]{:S(2)}) %collective-permute-start.58) | collective-permute-done | bytes 450592 | tf_op jit(solution)/shard_map/ppermute | solution.py:510
  277.8 11.0 %shard_map.235 = (f32[110,16,128]{2,1,0:T(8,128)}, f32[110,16,128]{2,1,0:T(8,128)}, f32[110,16,128]{2,1,0:T(8,128)}) custom-call(s32[15]{0:T(128)S(1)} %copy-done.18, f32[220]{0:T(256)S(1)} %reshape.42.dec, f32[110]{0:T(128)S(1)} %fusion.4.size, f32[110,16,128]{2,1,0:T(8,128)} %get-tuple-element.70.own, f32[110,16,128]{2,1,0:T(8,128)} %lroot.1, ...), custom_call_target="tpu_custom_call" | custom-call | flops 1 | bytes 1 | tf_op jit(solution)/shard_map/pallas_call | solution.py:853
  (225 shorter events, 73.3 us)
Async XLA Ops:
  3.8 15.9 %collective-permute-start.2 = (bf16[110,16,128]{2,1,0:T(8,128)(2,1)S(1)}, bf16[110,16,128]{2,1,0:T(8,128)(2,1)S(1)}, u32[]{:S(2)}, u32[]{:S(2)}) collective-permute-start(bf16[110,16,128]{2,1,0:T(8,128)(2,1)S(1)} %get-tuple-element.146.refs_5_), channel_id=1, source_target_pairs={{0,8},{8,0},{16,24},{24,16},{1,9},{9,1},{17,25},{25,17},{2,10},{10... | collective-permute-start | bytes 1351688 | tf_op jit(solution)/shard_map/ppermute | solution.py:526
  25.1 14.8 %collective-permute-start.7 = (bf16[110,16,128]{2,1,0:T(8,128)(2,1)S(1)}, bf16[110,16,128]{2,1,0:T(8,128)(2,1)S(1)}, u32[]{:S(2)}, u32[]{:S(2)}) collective-permute-start(bf16[110,16,128]{2,1,0:T(8,128)(2,1)S(1)} %get-tuple-element.77.refs_6_), channel_id=1, source_target_pairs={{0,4},{1,3},{2,6},{3,1},{4,0},{5,7},{6,2},{7,5},{8,12},{9,11},{10,... | collective-permute-start | bytes 1351688 | tf_op jit(solution)/shard_map/ppermute | solution.py:510
  25.6 14.3 %collective-permute-start.3 = (bf16[110,16,128]{2,1,0:T(8,128)(2,1)S(1)}, bf16[110,16,128]{2,1,0:T(8,128)(2,1)S(1)}, u32[]{:S(2)}, u32[]{:S(2)}) collective-permute-start(bf16[110,16,128]{2,1,0:T(8,128)(2,1)S(1)} %collective-permute-done.2.refs_0_.refs_1_.refs_3_.refs_2_), channel_id=1, source_target_pairs={{0,0},{8,16},{16,8},{24,24},{1,1},{9,17},{17,9},{25,25},{2,2},{10,... | collective-permute-start | bytes 1351688 | tf_op jit(solution)/shard_map/ppermute | solution.py:526
  26.3 13.6 %collective-permute-start.1 = (bf16[110,16,128]{2,1,0:T(8,128)(2,1)S(1)}, bf16[110,16,128]{2,1,0:T(8,128)(2,1)S(1)}, u32[]{:S(2)}, u32[]{:S(2)}) collective-permute-start(bf16[110,16,128]{2,1,0:T(8,128)(2,1)S(1)} %collective-permute-done.refs_2_.refs_1_), channel_id=1, source_target_pairs={{0,8},{8,0},{16,24},{24,16},{1,9},{9,1},{17,25},{25,17},{2,10},{10... | collective-permute-start | bytes 1351688 | tf_op jit(solution)/shard_map/ppermute | solution.py:526
  41.5 18.2 %collective-permute-start.9 = (bf16[4,110,16,128]{3,2,1,0:T(8,128)(2,1)}, bf16[4,110,16,128]{3,2,1,0:T(8,128)(2,1)S(1)}, u32[]{:S(2)}, u32[]{:S(2)}) collective-permute-start(bf16[4,110,16,128]{3,2,1,0:T(8,128)(2,1)} %get-tuple-element.78.rest_0_), channel_id=1, source_target_pairs={{0,1},{1,0},{2,3},{3,2},{4,5},{5,4},{6,7},{7,6},{8,9},{9,8},{10,11... | collective-permute-start | bytes 5406728 | tf_op jit(solution)/shard_map/ppermute | solution.py:510
  44.8 14.9 %collective-permute-start.12 = (bf16[110,16,128]{2,1,0:T(8,128)(2,1)S(1)}, bf16[110,16,128]{2,1,0:T(8,128)(2,1)S(1)}, u32[]{:S(2)}, u32[]{:S(2)}) collective-permute-start(bf16[110,16,128]{2,1,0:T(8,128)(2,1)S(1)} %get-tuple-element.80.refs_6_), channel_id=1, source_target_pairs={{0,4},{1,3},{2,6},{3,1},{4,0},{5,7},{6,2},{7,5},{8,12},{9,11},{10,... | collective-permute-start | bytes 1351688 | tf_op jit(solution)/shard_map/ppermute | solution.py:510
  45.3 14.4 %collective-permute-start.10 = (bf16[110,16,128]{2,1,0:T(8,128)(2,1)S(1)}, bf16[110,16,128]{2,1,0:T(8,128)(2,1)S(1)}, u32[]{:S(2)}, u32[]{:S(2)}) collective-permute-start(bf16[110,16,128]{2,1,0:T(8,128)(2,1)S(1)} %collective-permute-done.3.refs_2_.refs_1_), channel_id=1, source_target_pairs={{0,8},{8,0},{16,24},{24,16},{1,9},{9,1},{17,25},{25,17},{2,10},{10... | collective-permute-start | bytes 1351688 | tf_op jit(solution)/shard_map/ppermute | solution.py:526
  61.5 17.6 %collective-permute-start.14 = (bf16[4,110,16,128]{3,2,1,0:T(8,128)(2,1)}, bf16[4,110,16,128]{3,2,1,0:T(8,128)(2,1)S(1)}, u32[]{:S(2)}, u32[]{:S(2)}) collective-permute-start(bf16[4,110,16,128]{3,2,1,0:T(8,128)(2,1)} %get-tuple-element.81.rest_2_), channel_id=1, source_target_pairs={{0,1},{1,0},{2,3},{3,2},{4,5},{5,4},{6,7},{7,6},{8,9},{9,8},{10,11... | collective-permute-start | bytes 5406728 | tf_op jit(solution)/shard_map/ppermute | solution.py:510
  64.3 14.8 %collective-permute-start.17 = (bf16[110,16,128]{2,1,0:T(8,128)(2,1)S(1)}, bf16[110,16,128]{2,1,0:T(8,128)(2,1)S(1)}, u32[]{:S(2)}, u32[]{:S(2)}) collective-permute-start(bf16[110,16,128]{2,1,0:T(8,128)(2,1)S(1)} %get-tuple-element.82.refs_5_), channel_id=1, source_target_pairs={{0,4},{1,3},{2,6},{3,1},{4,0},{5,7},{6,2},{7,5},{8,12},{9,11},{10,... | collective-permute-start | bytes 1351688 | tf_op jit(solution)/shard_map/ppermute | solution.py:510
  81.8 15.4 %collective-permute-start.18 = (bf16[4,110,16,128]{3,2,1,0:T(8,128)(2,1)}, bf16[4,110,16,128]{3,2,1,0:T(8,128)(2,1)}, u32[]{:S(2)}, u32[]{:S(2)}) collective-permute-start(bf16[4,110,16,128]{3,2,1,0:T(8,128)(2,1)} %get-tuple-element.84.rest_4_), channel_id=1, source_target_pairs={{0,1},{1,0},{2,3},{3,2},{4,5},{5,4},{6,7},{7,6},{8,9},{9,8},{10,11... | collective-permute-start | bytes 5406728 | tf_op jit(solution)/shard_map/ppermute | solution.py:510
  92.3 42.3 %collective-permute-start.22 = (bf16[2,110,16,128]{3,2,1,0:T(8,128)(2,1)}, bf16[2,110,16,128]{3,2,1,0:T(8,128)(2,1)}, u32[]{:S(2)}, u32[]{:S(2)}) collective-permute-start(bf16[2,110,16,128]{3,2,1,0:T(8,128)(2,1)} %pad_maximum_fusion.rest_8_.rest_16_), channel_id=1, source_target_pairs={{0,2},{1,5},{2,0},{3,7},{4,6},{5,1},{6,4},{7,3},{8,10},{9,13},{10,... | collective-permute-start | bytes 2703368 | tf_op jit(solution)/shard_map/ppermute | solution.py:510
  93.6 41.1 %collective-permute-start.23 = (bf16[2,110,16,128]{3,2,1,0:T(8,128)(2,1)}, bf16[2,110,16,128]{3,2,1,0:T(8,128)(2,1)S(1)}, u32[]{:S(2)}, u32[]{:S(2)}) collective-permute-start(bf16[2,110,16,128]{3,2,1,0:T(8,128)(2,1)} %pad_maximum_fusion.rest_8_.rest_16_), channel_id=1, source_target_pairs={{0,4},{1,3},{2,6},{3,1},{4,0},{5,7},{6,2},{7,5},{8,12},{9,11},{10,... | collective-permute-start | bytes 2703368 | tf_op jit(solution)/shard_map/ppermute | solution.py:510
  94.9 40.0 %collective-permute-start.24 = (bf16[2,110,16,128]{3,2,1,0:T(8,128)(2,1)}, bf16[2,110,16,128]{3,2,1,0:T(8,128)(2,1)S(1)}, u32[]{:S(2)}, u32[]{:S(2)}) collective-permute-start(bf16[2,110,16,128]{3,2,1,0:T(8,128)(2,1)} %pad_maximum_fusion.rest_8_.rest_16_), channel_id=1, source_target_pairs={{0,6},{1,7},{2,4},{3,5},{4,2},{5,3},{6,0},{7,1},{8,14},{9,15},{10,... | collective-permute-start | bytes 2703368 | tf_op jit(solution)/shard_map/ppermute | solution.py:510
  95.9 46.6 %collective-permute-start.29 = (bf16[2,110,16,128]{3,2,1,0:T(8,128)(2,1)}, bf16[2,110,16,128]{3,2,1,0:T(8,128)(2,1)S(1)}, u32[]{:S(2)}, u32[]{:S(2)}) collective-permute-start(bf16[2,110,16,128]{3,2,1,0:T(8,128)(2,1)} %pad_maximum_fusion.rest_8_.rest_16_), channel_id=1, source_target_pairs={{0,1},{1,0},{2,3},{3,2},{4,5},{5,4},{6,7},{7,6},{8,9},{9,8},{10,11... | collective-permute-start | bytes 2703368 | tf_op jit(solution)/shard_map/ppermute | solution.py:510
  136.7 19.1 %collective-permute-start.27 = (bf16[2,144,16,128]{3,2,1,0:T(8,128)(2,1)S(1)}, bf16[2,144,16,128]{3,2,1,0:T(8,128)(2,1)S(1)}, u32[]{:S(2)}, u32[]{:S(2)}) collective-permute-start(bf16[2,144,16,128]{3,2,1,0:T(8,128)(2,1)S(1)} %copy-done.37), channel_id=1, source_target_pairs={{0,1},{1,0},{2,3},{3,2},{4,5},{5,4},{6,7},{7,6},{8,9},{9,8},{10,11... | collective-permute-start | bytes 3538952 | tf_op jit(solution)/shard_map/ppermute | solution.py:510
  140.6 16.3 %collective-permute-start.28 = (bf16[2,144,16,128]{3,2,1,0:T(8,128)(2,1)S(1)}, bf16[2,144,16,128]{3,2,1,0:T(8,128)(2,1)S(1)}, u32[]{:S(2)}, u32[]{:S(2)}) collective-permute-start(bf16[2,144,16,128]{3,2,1,0:T(8,128)(2,1)S(1)} %shard_map.220.rest_0_), channel_id=1, source_target_pairs={{0,4},{1,3},{2,6},{3,1},{4,0},{5,7},{6,2},{7,5},{8,12},{9,11},{10,... | collective-permute-start | bytes 3538952 | tf_op jit(solution)/shard_map/ppermute | solution.py:510
  142.0 13.3 %collective-permute-start.30 = (bf16[2,110,16,128]{3,2,1,0:T(8,128)(2,1)}, bf16[2,110,16,128]{3,2,1,0:T(8,128)(2,1)S(1)}, u32[]{:S(2)}, u32[]{:S(2)}) collective-permute-start(bf16[2,110,16,128]{3,2,1,0:T(8,128)(2,1)} %collective-permute-done.22.refs_1_.rest_9_.rest_17_), channel_id=1, source_target_pairs={{0,1},{1,0},{2,3},{3,2},{4,5},{5,4},{6,7},{7,6},{8,9},{9,8},{10,11... | collective-permute-start | bytes 2703368 | tf_op jit(solution)/shard_map/ppermute | solution.py:510
  142.0 13.8 %collective-permute-start.31 = (bf16[2,110,16,128]{3,2,1,0:T(8,128)(2,1)S(1)}, bf16[2,110,16,128]{3,2,1,0:T(8,128)(2,1)S(1)}, u32[]{:S(2)}, u32[]{:S(2)}) collective-permute-start(bf16[2,110,16,128]{3,2,1,0:T(8,128)(2,1)S(1)} %copy-done.5), channel_id=1, source_target_pairs={{0,1},{1,0},{2,3},{3,2},{4,5},{5,4},{6,7},{7,6},{8,9},{9,8},{10,11... | collective-permute-start | bytes 2703368 | tf_op jit(solution)/shard_map/ppermute | solution.py:510
  142.5 13.3 %collective-permute-start.32 = (bf16[2,110,16,128]{3,2,1,0:T(8,128)(2,1)S(1)}, bf16[2,110,16,128]{3,2,1,0:T(8,128)(2,1)S(1)}, u32[]{:S(2)}, u32[]{:S(2)}) collective-permute-start(bf16[2,110,16,128]{3,2,1,0:T(8,128)(2,1)S(1)} %copy-done.7), channel_id=1, source_target_pairs={{0,1},{1,0},{2,3},{3,2},{4,5},{5,4},{6,7},{7,6},{8,9},{9,8},{10,11... | collective-permute-start | bytes 2703368 | tf_op jit(solution)/shard_map/ppermute | solution.py:510
  159.6 32.5 %collective-permute-start.38 = (bf16[2,152,16,128]{3,2,1,0:T(8,128)(2,1)}, bf16[2,152,16,128]{3,2,1,0:T(8,128)(2,1)S(1)}, u32[]{:S(2)}, u32[]{:S(2)}) collective-permute-start(bf16[2,152,16,128]{3,2,1,0:T(8,128)(2,1)} %get-tuple-element.121), channel_id=1, source_target_pairs={{0,1},{1,0},{2,3},{3,2},{4,5},{5,4},{6,7},{7,6},{8,9},{9,8},{10,11... | collective-permute-start | bytes 3735560 | tf_op jit(solution)/shard_map/ppermute | solution.py:510
  162.5 29.6 %collective-permute-start.39 = (bf16[2,152,16,128]{3,2,1,0:T(8,128)(2,1)S(1)}, bf16[2,152,16,128]{3,2,1,0:T(8,128)(2,1)}, u32[]{:S(2)}, u32[]{:S(2)}) collective-permute-start(bf16[2,152,16,128]{3,2,1,0:T(8,128)(2,1)S(1)} %shard_map.224.rest_0_), channel_id=1, source_target_pairs={{0,4},{1,3},{2,6},{3,1},{4,0},{5,7},{6,2},{7,5},{8,12},{9,11},{10,... | collective-permute-start | bytes 3735560 | tf_op jit(solution)/shard_map/ppermute | solution.py:510
  174.5 15.0 %collective-permute-start.40 = (bf16[144,16,128]{2,1,0:T(8,128)(2,1)S(1)}, bf16[144,16,128]{2,1,0:T(8,128)(2,1)}, u32[]{:S(2)}, u32[]{:S(2)}) collective-permute-start(bf16[144,16,128]{2,1,0:T(8,128)(2,1)S(1)} %get-tuple-element.114.refs_1_), channel_id=1, source_target_pairs={{0,2},{1,5},{2,0},{3,7},{4,6},{5,1},{6,4},{7,3},{8,10},{9,13},{10,... | collective-permute-start | bytes 1769480 | tf_op jit(solution)/shard_map/ppermute | solution.py:510
  177.5 35.3 %collective-permute-start.43 = (bf16[2,144,16,128]{3,2,1,0:T(8,128)(2,1)}, bf16[2,144,16,128]{3,2,1,0:T(8,128)(2,1)}, u32[]{:S(2)}, u32[]{:S(2)}) collective-permute-start(bf16[2,144,16,128]{3,2,1,0:T(8,128)(2,1)} %get-tuple-element.129), channel_id=1, source_target_pairs={{0,1},{1,0},{2,3},{3,2},{4,5},{5,4},{6,7},{7,6},{8,9},{9,8},{10,11... | collective-permute-start | bytes 3538952 | tf_op jit(solution)/shard_map/ppermute | solution.py:510
  188.6 24.2 %collective-permute-start.46 = (bf16[2,144,16,128]{3,2,1,0:T(8,128)(2,1)}, bf16[2,144,16,128]{3,2,1,0:T(8,128)(2,1)}, u32[]{:S(2)}, u32[]{:S(2)}) collective-permute-start(bf16[2,144,16,128]{3,2,1,0:T(8,128)(2,1)} %shard_map.229), channel_id=1, source_target_pairs={{0,4},{1,3},{2,6},{3,1},{4,0},{5,7},{6,2},{7,5},{8,12},{9,11},{10,... | collective-permute-start | bytes 3538952 | tf_op jit(solution)/shard_map/ppermute | solution.py:510
  195.5 17.3 %collective-permute-start.47 = (bf16[110,16,128]{2,1,0:T(8,128)(2,1)S(1)}, bf16[110,16,128]{2,1,0:T(8,128)(2,1)S(1)}, u32[]{:S(2)}, u32[]{:S(2)}) collective-permute-start(bf16[110,16,128]{2,1,0:T(8,128)(2,1)S(1)} %get-tuple-element.123.refs_3_), channel_id=1, source_target_pairs={{0,8},{8,0},{16,24},{24,16},{1,9},{9,1},{17,25},{25,17},{2,10},{10... | collective-permute-start | bytes 1351688 | tf_op jit(solution)/shard_map/ppermute | solution.py:526
  220.4 31.8 %collective-permute-start.48 = (bf16[110,16,128]{2,1,0:T(8,128)(2,1)S(1)}, bf16[110,16,128]{2,1,0:T(8,128)(2,1)S(1)}, u32[]{:S(2)}, u32[]{:S(2)}) collective-permute-start(bf16[110,16,128]{2,1,0:T(8,128)(2,1)S(1)} %broadcast_select_fusion), channel_id=1, source_target_pairs={{0,8},{8,24},{16,0},{24,16},{1,9},{9,25},{17,1},{25,17},{2,10},{10... | collective-permute-start | bytes 1351688 | tf_op jit(solution)/shard_map/ppermute | solution.py:526
  221.0 15.6 %collective-permute-start.55 = (f32[14,768]{1,0:T(8,128)S(1)}, f32[14,768]{1,0:T(8,128)S(1)}, u32[]{:S(2)}, u32[]{:S(2)}) collective-permute-start(f32[14,768]{1,0:T(8,128)S(1)} %add.46.refs_2_), channel_id=1, source_target_pairs={{0,16},{8,24},{16,0},{24,8},{1,17},{9,25},{17,1},{25,9},{2,18},{10... | collective-permute-start | bytes 129032 | tf_op jit(solution)/shard_map/ppermute | solution.py:526
  226.0 26.1 %collective-permute-start.52 = (bf16[76,16,128]{2,1,0:T(8,128)(2,1)S(1)}, bf16[76,16,128]{2,1,0:T(8,128)(2,1)S(1)}, u32[]{:S(2)}, u32[]{:S(2)}) collective-permute-start(bf16[76,16,128]{2,1,0:T(8,128)(2,1)S(1)} %get-tuple-element.137), channel_id=1, source_target_pairs={{0,8},{8,0},{16,24},{24,16},{1,9},{9,1},{17,25},{25,17},{2,10},{10... | collective-permute-start | bytes 933896 | tf_op jit(solution)/shard_map/ppermute | solution.py:526
  226.7 25.5 %collective-permute-start.53 = (bf16[76,16,128]{2,1,0:T(8,128)(2,1)S(1)}, bf16[76,16,128]{2,1,0:T(8,128)(2,1)S(1)}, u32[]{:S(2)}, u32[]{:S(2)}) collective-permute-start(bf16[76,16,128]{2,1,0:T(8,128)(2,1)S(1)} %get-tuple-element.137), channel_id=1, source_target_pairs={{0,0},{8,16},{16,8},{24,24},{1,1},{9,17},{17,9},{25,25},{2,2},{10,... | collective-permute-start | bytes 933896 | tf_op jit(solution)/shard_map/ppermute | solution.py:526
  227.4 24.8 %collective-permute-start.54 = (bf16[76,16,128]{2,1,0:T(8,128)(2,1)S(1)}, bf16[76,16,128]{2,1,0:T(8,128)(2,1)S(1)}, u32[]{:S(2)}, u32[]{:S(2)}) collective-permute-start(bf16[76,16,128]{2,1,0:T(8,128)(2,1)S(1)} %get-tuple-element.136.h_stay), channel_id=1, source_target_pairs={{0,16},{8,0},{16,24},{24,8},{1,17},{9,1},{17,25},{25,9},{2,18},{10... | collective-permute-start | bytes 933896 | tf_op jit(solution)/shard_map/ppermute | solution.py:526
  236.6 15.6 %collective-permute-start.49 = (bf16[42,16,128]{2,1,0:T(8,128)(2,1)S(1)}, bf16[42,16,128]{2,1,0:T(8,128)(2,1)S(1)}, u32[]{:S(2)}, u32[]{:S(2)}) collective-permute-start(bf16[42,16,128]{2,1,0:T(8,128)(2,1)S(1)} %slice_select_fusion), channel_id=1, source_target_pairs={{0,16},{8,0},{16,24},{24,8},{1,17},{9,1},{17,25},{25,9},{2,18},{10... | collective-permute-start | bytes 516104 | tf_op jit(solution)/shard_map/ppermute | solution.py:526
  255.8 14.1 %collective-permute-start.57 = (bf16[110,16,128]{2,1,0:T(8,128)(2,1)S(1)}, bf16[110,16,128]{2,1,0:T(8,128)(2,1)S(1)}, u32[]{:S(2)}, u32[]{:S(2)}) collective-permute-start(bf16[110,16,128]{2,1,0:T(8,128)(2,1)S(1)} %get-tuple-element.139.rest_0_), channel_id=1, source_target_pairs={{0,4},{1,3},{2,6},{3,1},{4,0},{5,7},{6,2},{7,5},{8,12},{9,11},{10,... | collective-permute-start | bytes 1351688 | tf_op jit(solution)/shard_map/ppermute | solution.py:510
  (71 other events, 530.1 us)

commit v4 on v3

--- a/solution.py
+++ b/solution.py
@@ -606,7 +606,7 @@
 TURN = [(0, 2), (1, 0), (2, 3), (3, 1)]
 
 
-def gather_weights(narrow):
+def gather_weights(narrow, early):
     z = lax.axis_index("dp")
     e, o = along(narrow, EDGE), along(narrow, INNER)
     a0, b0 = near(narrow), far(narrow)
@@ -618,7 +618,7 @@
     a2, b2, c1 = near(t2), far(t2), far(a1)
     t3, a2, four1 = gate(z, [eoe, oe, e, eoe], [a2, [t1, a1, b1, c1]], (b2, d0))
     a3, b3, c2, d1 = near(t3), far(t3), far(a2), sibling(four1)
-    a3, four2, trio = gate(z, [], [a3, [t2, a2, b2, c2], [t3, a3, b3]], (d1,))
+    a3, four2, trio = gate(z, [], [a3, [t2, a2, b2, c2], [t3, a3, b3]], (d1, early))
     c3, d2, d3 = far(a3), sibling(four2), sibling(trio)
     last = sibling(c3)
     steps = chosen(z, [jnp.array(row, jnp.int32) for row in ((0, 1, 2, 3), (1, 0, 2, 3), (2, 1, 0, 3), (3, 2, 1, 0))])
@@ -694,7 +694,8 @@
         me = lax.axis_index("fsdp")
         core = lax.rem(me, 2)
         slots = slot_of(jnp.arange(GROUPS, dtype=jnp.int32) ^ me, core)
-        pieces, steps = gather_weights(narrow)
+        roots = jnp.stack([left_root.astype(BF), right_root.astype(BF)])
+        pieces, steps = gather_weights(narrow, roots)
     else:
         me = jnp.int32(0)
         core = jnp.int32(0)
@@ -761,8 +762,6 @@
         cut_h = 2 * PART - ATT
         rest_a, rest_h = ATT - PART, HID - cut_h
         ranges = jnp.stack([odd * cut_r, (1 - odd) * cut_r, odd * rest_a, (1 - odd) * rest_a, (1 - odd) * cut_h, odd * cut_h])
-        right, left = right_root.astype(BF), left_root.astype(BF)
-        roots = jnp.stack([left, right])
         roots = [roots, near(roots), far(roots), toward(roots, lambda i: i ^ 6)]
         r_rest, r_keep, send_rest, *send = r_ship
         r_pair = pair_sum(r_keep, [tie(send[0], roots[1:]), send[1]])
@@ -786,7 +785,7 @@
     local_vectors = jnp.concatenate([sums_a, sums_b], axis=0)
     local_norms = norms[:, 0]
     if staged:
-        weight_sums = jnp.sum(weights * weights, axis=(1, 2))
+        weight_sums = jnp.sum(jnp.square(lax.optimization_barrier(weights)), axis=(1, 2))
         packed = jnp.concatenate([local_norms, weight_sums, jnp.zeros((D - 2 - PART,), F32)])
         packed = jnp.concatenate([local_vectors, packed[None]], axis=0)
         packed = packed + sibling(packed)
@@ -815,13 +814,13 @@
     )
     if staged:
         packed = packed + toward(packed, lambda i: i ^ 2)
-        a_own, a_first = summed([*in_hbm([a_rest]), a_came, a_back], (r_leave, packed), split=True)
+        a_own, a_first = summed([*in_hbm([a_rest]), a_came, a_back], (r_leave,), split=True)
         a_last = near(a_first)
         h_rest, h_keep, send_rest, *send = h_ship
         h_pair = pair_sum(h_keep, send)
         h_back = far(h_pair)
         h_came = sibling(send_rest)
-        a_stay, a_leave = summed([a_own, a_last], (), [(2, PART), (3, PART)], ranges)
+        a_stay, a_leave = summed([a_own, a_last], (packed,), [(2, PART), (3, PART)], ranges)
         a_edge = along(a_leave, EDGE)
         packed = packed + toward(packed, lambda i: i ^ 4)
         weight_squares = packed[-1, 2 : 2 + PART]

time: 292 us -> 289 us (0.990)
  no operation moved by 1% of the time
where the time goes in v4:
time: 289 us; the launch traced here: 286 us
  waiting for transfers between devices  123 us (43%)
  Pallas kernels  95.7 us (33%)
  starting transfers between devices  55.3 us (19%)
  local copies, waits for them, and re-layouts  5.83 us (2%)
  other arithmetic  4.25 us (1%)
    ppermute x49, waiting for transfers between devices, toward(): return lax.ppermute(x, 'fsdp', [(i, move(i)) for i in range(GROUPS)])  92.7 us
    pallas_call x15, Pallas kernels, call(): pl.pallas_call(kernel, out_shape=outs, in_specs=in_specs + [ANY] * len(de...  78.2 us
    ppermute x49, starting transfers between devices, toward(): return lax.ppermute(x, 'fsdp', [(i, move(i)) for i in range(GROUPS)])  34.4 us
    ppermute x14, waiting for transfers between devices, along(): return lax.ppermute(x, 'dp', pairs)  30.2 us
    ppermute x14, starting transfers between devices, along(): return lax.ppermute(x, 'dp', pairs)  20.9 us
    pallas_call x1, Pallas kernels, local(): pl.pallas_call(step_kernel, grid=(PART // BATCH,), out_shape=[rows, rows,...  11 us
    pallas_call x4, Pallas kernels, gate(): pl.pallas_call(kernel, out_shape=outs, in_specs=[SM] + [ANY] * (count + l...  6.55 us
  transfers between devices with their start and end apart: 63, of which 29 were waited for; matrix products, arithmetic and copies ran while one was open for 1% of the time, Pallas kernels for 27%

profile of v4, /device:TPU:0, one launch (start us, length us, event | category | flops | bytes accessed | tf_op | source)
XLA Modules:
  0.0 286.2 jit_solution(6564397994938088755)
XLA Ops:
  2.6 5.9 %collective-permute-start.2 = (bf16[110,16,128]{2,1,0:T(8,128)(2,1)S(1)}, bf16[110,16,128]{2,1,0:T(8,128)(2,1)S(1)}, u32[]{:S(2)}, u32[]{:S(2)}) collective-permute-start(bf16[110,16,128]{2,1,0:T(8,128)(2,1)S(1)} %convert_element_type.9.refs_5_), channel_id=1, source_target_pairs={{0,8},{8,0},{16,24},{24,16},{1,9},{9,1},{17,25},{25,17},{2,10},{10... | collective-permute-start | bytes 1351688 | tf_op jit(solution)/shard_map/ppermute | solution.py:526
  11.5 7.0 %collective-permute-done.2.refs_0_.refs_1_.refs_3_.refs_2_ = bf16[110,16,128]{2,1,0:T(8,128)(2,1)S(1)} collective-permute-done((bf16[110,16,128]{2,1,0:T(8,128)(2,1)S(1)}, bf16[110,16,128]{2,1,0:T(8,128)(2,1)S(1)}, u32[]{:S(2)}, u32[]{:S(2)}) %collective-permute-start.2) | collective-permute-done | bytes 450592 | tf_op jit(solution)/shard_map/ppermute | solution.py:526
  18.5 2.7 collective-permute-done.5.refs_5_.refs_7_
  25.1 2.1 collective-permute-start.1
  27.2 6.7 %collective-permute-done.8.refs_9_.refs_7_ = bf16[110,16,128]{2,1,0:T(8,128)(2,1)S(1)} collective-permute-done((bf16[110,16,128]{2,1,0:T(8,128)(2,1)S(1)}, bf16[110,16,128]{2,1,0:T(8,128)(2,1)S(1)}, u32[]{:S(2)}, u32[]{:S(2)}) %collective-permute-start.8) | collective-permute-done | bytes 450592 | tf_op jit(solution)/shard_map/ppermute | solution.py:510
  33.9 2.8 collective-permute-done.6.refs_4_
  36.6 2.1 collective-permute-done.7.refs_8_
  44.6 8.3 %collective-permute-done.13.refs_9_.refs_3_ = bf16[110,16,128]{2,1,0:T(8,128)(2,1)S(1)} collective-permute-done((bf16[110,16,128]{2,1,0:T(8,128)(2,1)S(1)}, bf16[110,16,128]{2,1,0:T(8,128)(2,1)S(1)}, u32[]{:S(2)}, u32[]{:S(2)}) %collective-permute-start.13) | collective-permute-done | bytes 450592 | tf_op jit(solution)/shard_map/ppermute | solution.py:510
  52.8 2.4 collective-permute-done.11.refs_4_
  55.2 3.2 %collective-permute-done.12.refs_8_ = bf16[110,16,128]{2,1,0:T(8,128)(2,1)S(1)} collective-permute-done((bf16[110,16,128]{2,1,0:T(8,128)(2,1)S(1)}, bf16[110,16,128]{2,1,0:T(8,128)(2,1)S(1)}, u32[]{:S(2)}, u32[]{:S(2)}) %collective-permute-start.12) | collective-permute-done | bytes 450592 | tf_op jit(solution)/shard_map/ppermute | solution.py:510
  63.9 9.1 %collective-permute-done.15.refs_0_.refs_6_ = bf16[110,16,128]{2,1,0:T(8,128)(2,1)S(1)} collective-permute-done((bf16[110,16,128]{2,1,0:T(8,128)(2,1)S(1)}, bf16[110,16,128]{2,1,0:T(8,128)(2,1)S(1)}, u32[]{:S(2)}, u32[]{:S(2)}) %collective-permute-start.15) | collective-permute-done | bytes 450592 | tf_op jit(solution)/shard_map/ppermute | solution.py:510
  73.1 4.8 %collective-permute-done.17.refs_7_ = bf16[110,16,128]{2,1,0:T(8,128)(2,1)S(1)} collective-permute-done((bf16[110,16,128]{2,1,0:T(8,128)(2,1)S(1)}, bf16[110,16,128]{2,1,0:T(8,128)(2,1)S(1)}, u32[]{:S(2)}, u32[]{:S(2)}) %collective-permute-start.17) | collective-permute-done | bytes 450592 | tf_op jit(solution)/shard_map/ppermute | solution.py:510
  77.9 2.6 shard_map.217
  82.3 7.1 %collective-permute-done.19.rest_7_ = bf16[110,16,128]{2,1,0:T(8,128)(2,1)S(1)} collective-permute-done((bf16[110,16,128]{2,1,0:T(8,128)(2,1)S(1)}, bf16[110,16,128]{2,1,0:T(8,128)(2,1)S(1)}, u32[]{:S(2)}, u32[]{:S(2)}) %collective-permute-start.19) | collective-permute-done | bytes 450592 | tf_op jit(solution)/shard_map/ppermute | solution.py:510
  94.6 37.2 %shard_map.218 = (bf16[768,768]{1,0:T(8,128)(2,1)}, bf16[768,768]{1,0:T(8,128)(2,1)}, bf16[768,768]{1,0:T(8,128)(2,1)}, bf16[512,256]{1,0:T(8,128)(2,1)}, bf16[5...) custom-call(s32[15]{0:T(128)} %concatenate.9.sc, ...), custom_call_target="tpu_custom_call" | custom-call | flops 1 | bytes 1 | tf_op jit(solution)/shard_map/pallas_call | solution.py:490
  139.1 12.7 %shard_map.221 = (bf16[512,768]{1,0:T(8,128)(2,1)S(1)}, bf16[512,768]{1,0:T(8,128)(2,1)S(1)}, bf16[512,768]{1,0:T(8,128)(2,1)S(1)}, f32[3,768]{1,0:T(4,128)S(1)}...) custom-call(s32[15]{0:T(128)S(1)} %copy-done.17, ...), custom_call_target="tpu_custom_call" | custom-call | flops 1 | bytes 1 | tf_op jit(solution)/shard_map/pallas_call | solution.py:490
  162.0 9.8 %shard_map.225 = (bf16[512,768]{1,0:T(8,128)(2,1)}, bf16[2,144,16,128]{3,2,1,0:T(8,128)(2,1)}, bf16[2,144,16,128]{3,2,1,0:T(8,128)(2,1)}, bf16[2,144,16,128]{3,2...) custom-call(s32[15]{0:T(128)S(1)} %copy-done.17, ...), custom_call_target="tpu_custom_call" | custom-call | flops 1 | bytes 1 | tf_op jit(solution)/shard_map/pallas_call | solution.py:490
  174.9 2.6 shard_map.229
  178.6 7.7 %collective-permute-done.40.refs_1_ = bf16[144,16,128]{2,1,0:T(8,128)(2,1)} collective-permute-done((bf16[144,16,128]{2,1,0:T(8,128)(2,1)S(1)}, bf16[144,16,128]{2,1,0:T(8,128)(2,1)}, u32[]{:S(2)}, u32[]{:S(2)}) %collective-permute-start.40) | collective-permute-done | bytes 589856 | tf_op jit(solution)/shard_map/ppermute | solution.py:510
  188.8 2.1 shard_map.227
  193.5 10.2 %collective-permute-done.36 = f32[14,768]{1,0:T(8,128)S(1)} collective-permute-done((f32[14,768]{1,0:T(8,128)S(1)}, f32[14,768]{1,0:T(8,128)S(1)}, u32[]{:S(2)}, u32[]{:S(2)}) %collective-permute-start.36) | collective-permute-done | bytes 43040 | tf_op jit(solution)/shard_map/ppermute | solution.py:510
  207.0 3.0 %collective-permute-done.37 = f32[14,768]{1,0:T(8,128)S(1)} collective-permute-done((f32[14,768]{1,0:T(8,128)S(1)}, f32[14,768]{1,0:T(8,128)S(1)}, u32[]{:S(2)}, u32[]{:S(2)}) %collective-permute-start.37) | collective-permute-done | bytes 43040 | tf_op jit(solution)/shard_map/ppermute | solution.py:510
  210.1 2.4 shard_map.230
  215.1 3.0 %collective-permute-done.42.refs_1_ = bf16[110,16,128]{2,1,0:T(8,128)(2,1)} collective-permute-done((bf16[110,16,128]{2,1,0:T(8,128)(2,1)S(1)}, bf16[110,16,128]{2,1,0:T(8,128)(2,1)}, u32[]{:S(2)}, u32[]{:S(2)}) %collective-permute-start.42) | collective-permute-done | bytes 450592 | tf_op jit(solution)/shard_map/ppermute | solution.py:526
  220.0 2.4 collective-permute-start.55
  225.5 3.3 %collective-permute-start.54 = (bf16[76,16,128]{2,1,0:T(8,128)(2,1)S(1)}, bf16[76,16,128]{2,1,0:T(8,128)(2,1)S(1)}, u32[]{:S(2)}, u32[]{:S(2)}) collective-permute-start(bf16[76,16,128]{2,1,0:T(8,128)(2,1)S(1)} %get-tuple-element.136.h_stay), channel_id=1, source_target_pairs={{0,16},{8,0},{16,24},{24,8},{1,17},{9,1},{17,25},{25,9},{2,18},{10... | collective-permute-start | bytes 933896 | tf_op jit(solution)/shard_map/ppermute | solution.py:526
  228.9 6.9 %collective-permute-done.55 = f32[14,768]{1,0:T(8,128)S(1)} collective-permute-done((f32[14,768]{1,0:T(8,128)S(1)}, f32[14,768]{1,0:T(8,128)S(1)}, u32[]{:S(2)}, u32[]{:S(2)}) %collective-permute-start.55) | collective-permute-done | bytes 43040 | tf_op jit(solution)/shard_map/ppermute | solution.py:526
  235.9 13.1 %collective-permute-done.49.slim_x = bf16[42,16,128]{2,1,0:T(8,128)(2,1)S(1)} collective-permute-done((bf16[42,16,128]{2,1,0:T(8,128)(2,1)S(1)}, bf16[42,16,128]{2,1,0:T(8,128)(2,1)S(1)}, u32[]{:S(2)}, u32[]{:S(2)}) %collective-permute-start.49) | collective-permute-done | bytes 172064 | tf_op jit(solution)/shard_map/ppermute | solution.py:526
  249.1 2.0 shard_map.234
  253.8 10.2 %collective-permute-done.56.rest_1_ = bf16[110,16,128]{2,1,0:T(8,128)(2,1)S(1)} collective-permute-done((bf16[110,16,128]{2,1,0:T(8,128)(2,1)S(1)}, bf16[110,16,128]{2,1,0:T(8,128)(2,1)S(1)}, u32[]{:S(2)}, u32[]{:S(2)}) %collective-permute-start.56) | collective-permute-done | bytes 450592 | tf_op jit(solution)/shard_map/ppermute | solution.py:510
  266.4 5.9 %collective-permute-done.58.rest_3_ = bf16[110,16,128]{2,1,0:T(8,128)(2,1)S(1)} collective-permute-done((bf16[110,16,128]{2,1,0:T(8,128)(2,1)S(1)}, bf16[110,16,128]{2,1,0:T(8,128)(2,1)S(1)}, u32[]{:S(2)}, u32[]{:S(2)}) %collective-permute-start.58) | collective-permute-done | bytes 450592 | tf_op jit(solution)/shard_map/ppermute | solution.py:510
  275.0 11.0 %shard_map.235 = (f32[110,16,128]{2,1,0:T(8,128)}, f32[110,16,128]{2,1,0:T(8,128)}, f32[110,16,128]{2,1,0:T(8,128)}) custom-call(s32[15]{0:T(128)S(1)} %copy-done.17, f32[220]{0:T(256)S(1)} %reshape.42.dec, f32[110]{0:T(128)S(1)} %fusion.4.size, f32[110,16,128]{2,1,0:T(8,128)} %get-tuple-element.70.own, f32[110,16,128]{2,1,0:T(8,128)} %lroot.1, ...), custom_call_target="tpu_custom_call" | custom-call | flops 1 | bytes 1 | tf_op jit(solution)/shard_map/pallas_call | solution.py:852
  (228 shorter events, 71.6 us)
Async XLA Ops:
  2.6 15.9 %collective-permute-start.2 = (bf16[110,16,128]{2,1,0:T(8,128)(2,1)S(1)}, bf16[110,16,128]{2,1,0:T(8,128)(2,1)S(1)}, u32[]{:S(2)}, u32[]{:S(2)}) collective-permute-start(bf16[110,16,128]{2,1,0:T(8,128)(2,1)S(1)} %convert_element_type.9.refs_5_), channel_id=1, source_target_pairs={{0,8},{8,0},{16,24},{24,16},{1,9},{9,1},{17,25},{25,17},{2,10},{10... | collective-permute-start | bytes 1351688 | tf_op jit(solution)/shard_map/ppermute | solution.py:526
  23.9 14.8 %collective-permute-start.7 = (bf16[110,16,128]{2,1,0:T(8,128)(2,1)S(1)}, bf16[110,16,128]{2,1,0:T(8,128)(2,1)S(1)}, u32[]{:S(2)}, u32[]{:S(2)}) collective-permute-start(bf16[110,16,128]{2,1,0:T(8,128)(2,1)S(1)} %get-tuple-element.77.refs_6_), channel_id=1, source_target_pairs={{0,4},{1,3},{2,6},{3,1},{4,0},{5,7},{6,2},{7,5},{8,12},{9,11},{10,... | collective-permute-start | bytes 1351688 | tf_op jit(solution)/shard_map/ppermute | solution.py:510
  24.4 14.3 %collective-permute-start.3 = (bf16[110,16,128]{2,1,0:T(8,128)(2,1)S(1)}, bf16[110,16,128]{2,1,0:T(8,128)(2,1)S(1)}, u32[]{:S(2)}, u32[]{:S(2)}) collective-permute-start(bf16[110,16,128]{2,1,0:T(8,128)(2,1)S(1)} %collective-permute-done.2.refs_0_.refs_1_.refs_3_.refs_2_), channel_id=1, source_target_pairs={{0,0},{8,16},{16,8},{24,24},{1,1},{9,17},{17,9},{25,25},{2,2},{10,... | collective-permute-start | bytes 1351688 | tf_op jit(solution)/shard_map/ppermute | solution.py:526
  25.1 13.6 %collective-permute-start.1 = (bf16[110,16,128]{2,1,0:T(8,128)(2,1)S(1)}, bf16[110,16,128]{2,1,0:T(8,128)(2,1)S(1)}, u32[]{:S(2)}, u32[]{:S(2)}) collective-permute-start(bf16[110,16,128]{2,1,0:T(8,128)(2,1)S(1)} %collective-permute-done.refs_2_.refs_1_), channel_id=1, source_target_pairs={{0,8},{8,0},{16,24},{24,16},{1,9},{9,1},{17,25},{25,17},{2,10},{10... | collective-permute-start | bytes 1351688 | tf_op jit(solution)/shard_map/ppermute | solution.py:526
  40.3 18.2 %collective-permute-start.9 = (bf16[4,110,16,128]{3,2,1,0:T(8,128)(2,1)}, bf16[4,110,16,128]{3,2,1,0:T(8,128)(2,1)S(1)}, u32[]{:S(2)}, u32[]{:S(2)}) collective-permute-start(bf16[4,110,16,128]{3,2,1,0:T(8,128)(2,1)} %get-tuple-element.78.rest_0_), channel_id=1, source_target_pairs={{0,1},{1,0},{2,3},{3,2},{4,5},{5,4},{6,7},{7,6},{8,9},{9,8},{10,11... | collective-permute-start | bytes 5406728 | tf_op jit(solution)/shard_map/ppermute | solution.py:510
  42.0 13.3 %collective-permute-start.11 = (bf16[110,16,128]{2,1,0:T(8,128)(2,1)S(1)}, bf16[110,16,128]{2,1,0:T(8,128)(2,1)S(1)}, u32[]{:S(2)}, u32[]{:S(2)}) collective-permute-start(bf16[110,16,128]{2,1,0:T(8,128)(2,1)S(1)} %get-tuple-element.79.refs_1_), channel_id=1, source_target_pairs={{0,2},{1,5},{2,0},{3,7},{4,6},{5,1},{6,4},{7,3},{8,10},{9,13},{10,... | collective-permute-start | bytes 1351688 | tf_op jit(solution)/shard_map/ppermute | solution.py:510
  43.6 14.9 %collective-permute-start.12 = (bf16[110,16,128]{2,1,0:T(8,128)(2,1)S(1)}, bf16[110,16,128]{2,1,0:T(8,128)(2,1)S(1)}, u32[]{:S(2)}, u32[]{:S(2)}) collective-permute-start(bf16[110,16,128]{2,1,0:T(8,128)(2,1)S(1)} %get-tuple-element.80.refs_6_), channel_id=1, source_target_pairs={{0,4},{1,3},{2,6},{3,1},{4,0},{5,7},{6,2},{7,5},{8,12},{9,11},{10,... | collective-permute-start | bytes 1351688 | tf_op jit(solution)/shard_map/ppermute | solution.py:510
  44.1 14.4 %collective-permute-start.10 = (bf16[110,16,128]{2,1,0:T(8,128)(2,1)S(1)}, bf16[110,16,128]{2,1,0:T(8,128)(2,1)S(1)}, u32[]{:S(2)}, u32[]{:S(2)}) collective-permute-start(bf16[110,16,128]{2,1,0:T(8,128)(2,1)S(1)} %collective-permute-done.3.refs_2_.refs_1_), channel_id=1, source_target_pairs={{0,8},{8,0},{16,24},{24,16},{1,9},{9,1},{17,25},{25,17},{2,10},{10... | collective-permute-start | bytes 1351688 | tf_op jit(solution)/shard_map/ppermute | solution.py:526
  60.3 17.6 %collective-permute-start.14 = (bf16[4,110,16,128]{3,2,1,0:T(8,128)(2,1)}, bf16[4,110,16,128]{3,2,1,0:T(8,128)(2,1)S(1)}, u32[]{:S(2)}, u32[]{:S(2)}) collective-permute-start(bf16[4,110,16,128]{3,2,1,0:T(8,128)(2,1)} %get-tuple-element.81.rest_2_), channel_id=1, source_target_pairs={{0,1},{1,0},{2,3},{3,2},{4,5},{5,4},{6,7},{7,6},{8,9},{9,8},{10,11... | collective-permute-start | bytes 5406728 | tf_op jit(solution)/shard_map/ppermute | solution.py:510
  63.1 14.8 %collective-permute-start.17 = (bf16[110,16,128]{2,1,0:T(8,128)(2,1)S(1)}, bf16[110,16,128]{2,1,0:T(8,128)(2,1)S(1)}, u32[]{:S(2)}, u32[]{:S(2)}) collective-permute-start(bf16[110,16,128]{2,1,0:T(8,128)(2,1)S(1)} %get-tuple-element.82.refs_5_), channel_id=1, source_target_pairs={{0,4},{1,3},{2,6},{3,1},{4,0},{5,7},{6,2},{7,5},{8,12},{9,11},{10,... | collective-permute-start | bytes 1351688 | tf_op jit(solution)/shard_map/ppermute | solution.py:510
  80.6 14.0 %collective-permute-start.18 = (bf16[4,110,16,128]{3,2,1,0:T(8,128)(2,1)}, bf16[4,110,16,128]{3,2,1,0:T(8,128)(2,1)}, u32[]{:S(2)}, u32[]{:S(2)}) collective-permute-start(bf16[4,110,16,128]{3,2,1,0:T(8,128)(2,1)} %get-tuple-element.84.rest_4_), channel_id=1, source_target_pairs={{0,1},{1,0},{2,3},{3,2},{4,5},{5,4},{6,7},{7,6},{8,9},{9,8},{10,11... | collective-permute-start | bytes 5406728 | tf_op jit(solution)/shard_map/ppermute | solution.py:510
  89.4 42.4 %collective-permute-start.22 = (bf16[2,110,16,128]{3,2,1,0:T(8,128)(2,1)S(1)}, bf16[2,110,16,128]{3,2,1,0:T(8,128)(2,1)S(1)}, u32[]{:S(2)}, u32[]{:S(2)}) collective-permute-start(bf16[2,110,16,128]{3,2,1,0:T(8,128)(2,1)S(1)} %pad_maximum_fusion.refs_9_.rest_8_.rest_16_), channel_id=1, source_target_pairs={{0,2},{1,5},{2,0},{3,7},{4,6},{5,1},{6,4},{7,3},{8,10},{9,13},{10,... | collective-permute-start | bytes 2703368 | tf_op jit(solution)/shard_map/ppermute | solution.py:510
  90.6 41.2 %collective-permute-start.23 = (bf16[2,110,16,128]{3,2,1,0:T(8,128)(2,1)S(1)}, bf16[2,110,16,128]{3,2,1,0:T(8,128)(2,1)}, u32[]{:S(2)}, u32[]{:S(2)}) collective-permute-start(bf16[2,110,16,128]{3,2,1,0:T(8,128)(2,1)S(1)} %pad_maximum_fusion.refs_9_.rest_8_.rest_16_), channel_id=1, source_target_pairs={{0,4},{1,3},{2,6},{3,1},{4,0},{5,7},{6,2},{7,5},{8,12},{9,11},{10,... | collective-permute-start | bytes 2703368 | tf_op jit(solution)/shard_map/ppermute | solution.py:510
  91.9 40.5 %collective-permute-start.24 = (bf16[2,110,16,128]{3,2,1,0:T(8,128)(2,1)S(1)}, bf16[2,110,16,128]{3,2,1,0:T(8,128)(2,1)}, u32[]{:S(2)}, u32[]{:S(2)}) collective-permute-start(bf16[2,110,16,128]{3,2,1,0:T(8,128)(2,1)S(1)} %pad_maximum_fusion.refs_9_.rest_8_.rest_16_), channel_id=1, source_target_pairs={{0,6},{1,7},{2,4},{3,5},{4,2},{5,3},{6,0},{7,1},{8,14},{9,15},{10,... | collective-permute-start | bytes 2703368 | tf_op jit(solution)/shard_map/ppermute | solution.py:510
  93.2 45.9 %collective-permute-start.29 = (bf16[2,110,16,128]{3,2,1,0:T(8,128)(2,1)S(1)}, bf16[2,110,16,128]{3,2,1,0:T(8,128)(2,1)S(1)}, u32[]{:S(2)}, u32[]{:S(2)}) collective-permute-start(bf16[2,110,16,128]{3,2,1,0:T(8,128)(2,1)S(1)} %pad_maximum_fusion.refs_9_.rest_8_.rest_16_), channel_id=1, source_target_pairs={{0,1},{1,0},{2,3},{3,2},{4,5},{5,4},{6,7},{7,6},{8,9},{9,8},{10,11... | collective-permute-start | bytes 2703368 | tf_op jit(solution)/shard_map/ppermute | solution.py:510
  133.9 18.5 %collective-permute-start.27 = (bf16[2,144,16,128]{3,2,1,0:T(8,128)(2,1)S(1)}, bf16[2,144,16,128]{3,2,1,0:T(8,128)(2,1)S(1)}, u32[]{:S(2)}, u32[]{:S(2)}) collective-permute-start(bf16[2,144,16,128]{3,2,1,0:T(8,128)(2,1)S(1)} %copy-done.38), channel_id=1, source_target_pairs={{0,1},{1,0},{2,3},{3,2},{4,5},{5,4},{6,7},{7,6},{8,9},{9,8},{10,11... | collective-permute-start | bytes 3538952 | tf_op jit(solution)/shard_map/ppermute | solution.py:510
  137.4 16.3 %collective-permute-start.28 = (bf16[2,144,16,128]{3,2,1,0:T(8,128)(2,1)S(1)}, bf16[2,144,16,128]{3,2,1,0:T(8,128)(2,1)S(1)}, u32[]{:S(2)}, u32[]{:S(2)}) collective-permute-start(bf16[2,144,16,128]{3,2,1,0:T(8,128)(2,1)S(1)} %shard_map.220.rest_0_), channel_id=1, source_target_pairs={{0,4},{1,3},{2,6},{3,1},{4,0},{5,7},{6,2},{7,5},{8,12},{9,11},{10,... | collective-permute-start | bytes 3538952 | tf_op jit(solution)/shard_map/ppermute | solution.py:510
  138.5 13.3 %collective-permute-start.30 = (bf16[2,110,16,128]{3,2,1,0:T(8,128)(2,1)S(1)}, bf16[2,110,16,128]{3,2,1,0:T(8,128)(2,1)S(1)}, u32[]{:S(2)}, u32[]{:S(2)}) collective-permute-start(bf16[2,110,16,128]{3,2,1,0:T(8,128)(2,1)S(1)} %copy-done.6), channel_id=1, source_target_pairs={{0,1},{1,0},{2,3},{3,2},{4,5},{5,4},{6,7},{7,6},{8,9},{9,8},{10,11... | collective-permute-start | bytes 2703368 | tf_op jit(solution)/shard_map/ppermute | solution.py:510
  138.6 13.8 %collective-permute-start.31 = (bf16[2,110,16,128]{3,2,1,0:T(8,128)(2,1)}, bf16[2,110,16,128]{3,2,1,0:T(8,128)(2,1)S(1)}, u32[]{:S(2)}, u32[]{:S(2)}) collective-permute-start(bf16[2,110,16,128]{3,2,1,0:T(8,128)(2,1)} %collective-permute-done.23.refs_2_.rest_10_.rest_18_), channel_id=1, source_target_pairs={{0,1},{1,0},{2,3},{3,2},{4,5},{5,4},{6,7},{7,6},{8,9},{9,8},{10,11... | collective-permute-start | bytes 2703368 | tf_op jit(solution)/shard_map/ppermute | solution.py:510
  139.1 13.3 %collective-permute-start.32 = (bf16[2,110,16,128]{3,2,1,0:T(8,128)(2,1)}, bf16[2,110,16,128]{3,2,1,0:T(8,128)(2,1)S(1)}, u32[]{:S(2)}, u32[]{:S(2)}) collective-permute-start(bf16[2,110,16,128]{3,2,1,0:T(8,128)(2,1)} %collective-permute-done.24.refs_3_.rest_11_.rest_19_), channel_id=1, source_target_pairs={{0,1},{1,0},{2,3},{3,2},{4,5},{5,4},{6,7},{7,6},{8,9},{9,8},{10,11... | collective-permute-start | bytes 2703368 | tf_op jit(solution)/shard_map/ppermute | solution.py:510
  158.0 30.7 %collective-permute-start.38 = (bf16[2,152,16,128]{3,2,1,0:T(8,128)(2,1)}, bf16[2,152,16,128]{3,2,1,0:T(8,128)(2,1)S(1)}, u32[]{:S(2)}, u32[]{:S(2)}) collective-permute-start(bf16[2,152,16,128]{3,2,1,0:T(8,128)(2,1)} %get-tuple-element.121), channel_id=1, source_target_pairs={{0,1},{1,0},{2,3},{3,2},{4,5},{5,4},{6,7},{7,6},{8,9},{9,8},{10,11... | collective-permute-start | bytes 3735560 | tf_op jit(solution)/shard_map/ppermute | solution.py:510
  160.9 27.9 %collective-permute-start.39 = (bf16[2,152,16,128]{3,2,1,0:T(8,128)(2,1)S(1)}, bf16[2,152,16,128]{3,2,1,0:T(8,128)(2,1)}, u32[]{:S(2)}, u32[]{:S(2)}) collective-permute-start(bf16[2,152,16,128]{3,2,1,0:T(8,128)(2,1)S(1)} %shard_map.224.rest_0_), channel_id=1, source_target_pairs={{0,4},{1,3},{2,6},{3,1},{4,0},{5,7},{6,2},{7,5},{8,12},{9,11},{10,... | collective-permute-start | bytes 3735560 | tf_op jit(solution)/shard_map/ppermute | solution.py:510
  172.4 13.9 %collective-permute-start.40 = (bf16[144,16,128]{2,1,0:T(8,128)(2,1)S(1)}, bf16[144,16,128]{2,1,0:T(8,128)(2,1)}, u32[]{:S(2)}, u32[]{:S(2)}) collective-permute-start(bf16[144,16,128]{2,1,0:T(8,128)(2,1)S(1)} %get-tuple-element.114.refs_1_), channel_id=1, source_target_pairs={{0,2},{1,5},{2,0},{3,7},{4,6},{5,1},{6,4},{7,3},{8,10},{9,13},{10,... | collective-permute-start | bytes 1769480 | tf_op jit(solution)/shard_map/ppermute | solution.py:510
  174.1 36.0 %collective-permute-start.43 = (bf16[2,144,16,128]{3,2,1,0:T(8,128)(2,1)}, bf16[2,144,16,128]{3,2,1,0:T(8,128)(2,1)}, u32[]{:S(2)}, u32[]{:S(2)}) collective-permute-start(bf16[2,144,16,128]{3,2,1,0:T(8,128)(2,1)} %get-tuple-element.129), channel_id=1, source_target_pairs={{0,1},{1,0},{2,3},{3,2},{4,5},{5,4},{6,7},{7,6},{8,9},{9,8},{10,11... | collective-permute-start | bytes 3538952 | tf_op jit(solution)/shard_map/ppermute | solution.py:510
  177.5 32.6 %collective-permute-start.46 = (bf16[2,144,16,128]{3,2,1,0:T(8,128)(2,1)}, bf16[2,144,16,128]{3,2,1,0:T(8,128)(2,1)}, u32[]{:S(2)}, u32[]{:S(2)}) collective-permute-start(bf16[2,144,16,128]{3,2,1,0:T(8,128)(2,1)} %shard_map.229), channel_id=1, source_target_pairs={{0,4},{1,3},{2,6},{3,1},{4,0},{5,7},{6,2},{7,5},{8,12},{9,11},{10,... | collective-permute-start | bytes 3538952 | tf_op jit(solution)/shard_map/ppermute | solution.py:510
  191.7 18.4 %collective-permute-start.47 = (bf16[110,16,128]{2,1,0:T(8,128)(2,1)S(1)}, bf16[110,16,128]{2,1,0:T(8,128)(2,1)S(1)}, u32[]{:S(2)}, u32[]{:S(2)}) collective-permute-start(bf16[110,16,128]{2,1,0:T(8,128)(2,1)S(1)} %get-tuple-element.123.refs_3_), channel_id=1, source_target_pairs={{0,8},{8,0},{16,24},{24,16},{1,9},{9,1},{17,25},{25,17},{2,10},{10... | collective-permute-start | bytes 1351688 | tf_op jit(solution)/shard_map/ppermute | solution.py:526
  219.3 29.7 %collective-permute-start.48 = (bf16[110,16,128]{2,1,0:T(8,128)(2,1)S(1)}, bf16[110,16,128]{2,1,0:T(8,128)(2,1)S(1)}, u32[]{:S(2)}, u32[]{:S(2)}) collective-permute-start(bf16[110,16,128]{2,1,0:T(8,128)(2,1)S(1)} %broadcast_select_fusion), channel_id=1, source_target_pairs={{0,8},{8,24},{16,0},{24,16},{1,9},{9,25},{17,1},{25,17},{2,10},{10... | collective-permute-start | bytes 1351688 | tf_op jit(solution)/shard_map/ppermute | solution.py:526
  220.0 15.8 %collective-permute-start.55 = (f32[14,768]{1,0:T(8,128)S(1)}, f32[14,768]{1,0:T(8,128)S(1)}, u32[]{:S(2)}, u32[]{:S(2)}) collective-permute-start(f32[14,768]{1,0:T(8,128)S(1)} %add.46.refs_2_), channel_id=1, source_target_pairs={{0,16},{8,24},{16,0},{24,8},{1,17},{9,25},{17,1},{25,9},{2,18},{10... | collective-permute-start | bytes 129032 | tf_op jit(solution)/shard_map/ppermute | solution.py:526
  223.3 25.7 %collective-permute-start.52 = (bf16[76,16,128]{2,1,0:T(8,128)(2,1)S(1)}, bf16[76,16,128]{2,1,0:T(8,128)(2,1)S(1)}, u32[]{:S(2)}, u32[]{:S(2)}) collective-permute-start(bf16[76,16,128]{2,1,0:T(8,128)(2,1)S(1)} %get-tuple-element.137), channel_id=1, source_target_pairs={{0,8},{8,0},{16,24},{24,16},{1,9},{9,1},{17,25},{25,17},{2,10},{10... | collective-permute-start | bytes 933896 | tf_op jit(solution)/shard_map/ppermute | solution.py:526
  224.9 24.2 %collective-permute-start.53 = (bf16[76,16,128]{2,1,0:T(8,128)(2,1)S(1)}, bf16[76,16,128]{2,1,0:T(8,128)(2,1)S(1)}, u32[]{:S(2)}, u32[]{:S(2)}) collective-permute-start(bf16[76,16,128]{2,1,0:T(8,128)(2,1)S(1)} %get-tuple-element.137), channel_id=1, source_target_pairs={{0,0},{8,16},{16,8},{24,24},{1,1},{9,17},{17,9},{25,25},{2,2},{10,... | collective-permute-start | bytes 933896 | tf_op jit(solution)/shard_map/ppermute | solution.py:526
  225.5 23.5 %collective-permute-start.54 = (bf16[76,16,128]{2,1,0:T(8,128)(2,1)S(1)}, bf16[76,16,128]{2,1,0:T(8,128)(2,1)S(1)}, u32[]{:S(2)}, u32[]{:S(2)}) collective-permute-start(bf16[76,16,128]{2,1,0:T(8,128)(2,1)S(1)} %get-tuple-element.136.h_stay), channel_id=1, source_target_pairs={{0,16},{8,0},{16,24},{24,8},{1,17},{9,1},{17,25},{25,9},{2,18},{10... | collective-permute-start | bytes 933896 | tf_op jit(solution)/shard_map/ppermute | solution.py:526
  252.5 13.8 %collective-permute-start.57 = (bf16[110,16,128]{2,1,0:T(8,128)(2,1)S(1)}, bf16[110,16,128]{2,1,0:T(8,128)(2,1)S(1)}, u32[]{:S(2)}, u32[]{:S(2)}) collective-permute-start(bf16[110,16,128]{2,1,0:T(8,128)(2,1)S(1)} %get-tuple-element.139.rest_0_), channel_id=1, source_target_pairs={{0,4},{1,3},{2,6},{3,1},{4,0},{5,7},{6,2},{7,5},{8,12},{9,11},{10,... | collective-permute-start | bytes 1351688 | tf_op jit(solution)/shard_map/ppermute | solution.py:510
  (72 other events, 611.1 us)

commit v5 on v4

--- a/solution.py
+++ b/solution.py
@@ -834,17 +834,18 @@
         packed = packed + along(packed, EDGE)
         h_stay, h_leave = summed([h_own, h_last], (packed,), [(4, rest_h), (5, rest_h)], ranges)
         h_edge, h_inner, h_turn = along(h_leave, EDGE), along(h_leave, INNER), along(h_stay, TURN)
-        packed = packed + along(packed, CROSS)
         grad_rows, low_rows = call(
             assemble,
             [jnp.stack([z, jnp.int32(seq_total)])]
             + [a_half, r_half, wide_cross, slim_cross, h_stay, h_edge, h_inner, h_turn],
             [pltpu.HBM(weights.shape, F32), sds(weights.shape, BF)],
             [SM] + [VM] * 8,
-            limit=10, deps=(packed,),
+            limit=10,
         )
+        low_near, low_far = near(low_rows), far(low_rows)
+        packed = tie(packed, (low_near, low_far))
+        packed = packed + along(packed, CROSS)
         vector_total, norm_totals = packed[:-1], packed[-1, :2]
-        low_near, low_far = near(low_rows), far(low_rows)
         low = [low_rows, low_near, low_far, far(low_near)]
         rows = sds(weights.shape, F32)
         one = pl.BlockSpec((BATCH, row16, TB), lambda n: (n, 0, 0))

time: 289 us -> 289 us (level)
  transfers between devices with their start and end apart: 63 -> 63, of which waited for: 29 -> 29; matrix products, arithmetic and copies ran while one was open for 1% -> 2% of each run, Pallas kernels for 27% -> 27%
where the time goes in v5:
time: 289 us; the launch traced here: 285 us
  waiting for transfers between devices  124 us (43%)
  Pallas kernels  95.7 us (33%)
  starting transfers between devices  52.8 us (18%)
  local copies, waits for them, and re-layouts  5.85 us (2%)
  other arithmetic  5.05 us (2%)
    ppermute x49, waiting for transfers between devices, toward(): return lax.ppermute(x, 'fsdp', [(i, move(i)) for i in range(GROUPS)])  91.3 us
    pallas_call x15, Pallas kernels, call(): pl.pallas_call(kernel, out_shape=outs, in_specs=in_specs + [ANY] * len(de...  78.2 us
    ppermute x49, starting transfers between devices, toward(): return lax.ppermute(x, 'fsdp', [(i, move(i)) for i in range(GROUPS)])  34.1 us
    ppermute x14, waiting for transfers between devices, along(): return lax.ppermute(x, 'dp', pairs)  32.6 us
    ppermute x14, starting transfers between devices, along(): return lax.ppermute(x, 'dp', pairs)  18.6 us
    pallas_call x1, Pallas kernels, local(): pl.pallas_call(step_kernel, grid=(PART // BATCH,), out_shape=[rows, rows,...  11 us
    pallas_call x4, Pallas kernels, gate(): pl.pallas_call(kernel, out_shape=outs, in_specs=[SM] + [ANY] * (count + l...  6.5 us
  transfers between devices with their start and end apart: 63, of which 29 were waited for; matrix products, arithmetic and copies ran while one was open for 2% of the time, Pallas kernels for 27%

profile of v5, /device:TPU:0, one launch (start us, length us, event | category | flops | bytes accessed | tf_op | source)
XLA Modules:
  0.0 285.5 jit_solution(10550145674646512074)
XLA Ops:
  2.6 5.9 %collective-permute-start.2 = (bf16[110,16,128]{2,1,0:T(8,128)(2,1)S(1)}, bf16[110,16,128]{2,1,0:T(8,128)(2,1)S(1)}, u32[]{:S(2)}, u32[]{:S(2)}) collective-permute-start(bf16[110,16,128]{2,1,0:T(8,128)(2,1)S(1)} %convert_element_type.9.refs_5_), channel_id=1, source_target_pairs={{0,8},{8,0},{16,24},{24,16},{1,9},{9,1},{17,25},{25,17},{2,10},{10... | collective-permute-start | bytes 1351688 | tf_op jit(solution)/shard_map/ppermute | solution.py:526
  11.5 7.0 %collective-permute-done.2.refs_0_.refs_1_.refs_3_.refs_2_ = bf16[110,16,128]{2,1,0:T(8,128)(2,1)S(1)} collective-permute-done((bf16[110,16,128]{2,1,0:T(8,128)(2,1)S(1)}, bf16[110,16,128]{2,1,0:T(8,128)(2,1)S(1)}, u32[]{:S(2)}, u32[]{:S(2)}) %collective-permute-start.2) | collective-permute-done | bytes 450592 | tf_op jit(solution)/shard_map/ppermute | solution.py:526
  18.5 2.7 collective-permute-done.5.refs_5_.refs_7_
  25.1 2.1 collective-permute-start.1
  27.2 6.7 %collective-permute-done.8.refs_9_.refs_7_ = bf16[110,16,128]{2,1,0:T(8,128)(2,1)S(1)} collective-permute-done((bf16[110,16,128]{2,1,0:T(8,128)(2,1)S(1)}, bf16[110,16,128]{2,1,0:T(8,128)(2,1)S(1)}, u32[]{:S(2)}, u32[]{:S(2)}) %collective-permute-start.8) | collective-permute-done | bytes 450592 | tf_op jit(solution)/shard_map/ppermute | solution.py:510
  33.9 2.8 collective-permute-done.6.refs_4_
  36.6 2.1 collective-permute-done.7.refs_8_
  44.6 8.3 %collective-permute-done.13.refs_9_.refs_3_ = bf16[110,16,128]{2,1,0:T(8,128)(2,1)S(1)} collective-permute-done((bf16[110,16,128]{2,1,0:T(8,128)(2,1)S(1)}, bf16[110,16,128]{2,1,0:T(8,128)(2,1)S(1)}, u32[]{:S(2)}, u32[]{:S(2)}) %collective-permute-start.13) | collective-permute-done | bytes 450592 | tf_op jit(solution)/shard_map/ppermute | solution.py:510
  52.8 2.4 collective-permute-done.11.refs_4_
  55.2 3.2 %collective-permute-done.12.refs_8_ = bf16[110,16,128]{2,1,0:T(8,128)(2,1)S(1)} collective-permute-done((bf16[110,16,128]{2,1,0:T(8,128)(2,1)S(1)}, bf16[110,16,128]{2,1,0:T(8,128)(2,1)S(1)}, u32[]{:S(2)}, u32[]{:S(2)}) %collective-permute-start.12) | collective-permute-done | bytes 450592 | tf_op jit(solution)/shard_map/ppermute | solution.py:510
  63.9 9.1 %collective-permute-done.15.refs_0_.refs_6_ = bf16[110,16,128]{2,1,0:T(8,128)(2,1)S(1)} collective-permute-done((bf16[110,16,128]{2,1,0:T(8,128)(2,1)S(1)}, bf16[110,16,128]{2,1,0:T(8,128)(2,1)S(1)}, u32[]{:S(2)}, u32[]{:S(2)}) %collective-permute-start.15) | collective-permute-done | bytes 450592 | tf_op jit(solution)/shard_map/ppermute | solution.py:510
  73.1 4.8 %collective-permute-done.17.refs_7_ = bf16[110,16,128]{2,1,0:T(8,128)(2,1)S(1)} collective-permute-done((bf16[110,16,128]{2,1,0:T(8,128)(2,1)S(1)}, bf16[110,16,128]{2,1,0:T(8,128)(2,1)S(1)}, u32[]{:S(2)}, u32[]{:S(2)}) %collective-permute-start.17) | collective-permute-done | bytes 450592 | tf_op jit(solution)/shard_map/ppermute | solution.py:510
  77.9 2.6 shard_map.217
  82.2 7.1 %collective-permute-done.19.rest_7_ = bf16[110,16,128]{2,1,0:T(8,128)(2,1)S(1)} collective-permute-done((bf16[110,16,128]{2,1,0:T(8,128)(2,1)S(1)}, bf16[110,16,128]{2,1,0:T(8,128)(2,1)S(1)}, u32[]{:S(2)}, u32[]{:S(2)}) %collective-permute-start.19) | collective-permute-done | bytes 450592 | tf_op jit(solution)/shard_map/ppermute | solution.py:510
  94.5 37.2 %shard_map.218 = (bf16[768,768]{1,0:T(8,128)(2,1)}, bf16[768,768]{1,0:T(8,128)(2,1)}, bf16[768,768]{1,0:T(8,128)(2,1)}, bf16[512,256]{1,0:T(8,128)(2,1)}, bf16[5...) custom-call(s32[15]{0:T(128)} %concatenate.9.sc, ...), custom_call_target="tpu_custom_call" | custom-call | flops 1 | bytes 1 | tf_op jit(solution)/shard_map/pallas_call | solution.py:490
  139.1 12.7 %shard_map.221 = (bf16[512,768]{1,0:T(8,128)(2,1)S(1)}, bf16[512,768]{1,0:T(8,128)(2,1)S(1)}, bf16[512,768]{1,0:T(8,128)(2,1)S(1)}, f32[3,768]{1,0:T(4,128)S(1)}...) custom-call(s32[15]{0:T(128)S(1)} %copy-done.20, ...), custom_call_target="tpu_custom_call" | custom-call | flops 1 | bytes 1 | tf_op jit(solution)/shard_map/pallas_call | solution.py:490
  161.9 9.8 %shard_map.225 = (bf16[512,768]{1,0:T(8,128)(2,1)}, bf16[2,144,16,128]{3,2,1,0:T(8,128)(2,1)}, bf16[2,144,16,128]{3,2,1,0:T(8,128)(2,1)}, bf16[2,144,16,128]{3,2...) custom-call(s32[15]{0:T(128)S(1)} %copy-done.20, ...), custom_call_target="tpu_custom_call" | custom-call | flops 1 | bytes 1 | tf_op jit(solution)/shard_map/pallas_call | solution.py:490
  174.9 2.6 shard_map.229
  178.5 7.7 %collective-permute-done.40.refs_1_ = bf16[144,16,128]{2,1,0:T(8,128)(2,1)} collective-permute-done((bf16[144,16,128]{2,1,0:T(8,128)(2,1)S(1)}, bf16[144,16,128]{2,1,0:T(8,128)(2,1)}, u32[]{:S(2)}, u32[]{:S(2)}) %collective-permute-start.40) | collective-permute-done | bytes 589856 | tf_op jit(solution)/shard_map/ppermute | solution.py:510
  188.7 2.1 shard_map.227
  193.5 10.1 %collective-permute-done.36 = f32[14,768]{1,0:T(8,128)S(1)} collective-permute-done((f32[14,768]{1,0:T(8,128)S(1)}, f32[14,768]{1,0:T(8,128)S(1)}, u32[]{:S(2)}, u32[]{:S(2)}) %collective-permute-start.36) | collective-permute-done | bytes 43040 | tf_op jit(solution)/shard_map/ppermute | solution.py:510
  207.0 3.0 %collective-permute-done.37 = f32[14,768]{1,0:T(8,128)S(1)} collective-permute-done((f32[14,768]{1,0:T(8,128)S(1)}, f32[14,768]{1,0:T(8,128)S(1)}, u32[]{:S(2)}, u32[]{:S(2)}) %collective-permute-start.37) | collective-permute-done | bytes 43040 | tf_op jit(solution)/shard_map/ppermute | solution.py:510
  210.0 2.4 shard_map.230
  215.1 3.0 %collective-permute-done.42.refs_1_ = bf16[110,16,128]{2,1,0:T(8,128)(2,1)} collective-permute-done((bf16[110,16,128]{2,1,0:T(8,128)(2,1)S(1)}, bf16[110,16,128]{2,1,0:T(8,128)(2,1)}, u32[]{:S(2)}, u32[]{:S(2)}) %collective-permute-start.42) | collective-permute-done | bytes 450592 | tf_op jit(solution)/shard_map/ppermute | solution.py:526
  219.9 2.5 collective-permute-done.50.refs_1_
  225.5 3.3 %collective-permute-start.54 = (bf16[76,16,128]{2,1,0:T(8,128)(2,1)S(1)}, bf16[76,16,128]{2,1,0:T(8,128)(2,1)S(1)}, u32[]{:S(2)}, u32[]{:S(2)}) collective-permute-start(bf16[76,16,128]{2,1,0:T(8,128)(2,1)S(1)} %get-tuple-element.136.h_stay), channel_id=1, source_target_pairs={{0,16},{8,0},{16,24},{24,8},{1,17},{9,1},{17,25},{25,9},{2,18},{10... | collective-permute-start | bytes 933896 | tf_op jit(solution)/shard_map/ppermute | solution.py:526
  229.0 19.0 %collective-permute-done.49.slim_x = bf16[42,16,128]{2,1,0:T(8,128)(2,1)S(1)} collective-permute-done((bf16[42,16,128]{2,1,0:T(8,128)(2,1)S(1)}, bf16[42,16,128]{2,1,0:T(8,128)(2,1)S(1)}, u32[]{:S(2)}, u32[]{:S(2)}) %collective-permute-start.49) | collective-permute-done | bytes 172064 | tf_op jit(solution)/shard_map/ppermute | solution.py:526
  248.0 2.0 shard_map.234
  252.6 10.4 %collective-permute-done.55.rest_1_.refs_1_ = bf16[110,16,128]{2,1,0:T(8,128)(2,1)S(1)} collective-permute-done((bf16[110,16,128]{2,1,0:T(8,128)(2,1)S(1)}, bf16[110,16,128]{2,1,0:T(8,128)(2,1)S(1)}, u32[]{:S(2)}, u32[]{:S(2)}) %collective-permute-start.55) | collective-permute-done | bytes 450592 | tf_op jit(solution)/shard_map/ppermute | solution.py:510
  264.7 3.5 %collective-permute-done.62 = f32[14,768]{1,0:T(8,128)S(1)} collective-permute-done((f32[14,768]{1,0:T(8,128)}, f32[14,768]{1,0:T(8,128)S(1)}, u32[]{:S(2)}, u32[]{:S(2)}) %collective-permute-start.62) | collective-permute-done | bytes 43040 | tf_op jit(solution)/shard_map/ppermute | solution.py:526
  269.7 1.9 collective-permute-done.57.rest_3_
  274.2 11.0 %shard_map.235 = (f32[110,16,128]{2,1,0:T(8,128)}, f32[110,16,128]{2,1,0:T(8,128)}, f32[110,16,128]{2,1,0:T(8,128)}) custom-call(s32[15]{0:T(128)S(1)} %copy-done.20, f32[220]{0:T(256)S(1)} %reshape.42.dec, f32[110]{0:T(128)S(1)} %fusion.4.size, f32[110,16,128]{2,1,0:T(8,128)} %get-tuple-element.70.own, f32[110,16,128]{2,1,0:T(8,128)} %lroot.1, ...), custom_call_target="tpu_custom_call" | custom-call | flops 1 | bytes 1 | tf_op jit(solution)/shard_map/pallas_call | solution.py:853
  (231 shorter events, 72.2 us)
Async XLA Ops:
  2.6 15.9 %collective-permute-start.2 = (bf16[110,16,128]{2,1,0:T(8,128)(2,1)S(1)}, bf16[110,16,128]{2,1,0:T(8,128)(2,1)S(1)}, u32[]{:S(2)}, u32[]{:S(2)}) collective-permute-start(bf16[110,16,128]{2,1,0:T(8,128)(2,1)S(1)} %convert_element_type.9.refs_5_), channel_id=1, source_target_pairs={{0,8},{8,0},{16,24},{24,16},{1,9},{9,1},{17,25},{25,17},{2,10},{10... | collective-permute-start | bytes 1351688 | tf_op jit(solution)/shard_map/ppermute | solution.py:526
  23.4 13.3 %collective-permute-start.6 = (bf16[110,16,128]{2,1,0:T(8,128)(2,1)S(1)}, bf16[110,16,128]{2,1,0:T(8,128)(2,1)S(1)}, u32[]{:S(2)}, u32[]{:S(2)}) collective-permute-start(bf16[110,16,128]{2,1,0:T(8,128)(2,1)S(1)} %get-tuple-element.76.refs_5_), channel_id=1, source_target_pairs={{0,2},{1,5},{2,0},{3,7},{4,6},{5,1},{6,4},{7,3},{8,10},{9,13},{10,... | collective-permute-start | bytes 1351688 | tf_op jit(solution)/shard_map/ppermute | solution.py:510
  23.9 14.8 %collective-permute-start.7 = (bf16[110,16,128]{2,1,0:T(8,128)(2,1)S(1)}, bf16[110,16,128]{2,1,0:T(8,128)(2,1)S(1)}, u32[]{:S(2)}, u32[]{:S(2)}) collective-permute-start(bf16[110,16,128]{2,1,0:T(8,128)(2,1)S(1)} %get-tuple-element.77.refs_6_), channel_id=1, source_target_pairs={{0,4},{1,3},{2,6},{3,1},{4,0},{5,7},{6,2},{7,5},{8,12},{9,11},{10,... | collective-permute-start | bytes 1351688 | tf_op jit(solution)/shard_map/ppermute | solution.py:510
  24.4 14.3 %collective-permute-start.3 = (bf16[110,16,128]{2,1,0:T(8,128)(2,1)S(1)}, bf16[110,16,128]{2,1,0:T(8,128)(2,1)S(1)}, u32[]{:S(2)}, u32[]{:S(2)}) collective-permute-start(bf16[110,16,128]{2,1,0:T(8,128)(2,1)S(1)} %collective-permute-done.2.refs_0_.refs_1_.refs_3_.refs_2_), channel_id=1, source_target_pairs={{0,0},{8,16},{16,8},{24,24},{1,1},{9,17},{17,9},{25,25},{2,2},{10,... | collective-permute-start | bytes 1351688 | tf_op jit(solution)/shard_map/ppermute | solution.py:526
  25.1 13.6 %collective-permute-start.1 = (bf16[110,16,128]{2,1,0:T(8,128)(2,1)S(1)}, bf16[110,16,128]{2,1,0:T(8,128)(2,1)S(1)}, u32[]{:S(2)}, u32[]{:S(2)}) collective-permute-start(bf16[110,16,128]{2,1,0:T(8,128)(2,1)S(1)} %collective-permute-done.refs_2_.refs_1_), channel_id=1, source_target_pairs={{0,8},{8,0},{16,24},{24,16},{1,9},{9,1},{17,25},{25,17},{2,10},{10... | collective-permute-start | bytes 1351688 | tf_op jit(solution)/shard_map/ppermute | solution.py:526
  40.3 18.2 %collective-permute-start.9 = (bf16[4,110,16,128]{3,2,1,0:T(8,128)(2,1)}, bf16[4,110,16,128]{3,2,1,0:T(8,128)(2,1)S(1)}, u32[]{:S(2)}, u32[]{:S(2)}) collective-permute-start(bf16[4,110,16,128]{3,2,1,0:T(8,128)(2,1)} %get-tuple-element.78.rest_0_), channel_id=1, source_target_pairs={{0,1},{1,0},{2,3},{3,2},{4,5},{5,4},{6,7},{7,6},{8,9},{9,8},{10,11... | collective-permute-start | bytes 5406728 | tf_op jit(solution)/shard_map/ppermute | solution.py:510
  41.9 13.3 %collective-permute-start.11 = (bf16[110,16,128]{2,1,0:T(8,128)(2,1)S(1)}, bf16[110,16,128]{2,1,0:T(8,128)(2,1)S(1)}, u32[]{:S(2)}, u32[]{:S(2)}) collective-permute-start(bf16[110,16,128]{2,1,0:T(8,128)(2,1)S(1)} %get-tuple-element.79.refs_1_), channel_id=1, source_target_pairs={{0,2},{1,5},{2,0},{3,7},{4,6},{5,1},{6,4},{7,3},{8,10},{9,13},{10,... | collective-permute-start | bytes 1351688 | tf_op jit(solution)/shard_map/ppermute | solution.py:510
  43.6 14.9 %collective-permute-start.12 = (bf16[110,16,128]{2,1,0:T(8,128)(2,1)S(1)}, bf16[110,16,128]{2,1,0:T(8,128)(2,1)S(1)}, u32[]{:S(2)}, u32[]{:S(2)}) collective-permute-start(bf16[110,16,128]{2,1,0:T(8,128)(2,1)S(1)} %get-tuple-element.80.refs_6_), channel_id=1, source_target_pairs={{0,4},{1,3},{2,6},{3,1},{4,0},{5,7},{6,2},{7,5},{8,12},{9,11},{10,... | collective-permute-start | bytes 1351688 | tf_op jit(solution)/shard_map/ppermute | solution.py:510
  44.1 14.4 %collective-permute-start.10 = (bf16[110,16,128]{2,1,0:T(8,128)(2,1)S(1)}, bf16[110,16,128]{2,1,0:T(8,128)(2,1)S(1)}, u32[]{:S(2)}, u32[]{:S(2)}) collective-permute-start(bf16[110,16,128]{2,1,0:T(8,128)(2,1)S(1)} %collective-permute-done.3.refs_2_.refs_1_), channel_id=1, source_target_pairs={{0,8},{8,0},{16,24},{24,16},{1,9},{9,1},{17,25},{25,17},{2,10},{10... | collective-permute-start | bytes 1351688 | tf_op jit(solution)/shard_map/ppermute | solution.py:526
  60.3 17.6 %collective-permute-start.14 = (bf16[4,110,16,128]{3,2,1,0:T(8,128)(2,1)}, bf16[4,110,16,128]{3,2,1,0:T(8,128)(2,1)S(1)}, u32[]{:S(2)}, u32[]{:S(2)}) collective-permute-start(bf16[4,110,16,128]{3,2,1,0:T(8,128)(2,1)} %get-tuple-element.81.rest_2_), channel_id=1, source_target_pairs={{0,1},{1,0},{2,3},{3,2},{4,5},{5,4},{6,7},{7,6},{8,9},{9,8},{10,11... | collective-permute-start | bytes 5406728 | tf_op jit(solution)/shard_map/ppermute | solution.py:510
  63.1 14.8 %collective-permute-start.17 = (bf16[110,16,128]{2,1,0:T(8,128)(2,1)S(1)}, bf16[110,16,128]{2,1,0:T(8,128)(2,1)S(1)}, u32[]{:S(2)}, u32[]{:S(2)}) collective-permute-start(bf16[110,16,128]{2,1,0:T(8,128)(2,1)S(1)} %get-tuple-element.82.refs_5_), channel_id=1, source_target_pairs={{0,4},{1,3},{2,6},{3,1},{4,0},{5,7},{6,2},{7,5},{8,12},{9,11},{10,... | collective-permute-start | bytes 1351688 | tf_op jit(solution)/shard_map/ppermute | solution.py:510
  80.5 14.0 %collective-permute-start.18 = (bf16[4,110,16,128]{3,2,1,0:T(8,128)(2,1)}, bf16[4,110,16,128]{3,2,1,0:T(8,128)(2,1)}, u32[]{:S(2)}, u32[]{:S(2)}) collective-permute-start(bf16[4,110,16,128]{3,2,1,0:T(8,128)(2,1)} %get-tuple-element.84.rest_4_), channel_id=1, source_target_pairs={{0,1},{1,0},{2,3},{3,2},{4,5},{5,4},{6,7},{7,6},{8,9},{9,8},{10,11... | collective-permute-start | bytes 5406728 | tf_op jit(solution)/shard_map/ppermute | solution.py:510
  89.4 42.4 %collective-permute-start.22 = (bf16[2,110,16,128]{3,2,1,0:T(8,128)(2,1)S(1)}, bf16[2,110,16,128]{3,2,1,0:T(8,128)(2,1)S(1)}, u32[]{:S(2)}, u32[]{:S(2)}) collective-permute-start(bf16[2,110,16,128]{3,2,1,0:T(8,128)(2,1)S(1)} %pad_maximum_fusion.refs_9_.rest_8_.rest_16_), channel_id=1, source_target_pairs={{0,2},{1,5},{2,0},{3,7},{4,6},{5,1},{6,4},{7,3},{8,10},{9,13},{10,... | collective-permute-start | bytes 2703368 | tf_op jit(solution)/shard_map/ppermute | solution.py:510
  90.6 41.2 %collective-permute-start.23 = (bf16[2,110,16,128]{3,2,1,0:T(8,128)(2,1)S(1)}, bf16[2,110,16,128]{3,2,1,0:T(8,128)(2,1)}, u32[]{:S(2)}, u32[]{:S(2)}) collective-permute-start(bf16[2,110,16,128]{3,2,1,0:T(8,128)(2,1)S(1)} %pad_maximum_fusion.refs_9_.rest_8_.rest_16_), channel_id=1, source_target_pairs={{0,4},{1,3},{2,6},{3,1},{4,0},{5,7},{6,2},{7,5},{8,12},{9,11},{10,... | collective-permute-start | bytes 2703368 | tf_op jit(solution)/shard_map/ppermute | solution.py:510
  91.9 40.5 %collective-permute-start.24 = (bf16[2,110,16,128]{3,2,1,0:T(8,128)(2,1)S(1)}, bf16[2,110,16,128]{3,2,1,0:T(8,128)(2,1)}, u32[]{:S(2)}, u32[]{:S(2)}) collective-permute-start(bf16[2,110,16,128]{3,2,1,0:T(8,128)(2,1)S(1)} %pad_maximum_fusion.refs_9_.rest_8_.rest_16_), channel_id=1, source_target_pairs={{0,6},{1,7},{2,4},{3,5},{4,2},{5,3},{6,0},{7,1},{8,14},{9,15},{10,... | collective-permute-start | bytes 2703368 | tf_op jit(solution)/shard_map/ppermute | solution.py:510
  93.1 45.9 %collective-permute-start.29 = (bf16[2,110,16,128]{3,2,1,0:T(8,128)(2,1)S(1)}, bf16[2,110,16,128]{3,2,1,0:T(8,128)(2,1)S(1)}, u32[]{:S(2)}, u32[]{:S(2)}) collective-permute-start(bf16[2,110,16,128]{3,2,1,0:T(8,128)(2,1)S(1)} %pad_maximum_fusion.refs_9_.rest_8_.rest_16_), channel_id=1, source_target_pairs={{0,1},{1,0},{2,3},{3,2},{4,5},{5,4},{6,7},{7,6},{8,9},{9,8},{10,11... | collective-permute-start | bytes 2703368 | tf_op jit(solution)/shard_map/ppermute | solution.py:510
  133.8 18.5 %collective-permute-start.27 = (bf16[2,144,16,128]{3,2,1,0:T(8,128)(2,1)S(1)}, bf16[2,144,16,128]{3,2,1,0:T(8,128)(2,1)S(1)}, u32[]{:S(2)}, u32[]{:S(2)}) collective-permute-start(bf16[2,144,16,128]{3,2,1,0:T(8,128)(2,1)S(1)} %copy-done.39), channel_id=1, source_target_pairs={{0,1},{1,0},{2,3},{3,2},{4,5},{5,4},{6,7},{7,6},{8,9},{9,8},{10,11... | collective-permute-start | bytes 3538952 | tf_op jit(solution)/shard_map/ppermute | solution.py:510
  137.4 16.3 %collective-permute-start.28 = (bf16[2,144,16,128]{3,2,1,0:T(8,128)(2,1)S(1)}, bf16[2,144,16,128]{3,2,1,0:T(8,128)(2,1)S(1)}, u32[]{:S(2)}, u32[]{:S(2)}) collective-permute-start(bf16[2,144,16,128]{3,2,1,0:T(8,128)(2,1)S(1)} %shard_map.220.rest_0_), channel_id=1, source_target_pairs={{0,4},{1,3},{2,6},{3,1},{4,0},{5,7},{6,2},{7,5},{8,12},{9,11},{10,... | collective-permute-start | bytes 3538952 | tf_op jit(solution)/shard_map/ppermute | solution.py:510
  138.5 13.3 %collective-permute-start.30 = (bf16[2,110,16,128]{3,2,1,0:T(8,128)(2,1)S(1)}, bf16[2,110,16,128]{3,2,1,0:T(8,128)(2,1)S(1)}, u32[]{:S(2)}, u32[]{:S(2)}) collective-permute-start(bf16[2,110,16,128]{3,2,1,0:T(8,128)(2,1)S(1)} %copy-done.6), channel_id=1, source_target_pairs={{0,1},{1,0},{2,3},{3,2},{4,5},{5,4},{6,7},{7,6},{8,9},{9,8},{10,11... | collective-permute-start | bytes 2703368 | tf_op jit(solution)/shard_map/ppermute | solution.py:510
  138.5 13.8 %collective-permute-start.31 = (bf16[2,110,16,128]{3,2,1,0:T(8,128)(2,1)}, bf16[2,110,16,128]{3,2,1,0:T(8,128)(2,1)S(1)}, u32[]{:S(2)}, u32[]{:S(2)}) collective-permute-start(bf16[2,110,16,128]{3,2,1,0:T(8,128)(2,1)} %collective-permute-done.23.refs_2_.rest_10_.rest_18_), channel_id=1, source_target_pairs={{0,1},{1,0},{2,3},{3,2},{4,5},{5,4},{6,7},{7,6},{8,9},{9,8},{10,11... | collective-permute-start | bytes 2703368 | tf_op jit(solution)/shard_map/ppermute | solution.py:510
  139.0 13.3 %collective-permute-start.32 = (bf16[2,110,16,128]{3,2,1,0:T(8,128)(2,1)}, bf16[2,110,16,128]{3,2,1,0:T(8,128)(2,1)S(1)}, u32[]{:S(2)}, u32[]{:S(2)}) collective-permute-start(bf16[2,110,16,128]{3,2,1,0:T(8,128)(2,1)} %collective-permute-done.24.refs_3_.rest_11_.rest_19_), channel_id=1, source_target_pairs={{0,1},{1,0},{2,3},{3,2},{4,5},{5,4},{6,7},{7,6},{8,9},{9,8},{10,11... | collective-permute-start | bytes 2703368 | tf_op jit(solution)/shard_map/ppermute | solution.py:510
  158.0 30.7 %collective-permute-start.38 = (bf16[2,152,16,128]{3,2,1,0:T(8,128)(2,1)}, bf16[2,152,16,128]{3,2,1,0:T(8,128)(2,1)S(1)}, u32[]{:S(2)}, u32[]{:S(2)}) collective-permute-start(bf16[2,152,16,128]{3,2,1,0:T(8,128)(2,1)} %get-tuple-element.121), channel_id=1, source_target_pairs={{0,1},{1,0},{2,3},{3,2},{4,5},{5,4},{6,7},{7,6},{8,9},{9,8},{10,11... | collective-permute-start | bytes 3735560 | tf_op jit(solution)/shard_map/ppermute | solution.py:510
  160.8 27.9 %collective-permute-start.39 = (bf16[2,152,16,128]{3,2,1,0:T(8,128)(2,1)S(1)}, bf16[2,152,16,128]{3,2,1,0:T(8,128)(2,1)}, u32[]{:S(2)}, u32[]{:S(2)}) collective-permute-start(bf16[2,152,16,128]{3,2,1,0:T(8,128)(2,1)S(1)} %shard_map.224.rest_0_), channel_id=1, source_target_pairs={{0,4},{1,3},{2,6},{3,1},{4,0},{5,7},{6,2},{7,5},{8,12},{9,11},{10,... | collective-permute-start | bytes 3735560 | tf_op jit(solution)/shard_map/ppermute | solution.py:510
  172.3 13.9 %collective-permute-start.40 = (bf16[144,16,128]{2,1,0:T(8,128)(2,1)S(1)}, bf16[144,16,128]{2,1,0:T(8,128)(2,1)}, u32[]{:S(2)}, u32[]{:S(2)}) collective-permute-start(bf16[144,16,128]{2,1,0:T(8,128)(2,1)S(1)} %get-tuple-element.114.refs_1_), channel_id=1, source_target_pairs={{0,2},{1,5},{2,0},{3,7},{4,6},{5,1},{6,4},{7,3},{8,10},{9,13},{10,... | collective-permute-start | bytes 1769480 | tf_op jit(solution)/shard_map/ppermute | solution.py:510
  174.0 36.0 %collective-permute-start.43 = (bf16[2,144,16,128]{3,2,1,0:T(8,128)(2,1)}, bf16[2,144,16,128]{3,2,1,0:T(8,128)(2,1)}, u32[]{:S(2)}, u32[]{:S(2)}) collective-permute-start(bf16[2,144,16,128]{3,2,1,0:T(8,128)(2,1)} %get-tuple-element.129), channel_id=1, source_target_pairs={{0,1},{1,0},{2,3},{3,2},{4,5},{5,4},{6,7},{7,6},{8,9},{9,8},{10,11... | collective-permute-start | bytes 3538952 | tf_op jit(solution)/shard_map/ppermute | solution.py:510
  177.4 32.6 %collective-permute-start.46 = (bf16[2,144,16,128]{3,2,1,0:T(8,128)(2,1)}, bf16[2,144,16,128]{3,2,1,0:T(8,128)(2,1)}, u32[]{:S(2)}, u32[]{:S(2)}) collective-permute-start(bf16[2,144,16,128]{3,2,1,0:T(8,128)(2,1)} %shard_map.229), channel_id=1, source_target_pairs={{0,4},{1,3},{2,6},{3,1},{4,0},{5,7},{6,2},{7,5},{8,12},{9,11},{10,... | collective-permute-start | bytes 3538952 | tf_op jit(solution)/shard_map/ppermute | solution.py:510
  191.6 18.4 %collective-permute-start.47 = (bf16[110,16,128]{2,1,0:T(8,128)(2,1)S(1)}, bf16[110,16,128]{2,1,0:T(8,128)(2,1)S(1)}, u32[]{:S(2)}, u32[]{:S(2)}) collective-permute-start(bf16[110,16,128]{2,1,0:T(8,128)(2,1)S(1)} %get-tuple-element.123.refs_3_), channel_id=1, source_target_pairs={{0,8},{8,0},{16,24},{24,16},{1,9},{9,1},{17,25},{25,17},{2,10},{10... | collective-permute-start | bytes 1351688 | tf_op jit(solution)/shard_map/ppermute | solution.py:526
  219.3 28.7 %collective-permute-start.48 = (bf16[110,16,128]{2,1,0:T(8,128)(2,1)S(1)}, bf16[110,16,128]{2,1,0:T(8,128)(2,1)S(1)}, u32[]{:S(2)}, u32[]{:S(2)}) collective-permute-start(bf16[110,16,128]{2,1,0:T(8,128)(2,1)S(1)} %broadcast_select_fusion), channel_id=1, source_target_pairs={{0,8},{8,24},{16,0},{24,16},{1,9},{9,25},{17,1},{25,17},{2,10},{10... | collective-permute-start | bytes 1351688 | tf_op jit(solution)/shard_map/ppermute | solution.py:526
  223.3 24.7 %collective-permute-start.52 = (bf16[76,16,128]{2,1,0:T(8,128)(2,1)S(1)}, bf16[76,16,128]{2,1,0:T(8,128)(2,1)S(1)}, u32[]{:S(2)}, u32[]{:S(2)}) collective-permute-start(bf16[76,16,128]{2,1,0:T(8,128)(2,1)S(1)} %get-tuple-element.137), channel_id=1, source_target_pairs={{0,8},{8,0},{16,24},{24,16},{1,9},{9,1},{17,25},{25,17},{2,10},{10... | collective-permute-start | bytes 933896 | tf_op jit(solution)/shard_map/ppermute | solution.py:526
  224.8 23.2 %collective-permute-start.53 = (bf16[76,16,128]{2,1,0:T(8,128)(2,1)S(1)}, bf16[76,16,128]{2,1,0:T(8,128)(2,1)S(1)}, u32[]{:S(2)}, u32[]{:S(2)}) collective-permute-start(bf16[76,16,128]{2,1,0:T(8,128)(2,1)S(1)} %get-tuple-element.137), channel_id=1, source_target_pairs={{0,0},{8,16},{16,8},{24,24},{1,1},{9,17},{17,9},{25,25},{2,2},{10,... | collective-permute-start | bytes 933896 | tf_op jit(solution)/shard_map/ppermute | solution.py:526
  225.5 22.5 %collective-permute-start.54 = (bf16[76,16,128]{2,1,0:T(8,128)(2,1)S(1)}, bf16[76,16,128]{2,1,0:T(8,128)(2,1)S(1)}, u32[]{:S(2)}, u32[]{:S(2)}) collective-permute-start(bf16[76,16,128]{2,1,0:T(8,128)(2,1)S(1)} %get-tuple-element.136.h_stay), channel_id=1, source_target_pairs={{0,16},{8,0},{16,24},{24,8},{1,17},{9,1},{17,25},{25,9},{2,18},{10... | collective-permute-start | bytes 933896 | tf_op jit(solution)/shard_map/ppermute | solution.py:526
  228.8 19.1 %collective-permute-start.49 = (bf16[42,16,128]{2,1,0:T(8,128)(2,1)S(1)}, bf16[42,16,128]{2,1,0:T(8,128)(2,1)S(1)}, u32[]{:S(2)}, u32[]{:S(2)}) collective-permute-start(bf16[42,16,128]{2,1,0:T(8,128)(2,1)S(1)} %slice_select_fusion), channel_id=1, source_target_pairs={{0,16},{8,0},{16,24},{24,8},{1,17},{9,1},{17,25},{25,9},{2,18},{10... | collective-permute-start | bytes 516104 | tf_op jit(solution)/shard_map/ppermute | solution.py:526
  (73 other events, 638.8 us)
